TPU v7x, 32 devices: a whole 2x2x4 slice. The times are simulated.
32 devices in a mesh: row: 8 (over y, x, core), col: 4 (over z).
Axes of the slice: x: 2, y: 2, z: 4, core: 2. Of those that a mesh axis runs over, the one named last changes fastest.
Arguments:
- diag_inverse: float32 [512, 512], replicated, may hold values from -1 to 2, as said below
- panel: float32 [12288, 512], P('row', 'col'), may hold values from -0.3 to 0.3
- trailing: float32 [12288, 12288], P('row', 'col'), may hold values from -6 to 6
- agg_vals: float32 [8, 4, 12, 1024], P('row', 'col'), may hold values from -6 to 6
- agg_dest: int32 [8, 4, 12, 1], P('row', 'col'), may hold values from 0 to 7; in each aligned block of 12 rows (0 to 11, 12 to 23, ..., all dimensions but the last counted through in order) at most 2 rows name the same one
- agg_tile: int32 [8, 4, 12], P('row', 'col'), may hold values from 0 to 4607
Outputs:
- updated: float32 [12288, 12288], P('row', 'col')
- panel_factor: float32 [12288, 512], P('row', 'col')
Inputs may be any that keep to these rules, and one draw needn't show every extreme that they name: `diag_inverse`: lower triangular with diagonal entries between 0.5 and 2. `agg_dest`: among the aggregates of one device no row index is named more than 2 times, and in some device one is named exactly 2 times.
All inputs are finite; a program needn't handle non-finite values.
Results may differ from a plain program's by a relative error of at most 0.000071.
Values sent between devices are 32-bit elements; how exact they have to be, the bound alone decides.
No kernel may reach another device: no remote copies, remote signals or barrier semaphores. Data moves between devices by JAX's collectives and lax.ppermute only.
A program may use at most 128 MiB of HBM per device.

v0:
```python
import jax
import jax.numpy as jnp
from jax import lax
from jax.sharding import PartitionSpec as P

TILE_ROWS = 8
TILE_COLS = 128
CAP = 2


def per_device(diag_inverse, panel, trailing, agg_vals, agg_dest, agg_tile):
    row_devices = lax.axis_size("row")
    col_devices = lax.axis_size("col")
    local_rows, local_cols = trailing.shape
    panel_width = diag_inverse.shape[0]
    part_width = panel_width // col_devices
    col_index = lax.axis_index("col")
    contract_last = (((1,), (1,)), ((), ()))
    panel_whole = lax.all_gather(panel, "col", axis=1, tiled=True)
    own_full = jnp.dot(
        panel_whole,
        diag_inverse.T,
        precision=lax.Precision.HIGHEST,
        preferred_element_type=jnp.float32,
    )
    own_block = lax.dynamic_slice_in_dim(own_full, col_index * part_width, part_width, 1)
    column_all = lax.all_gather(own_block, "row", axis=0, tiled=True)
    split_rows = column_all.reshape(col_devices, local_cols, part_width)
    swapped = lax.all_to_all(split_rows, "col", split_axis=0, concat_axis=2, tiled=True)
    partner = swapped.reshape(local_cols, panel_width)
    tile_rows = local_rows // TILE_ROWS
    tile_cols = local_cols // TILE_COLS
    tiles_dev = tile_rows * tile_cols
    tile_values = agg_vals.reshape(agg_vals.shape[2], agg_vals.shape[3])
    targets = agg_dest.reshape(-1)
    tile_ids = agg_tile.reshape(-1)
    matches = (targets[:, None] == jnp.arange(row_devices, dtype=jnp.int32)[None, :]).astype(
        jnp.int32
    )
    earlier = jnp.cumsum(matches, axis=0) - matches
    ranks = jnp.sum(earlier * matches, axis=1)
    position = targets * CAP + ranks
    send_values = (
        jnp.zeros((row_devices * CAP, tile_values.shape[1]), jnp.float32)
        .at[position]
        .set(tile_values)
    )
    send_ids = (
        jnp.full((row_devices * CAP,), float(tiles_dev), jnp.float32)
        .at[position]
        .set(tile_ids.astype(jnp.float32))
    )
    got_values, got_ids = (
        lax.all_to_all(send_values, "row", split_axis=0, concat_axis=0, tiled=True),
        lax.all_to_all(send_ids, "row", split_axis=0, concat_axis=0, tiled=True),
    )
    landing = got_ids.astype(jnp.int32)
    blocked = trailing.reshape(tile_rows, TILE_ROWS, tile_cols, TILE_COLS)
    blocked = blocked.at[landing // tile_cols, :, landing % tile_cols, :].add(
        got_values.reshape(-1, TILE_ROWS, TILE_COLS), mode="drop"
    )
    assembled = blocked.reshape(local_rows, local_cols)
    product = lax.dot_general(
        own_full,
        partner,
        contract_last,
        precision=lax.Precision.HIGHEST,
        preferred_element_type=jnp.float32,
    )
    updated = assembled - product
    return (updated, own_block)


def solution(mesh):
    in_specs = (
        P(),
        P("row", "col"),
        P("row", "col"),
        P("row", "col", None, None),
        P("row", "col", None, None),
        P("row", "col", None),
    )
    out_specs = (P("row", "col"), P("row", "col"))
    return jax.shard_map(
        per_device, mesh=mesh, in_specs=in_specs, out_specs=out_specs, check_vma=False
    )
```

profile of v0, /device:TPU:0, one launch (start us, length us, event | category | flops | bytes accessed | tf_op | source)
XLA Modules:
  0.0 336.6 jit_solution(5946130610383401241)
XLA Ops:
  7.2 14.9 %copy.20 = f32[1536,3072]{1,0:T(8,128)} copy(f32[1536,3072]{1,0:T(8,128)} %param.8) | data formatting | bytes 37748736
  22.1 0.0 all-gather.5.cloned.1.call-start
  22.2 66.2 %all-gather.3.cloned.1.call-done = f32[1536,512]{1,0:T(8,128)} async-done(((f32[1536,128]{1,0:T(8,128)}), f32[1536,512]{1,0:T(8,128)}) %all-gather.3.cloned.1.call-update) | async-done | bytes 3145744 | tf_op jit(solution)/shard_map/all_gather | solution.py:19
  88.4 7.3 %fusion.10 = f32[1536,512]{1,0:T(8,128)S(1)} fusion(f32[1536,512]{1,0:T(8,128)} %all-gather.3.cloned.1.call-done, f32[512,512]{1,0:T(8,128)S(1)} %copy-done), kind=kOutput, calls=%fused_computation.30 | convolution fusion | flops 4831838208 | bytes 7340032 | tf_op jit(solution)/shard_map/dot_general | solution.py:20
  95.7 1.7 copy-done.2
  97.5 1.0 constant_dynamic-slice_fusion
  98.5 0.2 reduce_window_sum.11
  98.7 0.6 scatter_custom_fusion
  99.3 0.7 all_to_all.23
  100.0 3.7 %all-to-all-start = ((f32[8,2,1]{1,2,0:T(1,128)}), f32[8,2,1]{1,2,0:T(1,128)S(1)}, u32[]{:S(2)}, u32[]{:S(2)}) async-start(f32[8,2,1]{1,2,0:T(1,128)} %bitcast.6), calls=%async_computation | async-start | bytes 8192 | tf_op jit(solution)/shard_map/all_to_all | solution.py:55
  103.7 0.7 scatter_custom_fusion.1
  104.4 0.7 all_to_all.25
  105.0 3.3 all-to-all-done
  108.3 3.3 all-to-all-start.1
  111.6 31.4 %all-gather.5.cloned.1.call-done = f32[12288,128]{1,0:T(8,128)} async-done(((f32[1536,128]{1,0:T(8,128)}), f32[12288,128]{1,0:T(8,128)}) %all-gather.5.cloned.1.call-update) | async-done | bytes 6291472 | tf_op jit(solution)/shard_map/all_gather | solution.py:27
  143.1 6.6 %copy.12 = f32[4,3072,128]{1,2,0:T(8,128)} copy(f32[4,3072,128]{2,1,0:T(8,128)} %bitcast.31) | data formatting | bytes 12582912 | tf_op jit(solution)/shard_map/reshape | solution.py:28
  149.6 5.4 %all-to-all-start.2 = ((f32[4,3072,128]{1,2,0:T(8,128)}), f32[4,3072,128]{1,2,0:T(8,128)}, u32[]{:S(2)}, u32[]{:S(2)}) async-start(f32[4,3072,128]{1,2,0:T(8,128)} %copy.12), calls=%async_computation.2 | async-start | bytes 12582912 | tf_op jit(solution)/shard_map/all_to_all | solution.py:29
  155.1 0.1 div.17
  155.2 0.1 rem.30
  155.3 0.1 ne.48
  155.4 0.1 reshape.160
  155.5 2.3 scatter_fusion
  157.8 135.9 %all-to-all-done.2 = f32[4,3072,128]{1,2,0:T(8,128)} async-done(((f32[4,3072,128]{1,2,0:T(8,128)}), f32[4,3072,128]{1,2,0:T(8,128)}, u32[]{:S(2)}, u32[]{:S(2)}) %all-to-all-start.2) | async-done | bytes 6291488 | tf_op jit(solution)/shard_map/all_to_all | solution.py:29
  293.7 36.0 %bitcast_subtract_fusion = f32[1536,3072]{1,0:T(8,128)} fusion(f32[192,8,24,128]{3,1,2,0:T(8,128)} %scatter_fusion, f32[1536,512]{1,0:T(8,128)} %copy-done.2, f32[3072,512]{0,1:T(8,128)} %bitcast.12), kind=kOutput, calls=%fused_computation.3 | convolution fusion | flops 28995747840 | bytes 47185920 | tf_op jit(solution)/shard_map/dot_general | solution.py:63
  (22 shorter events, 0.2 us)
Async XLA Ops:
  7.2 81.2 %copy-start = (f32[512,512]{1,0:T(8,128)S(1)}, f32[512,512]{1,0:T(8,128)}, u32[]{:S(2)}) copy-start(f32[512,512]{1,0:T(8,128)} %param.6) | copy-start | bytes 3145732
  7.2 81.2 %all-gather.3.cloned.1.call-start = ((), (), s32[]{:S(2)}) async-start(), calls=%async_computation.3 | async-start | bytes 3932160 | tf_op jit(solution)/shard_map/all_gather | solution.py:19
  22.1 76.4 %copy-start.4 = (s32[1,1,12,1]{2,3,1,0:T(1,128)S(1)}, s32[1,1,12,1]{2,3,1,0:T(1,128)}, u32[]{:S(2)}) copy-start(s32[1,1,12,1]{2,3,1,0:T(1,128)} %param.10) | copy-start | bytes 148
  22.1 76.6 %copy-start.5 = (s32[1,1,12]{2,1,0:T(1,128)S(1)}, s32[1,1,12]{2,1,0:T(1,128)}, u32[]{:S(2)}) copy-start(s32[1,1,12]{2,1,0:T(1,128)} %param.11) | copy-start | bytes 148
  22.1 81.6 %copy-start.3 = (f32[1,1,12,1024]{3,1,2,0:T(1,128)S(1)}, f32[1,1,12,1024]{3,1,2,0:T(1,128)}, u32[]{:S(2)}) copy-start(f32[1,1,12,1024]{3,1,2,0:T(1,128)} %param.9) | copy-start | bytes 147460
  22.1 120.9 %all-gather.5.cloned.1.call-start = ((), (), s32[]{:S(2)}) async-start(), calls=%async_computation.4 | async-start | bytes 7077888 | tf_op jit(solution)/shard_map/all_gather | solution.py:27
  95.7 1.8 copy-start.2
  100.0 8.2 %all-to-all-start = ((f32[8,2,1]{1,2,0:T(1,128)}), f32[8,2,1]{1,2,0:T(1,128)S(1)}, u32[]{:S(2)}, u32[]{:S(2)}) async-start(f32[8,2,1]{1,2,0:T(1,128)} %bitcast.6), calls=%async_computation | async-start | bytes 8192 | tf_op jit(solution)/shard_map/all_to_all | solution.py:55
  108.3 41.4 %all-to-all-start.1 = ((f32[8,2,1024]{2,1,0:T(2,128)}), f32[8,2,1024]{2,1,0:T(2,128)S(1)}, u32[]{:S(2)}, u32[]{:S(2)}) async-start(f32[8,2,1024]{2,1,0:T(2,128)} %all_to_all.25), calls=%async_computation.1 | async-start | bytes 131072 | tf_op jit(solution)/shard_map/all_to_all | solution.py:54
  149.6 144.1 %all-to-all-start.2 = ((f32[4,3072,128]{1,2,0:T(8,128)}), f32[4,3072,128]{1,2,0:T(8,128)}, u32[]{:S(2)}, u32[]{:S(2)}) async-start(f32[4,3072,128]{1,2,0:T(8,128)} %copy.12), calls=%async_computation.2 | async-start | bytes 12582912 | tf_op jit(solution)/shard_map/all_to_all | solution.py:29
  293.7 36.0 %copy-start.1 = (f32[512,512]{1,0:T(8,128)S(1)}, f32[512,512]{1,0:T(8,128)}, u32[]{:S(2)}) copy-start(f32[512,512]{1,0:T(8,128)} %param.6) | copy-start | bytes 3145732
Sparse Core Ops, SparseCore 0:
  22.2 66.1 all-gather.2
  98.6 44.3 all-gather.4
where the time goes:
time: 337 us
  waiting for transfers between devices  237 us (70%)
  matrix products  43.3 us (13%)
  local copies, waits for them, and re-layouts  27.1 us (8%)
  between operations  14.2 us (4%)
  starting transfers between devices  12.5 us (4%)
    all_to_all x1, waiting for transfers between devices, per_device(): lax.all_to_all(split_rows, 'col', split_axis=0, concat_axis=2, tiled=True)  136 us
    all_gather x1, waiting for transfers between devices, per_device(): panel_whole = lax.all_gather(panel, 'col', axis=1, tiled=True)  66.2 us
    dot_general x1, matrix products, per_device(): lax.dot_general(own_full, partner, contract_last, precision=lax.Precision...  36 us
    all_gather x1, waiting for transfers between devices, per_device(): column_all = lax.all_gather(own_block, 'row', axis=0, tiled=True)  31.4 us
    unnamed x13, local copies, waits for them, and re-layouts  16.6 us
    dot_general x1, matrix products, per_device(): jnp.dot(panel_whole, diag_inverse.T, precision=lax.Precision.HIGHEST, pre...  7.33 us
  transfers between devices with their start and end apart: 5, of which 4 were waited for; matrix products, arithmetic and copies ran while one was open for 3% of the time, Pallas kernels for 0%

commit v1 on v0

v1 whole, which is shorter than its diff:
```python
import functools

import jax
import jax.numpy as jnp
from jax import lax
from jax.experimental import pallas as pl
from jax.experimental.pallas import tpu as pltpu
from jax.sharding import PartitionSpec as P

TILE_ROWS = 8
TILE_COLS = 128
CAP = 2
NEXT = {0: 1, 1: 3, 3: 2, 2: 0}
PREV = {v: k for k, v in NEXT.items()}
BOTH = ("row", "col")
SMALL_GATHER = 4 << 20
NN = (((1,), (0,)), ((), ()))
NT = (((1,), (1,)), ((), ()))


def split(x):
    hi = x.astype(jnp.bfloat16)
    lo = (x - hi.astype(jnp.float32)).astype(jnp.bfloat16)
    return hi, lo


def hop(x, source, target, row_devices, col_devices):
    perm = [
        (((q ^ source) * 2 + k) * col_devices + q, ((q ^ target) * 2 + k) * col_devices + q)
        for q in range(col_devices)
        for k in range(2)
    ]
    return lax.ppermute(x, BOTH, perm)


def pick_kernel(role_ref, *refs):
    choices, out_ref, sem = refs[:-2], refs[-2], refs[-1]
    half = out_ref.shape[0] // 2
    role = role_ref[0]
    first, second = choices[:4], choices[4:]
    for r in range(4):

        @pl.when(role == r)
        def _(r=r):
            one = pltpu.make_async_copy(first[r], out_ref.at[pl.ds(0, half)], sem.at[0])
            two = pltpu.make_async_copy(second[r], out_ref.at[pl.ds(half, half)], sem.at[1])
            one.start()
            two.start()
            one.wait()
            two.wait()


def pick(role, first, second):
    rows, width = first[0].shape
    return pl.pallas_call(
        pick_kernel,
        out_shape=jax.ShapeDtypeStruct((2 * rows, width), jnp.float32),
        in_specs=[pl.BlockSpec(memory_space=pltpu.SMEM)]
        + [pl.BlockSpec(memory_space=pl.ANY)] * 8,
        out_specs=pl.BlockSpec(memory_space=pl.ANY),
        scratch_shapes=[pltpu.SemaphoreType.DMA((2,))],
        name="pick",
    )(role, *first, *second)


def front_kernel(
    own_plan,
    pair_plan,
    bm,
    bn,
    place_ref,
    entry_ref,
    start_ref,
    d_ref,
    dt_ref,
    agg_ref,
    trail_ref,
    *refs,
):
    n_own, n_pair = len(own_plan), len(pair_plan)
    own_refs = refs[:n_own]
    pair_refs = refs[n_own : n_own + n_pair]
    out_ref, block_ref = refs[n_own + n_pair : n_own + n_pair + 2]
    own_stage, pair_stage, dcat, dtcat, own_cat, pair_cat, own_full, sem = refs[
        n_own + n_pair + 2 :
    ]
    i, j = pl.program_id(0), pl.program_id(1)
    n_j = pl.num_programs(1)
    width = d_ref.shape[0]
    part = own_stage.shape[1] // 4

    def lanes(s):
        return pl.ds(pl.multiple_of(place_ref[s] * part, part), part)

    def copies():
        out = []
        for n, (s, base, row, rows) in enumerate(pair_plan):
            at = pl.multiple_of(place_ref[4 + base] + row, 16)
            out.append(
                pltpu.make_async_copy(
                    pair_refs[n], pair_stage.at[pl.ds(at, rows), lanes(s)], sem.at[n]
                )
            )
        for n, (s, row, rows) in enumerate(own_plan):
            out.append(
                pltpu.make_async_copy(
                    own_refs[n], own_stage.at[pl.ds(row, rows), lanes(s)], sem.at[n_pair + n]
                )
            )
        return out

    @pl.when((i == 0) & (j == 0))
    def _():
        todo = copies()
        for c in todo:
            c.start()
        hi, lo = split(d_ref[...])
        dcat[:, 0:width] = hi
        dcat[:, width : 2 * width] = hi
        dcat[:, 2 * width :] = lo
        hi, lo = split(dt_ref[...])
        dtcat[0:width, :] = hi
        dtcat[width : 2 * width, :] = hi
        dtcat[2 * width :, :] = lo
        for c in todo:
            c.wait()

        def body(n, carry):
            at = pl.ds(pl.multiple_of(n * width, width), width)
            hi, lo = split(pair_stage[at, :])
            rhs = jnp.concatenate([hi, lo, hi], axis=1)
            turned = lax.dot_general(dcat[...], rhs, NT, preferred_element_type=jnp.float32)
            hi, lo = split(turned)
            pair_cat[0:width, at] = hi
            pair_cat[width : 2 * width, at] = lo
            pair_cat[2 * width :, at] = hi
            return carry

        lax.fori_loop(0, pair_stage.shape[0] // width, body, 0)

    @pl.when(j == 0)
    def _():
        hi, lo = split(own_stage[pl.ds(pl.multiple_of(i * bm, bm), bm), :])
        lhs = jnp.concatenate([hi, lo, hi], axis=1)
        full = lax.dot_general(lhs, dtcat[...], NN, preferred_element_type=jnp.float32)
        own_full[...] = full
        block_ref[...] = own_full[:, pl.ds(pl.multiple_of(place_ref[6] * part, part), part)]
        hi, lo = split(full)
        own_cat[:, 0:width] = hi
        own_cat[:, width : 2 * width] = hi
        own_cat[:, 2 * width :] = lo

    cols = pl.ds(pl.multiple_of(j * bn, bn), bn)
    product = lax.dot_general(
        own_cat[...], pair_cat[:, cols], NN, preferred_element_type=jnp.float32
    )
    out_ref[...] = trail_ref[...] - product
    step = i * n_j + j

    def add(e, carry):
        r = pl.multiple_of(entry_ref[1, e], TILE_ROWS)
        c = pl.multiple_of(entry_ref[2, e], TILE_COLS)
        here = (pl.ds(r, TILE_ROWS), pl.ds(c, TILE_COLS))
        out_ref[here] = out_ref[here] + agg_ref[entry_ref[0, e]]
        return carry

    lax.fori_loop(start_ref[step], start_ref[step + 1], add, 0)


def front(place, entries, starts, d, agg, trailing, own, own_plan, pair, pair_plan, bm, bn):
    rows, cols = trailing.shape
    width = d.shape[0]
    part = width // 4
    anywhere = pl.BlockSpec(memory_space=pl.ANY)
    whole = pl.BlockSpec(memory_space=pltpu.VMEM)
    smem = pl.BlockSpec(memory_space=pltpu.SMEM)
    return pl.pallas_call(
        functools.partial(front_kernel, own_plan, pair_plan, bm, bn),
        grid=(rows // bm, cols // bn),
        out_shape=(
            jax.ShapeDtypeStruct((rows, cols), jnp.float32),
            jax.ShapeDtypeStruct((rows, part), jnp.float32),
        ),
        in_specs=[smem, smem, smem, whole, whole, whole]
        + [pl.BlockSpec((bm, bn), lambda i, j: (i, j))]
        + [anywhere] * (len(own) + len(pair)),
        out_specs=(
            pl.BlockSpec((bm, bn), lambda i, j: (i, j)),
            pl.BlockSpec((bm, part), lambda i, j: (i, 0)),
        ),
        scratch_shapes=[
            pltpu.VMEM((rows, width), jnp.float32),
            pltpu.VMEM((cols, width), jnp.float32),
            pltpu.VMEM((width, 3 * width), jnp.bfloat16),
            pltpu.VMEM((3 * width, width), jnp.bfloat16),
            pltpu.VMEM((bm, 3 * width), jnp.bfloat16),
            pltpu.VMEM((3 * width, cols), jnp.bfloat16),
            pltpu.VMEM((bm, width), jnp.float32),
            pltpu.SemaphoreType.DMA((len(own) + len(pair),)),
        ],
        compiler_params=pltpu.CompilerParams(vmem_limit_bytes=56 << 20),
        name="front",
    )(place, entries, starts, d, d.T, agg, trailing, *own, *pair)


def exchange_tiles(agg_vals, agg_dest, agg_tile, tiles_dev):
    row_devices = lax.axis_size("row")
    agg = agg_vals.shape[2]
    values = agg_vals.reshape(agg, TILE_ROWS, TILE_COLS)
    targets = agg_dest.reshape(-1)
    tile_ids = agg_tile.reshape(-1)
    if row_devices * agg * TILE_ROWS * TILE_COLS * 4 <= SMALL_GATHER:
        numbers = jnp.stack([targets, tile_ids]).astype(jnp.float32)
        numbers = jnp.pad(numbers, ((0, TILE_ROWS - 2), (0, TILE_COLS - agg)))
        got = lax.all_gather(jnp.concatenate([values, numbers[None]]), "row", axis=0)
        dest = got[:, agg, 0, :agg].astype(jnp.int32)
        ids = got[:, agg, 1, :agg].astype(jnp.int32)
        landing = jnp.where(dest == lax.axis_index("row"), ids, tiles_dev)
        landing = jnp.pad(landing, ((0, 0), (0, 1)), constant_values=tiles_dev)
        return got.reshape(-1, TILE_ROWS, TILE_COLS), landing.reshape(-1)
    matches = (targets[:, None] == jnp.arange(row_devices, dtype=jnp.int32)[None, :]).astype(
        jnp.int32
    )
    earlier = jnp.cumsum(matches, axis=0) - matches
    position = targets * CAP + jnp.sum(earlier * matches, axis=1)
    slots = row_devices * CAP
    send_values = jnp.zeros((slots, TILE_ROWS, TILE_COLS), jnp.float32).at[position].set(values)
    send_ids = jnp.full((slots,), tiles_dev, jnp.int32).at[position].set(tile_ids)
    got = lax.all_to_all(send_values, "row", split_axis=0, concat_axis=0, tiled=True)
    ids = lax.all_to_all(send_ids, "row", split_axis=0, concat_axis=0, tiled=True)
    return got, ids


def order_tiles(landing, slots, tiles_dev, tile_cols, bm, bn, n_i, n_j):
    row = (landing // tile_cols) * TILE_ROWS
    col = (landing % tile_cols) * TILE_COLS
    count = landing.shape[0]
    number = jnp.arange(count, dtype=jnp.int32)
    step = jnp.where(landing < tiles_dev, (row // bm) * n_j + col // bn, n_i * n_j)
    key = step * count + number
    rank = jnp.sum((key[None, :] < key[:, None]).astype(jnp.int32), axis=1)
    hit = (rank[None, :] == jnp.arange(slots, dtype=jnp.int32)[:, None]).astype(jnp.int32)
    fields = jnp.stack([number, row % bm, col % bn])
    entries = jnp.sum(hit[None] * fields[:, None, :], axis=2)
    edges = jnp.arange(n_i * n_j + 1, dtype=jnp.int32)
    starts = jnp.sum((step[None, :] < edges[:, None]).astype(jnp.int32), axis=1)
    return entries, starts


def per_device(diag_inverse, panel, trailing, agg_vals, agg_dest, agg_tile):
    row_devices = lax.axis_size("row")
    col_devices = lax.axis_size("col")
    local_rows, local_cols = trailing.shape
    col_index = lax.axis_index("col")
    row_index = lax.axis_index("row")
    tile_cols = local_cols // TILE_COLS
    tiles_dev = (local_rows // TILE_ROWS) * tile_cols
    bm = 512 if local_rows % 512 == 0 else local_rows
    bn = 768
    n_i, n_j = local_rows // bm, local_cols // bn

    agg, landing = exchange_tiles(agg_vals, agg_dest, agg_tile, tiles_dev)

    if row_devices == 8 and col_devices == 4:
        half = local_rows // 2
        role = (row_index // 2) ^ col_index
        core = row_index % 2
        siblings = [(p, p ^ 1) for p in range(row_devices)]
        ring = list(NEXT.items())
        parts = [(panel[:half], panel[half:])]
        for _ in range(3):
            parts.append(tuple(lax.ppermute(x, "col", ring) for x in parts[-1]))
        mine, other = [], []
        move = functools.partial(hop, row_devices=row_devices, col_devices=col_devices)
        for first, second in parts:
            a1 = move(first, 0, 1)
            b1 = move(second, 0, 2)
            a2 = move(a1, 1, 3)
            b2 = move(b1, 2, 3)
            a3 = move(a2, 3, 2)
            b3 = move(b2, 3, 1)
            got = pick(role.reshape(1), (first, a1, a3, a2), (second, b3, b1, b2))
            mine.append(got)
            other.append(lax.ppermute(got, "row", siblings))
        sources = [jnp.arange(4, dtype=jnp.int32)]
        back = jnp.array([PREV[q] for q in range(4)], jnp.int32)
        for _ in range(3):
            sources.append(back[sources[-1]])
        order = jnp.stack(sources)[:, col_index]
        place = jnp.concatenate(
            [order, jnp.stack([core * local_rows, (1 - core) * local_rows, col_index])]
        ).astype(jnp.int32)
        own = [x for pieces in parts for x in pieces]
        own_plan = [(s, r * half, half) for s in range(4) for r in range(2)]
        pair = mine + other
        pair_plan = [(s, b, 0, local_rows) for b in range(2) for s in range(4)]
    else:
        whole = lax.all_gather(panel, "col", axis=0)
        column = lax.all_gather(panel, "row", axis=0, tiled=True)
        column = column.reshape(col_devices, local_cols, panel.shape[1])
        partner = lax.all_to_all(column, "col", split_axis=0, concat_axis=0, tiled=True)
        own = [whole[s] for s in range(col_devices)]
        own_plan = [(s, 0, local_rows) for s in range(col_devices)]
        pair = [partner[s] for s in range(col_devices)]
        pair_plan = [(s, 0, 0, local_cols) for s in range(col_devices)]
        place = jnp.concatenate(
            [jnp.arange(4), jnp.zeros(2, jnp.int32), col_index.reshape(1)]
        ).astype(jnp.int32)

    entries, starts = order_tiles(
        landing, row_devices * CAP, tiles_dev, tile_cols, bm, bn, n_i, n_j
    )
    return front(
        place,
        entries,
        starts,
        diag_inverse,
        agg,
        trailing,
        own,
        own_plan,
        pair,
        pair_plan,
        bm,
        bn,
    )


def solution(mesh):
    in_specs = (
        P(),
        P("row", "col"),
        P("row", "col"),
        P("row", "col", None, None),
        P("row", "col", None, None),
        P("row", "col", None),
    )
    out_specs = (P("row", "col"), P("row", "col"))
    return jax.shard_map(
        per_device, mesh=mesh, in_specs=in_specs, out_specs=out_specs, check_vma=False
    )
```

time: 337 us -> 246 us (0.73)
  the two profiles are of different devices: /device:TPU:0 before, /device:TPU:25 now
where the time goes in v1:
time: 246 us; the launch traced here: 245 us
  Pallas kernels  137 us (56%)
  starting transfers between devices  56.1 us (23%)
  waiting for transfers between devices  24.9 us (10%)
  blocking collectives  16.1 us (7%)
  local copies, waits for them, and re-layouts  5.96 us (2%)
  other arithmetic  3.78 us (2%)
    pallas_call x4, Pallas kernels, pick(): pl.pallas_call(pick_kernel, out_shape=jax.ShapeDtypeStruct((2 * rows, wid...  99.8 us
    ppermute x24, starting transfers between devices, hop(): return lax.ppermute(x, BOTH, perm)  45.8 us
    pallas_call x1, Pallas kernels, front(): pl.pallas_call(functools.partial(front_kernel, own_plan, pair_plan, bm, b...  36.8 us
    ppermute x6, waiting for transfers between devices, per_device(): parts.append(tuple((lax.ppermute(x, 'col', ring) for x in parts[-1])))  21.7 us
    all_gather x1, blocking collectives, exchange_tiles(): lax.all_gather(jnp.concatenate([values, numbers[None]]), 'row', axis=0)  16.1 us
    ppermute x6, starting transfers between devices, per_device(): parts.append(tuple((lax.ppermute(x, 'col', ring) for x in parts[-1])))  8.49 us
  transfers between devices with their start and end apart: 34, of which 9 were waited for; matrix products, arithmetic and copies ran while one was open for 3% of the time, Pallas kernels for 41%

profile of v1, /device:TPU:25, one launch (start us, length us, event | category | flops | bytes accessed | tf_op | source)
XLA Modules:
  0.0 244.5 jit_solution(15372192345956279374)
XLA Ops:
  4.0 2.0 collective-permute-start
  7.3 6.1 %collective-permute-done.1.refs_4_.refs_3_ = f32[768,128]{1,0:T(8,128)S(1)} collective-permute-done((f32[768,128]{1,0:T(8,128)S(1)}, f32[768,128]{1,0:T(8,128)S(1)}, u32[]{:S(2)}, u32[]{:S(2)}) %collective-permute-start.1) | collective-permute-done | bytes 393248 | tf_op jit(solution)/shard_map/ppermute | solution.py:272
  14.1 3.1 %collective-permute-start.3 = (f32[768,128]{1,0:T(8,128)S(1)}, f32[768,128]{1,0:T(8,128)S(1)}, u32[]{:S(2)}, u32[]{:S(2)}) collective-permute-start(f32[768,128]{1,0:T(8,128)S(1)} %collective-permute-done.1.refs_4_.refs_3_), channel_id=1, source_target_pairs={{0,1},{1,3},{3,2},{2,0},{4,5},{5,7},{7,6},{6,4},{8,9},{9,11},{11,1... | collective-permute-start | bytes 1179656 | tf_op jit(solution)/shard_map/ppermute | solution.py:272
  18.6 3.3 %collective-permute-done.refs_0_.refs_2_ = f32[768,128]{1,0:T(8,128)S(1)} collective-permute-done((f32[768,128]{1,0:T(8,128)S(1)}, f32[768,128]{1,0:T(8,128)S(1)}, u32[]{:S(2)}, u32[]{:S(2)}) %collective-permute-start) | collective-permute-done | bytes 393248 | tf_op jit(solution)/shard_map/ppermute | solution.py:272
  24.2 6.1 %collective-permute-start.11 = (f32[768,128]{1,0:T(8,128)}, f32[768,128]{1,0:T(8,128)}, u32[]{:S(2)}, u32[]{:S(2)}) collective-permute-start(f32[768,128]{1,0:T(8,128)} %collective-permute-done.10.refs_7_), channel_id=1, source_target_pairs={{24,8},{28,12},{17,1},{21,5},{10,26},{14,30},{3,19},{7,23}} | collective-permute-start | bytes 1179656 | tf_op jit(solution)/shard_map/ppermute | solution.py:33
  33.0 2.5 %collective-permute-start.5 = (f32[768,128]{1,0:T(8,128)S(1)}, f32[768,128]{1,0:T(8,128)S(1)}, u32[]{:S(2)}, u32[]{:S(2)}) collective-permute-start(f32[768,128]{1,0:T(8,128)S(1)} %collective-permute-done.3.refs_4_.refs_5_), channel_id=1, source_target_pairs={{0,1},{1,3},{3,2},{2,0},{4,5},{5,7},{7,6},{6,4},{8,9},{9,11},{11,1... | collective-permute-start | bytes 1179656 | tf_op jit(solution)/shard_map/ppermute | solution.py:272
  35.6 3.2 %collective-permute-done.2.refs_0_.refs_4_ = f32[768,128]{1,0:T(8,128)S(1)} collective-permute-done((f32[768,128]{1,0:T(8,128)S(1)}, f32[768,128]{1,0:T(8,128)S(1)}, u32[]{:S(2)}, u32[]{:S(2)}) %collective-permute-start.2) | collective-permute-done | bytes 393248 | tf_op jit(solution)/shard_map/ppermute | solution.py:272
  40.2 3.7 %collective-permute-start.8 = (f32[768,128]{1,0:T(8,128)}, f32[768,128]{1,0:T(8,128)S(1)}, u32[]{:S(2)}, u32[]{:S(2)}) collective-permute-start(f32[768,128]{1,0:T(8,128)} %copy-done.15), channel_id=1, source_target_pairs={{24,16},{28,20},{17,25},{21,29},{10,2},{14,6},{3,11},{7,15}} | collective-permute-start | bytes 1179656 | tf_op jit(solution)/shard_map/ppermute | solution.py:33
  45.2 1.9 collective-permute-done.5.refs_4_.refs_7_
  48.6 7.1 %collective-permute-done.4.refs_0_.refs_6_ = f32[768,128]{1,0:T(8,128)} collective-permute-done((f32[768,128]{1,0:T(8,128)S(1)}, f32[768,128]{1,0:T(8,128)}, u32[]{:S(2)}, u32[]{:S(2)}) %collective-permute-start.4) | collective-permute-done | bytes 393248 | tf_op jit(solution)/shard_map/ppermute | solution.py:272
  58.6 16.1 %all-gather.agg_ref = f32[104,8,128]{2,1,0:T(8,128)S(1)} all-gather(f32[13,8,128]{2,1,0:T(8,128)S(1)} %pad_maximum_fusion), channel_id=2, replica_groups=mesh['row'=8,'col'=4] {'row'}, dimensions={0}, use_global_device_ids=true | all-gather | bytes 479232 | tf_op jit(solution)/shard_map/all_gather | solution.py:215
  74.8 2.1 collective-permute-start.17
  82.7 2.6 %copy.14 = f32[512,512]{0,1:T(8,128)} copy(f32[512,512]{1,0:T(8,128)} %d_ref.1) | data formatting | bytes 2097152 | tf_op args[0]
  86.0 6.4 %collective-permute-start.14 = (f32[768,128]{1,0:T(8,128)}, f32[768,128]{1,0:T(8,128)}, u32[]{:S(2)}, u32[]{:S(2)}) collective-permute-start(f32[768,128]{1,0:T(8,128)} %copy-done.16), channel_id=1, source_target_pairs={{24,16},{28,20},{17,25},{21,29},{10,2},{14,6},{3,11},{7,15}} | collective-permute-start | bytes 1179656 | tf_op jit(solution)/shard_map/ppermute | solution.py:33
  92.4 2.1 collective-permute-start.23
  94.4 2.0 collective-permute-start.20
  96.5 1.5 collective-permute-done.28.refs_7_
  98.0 2.0 collective-permute-start.29
  100.1 2.0 collective-permute-start.26
  102.7 25.0 %pick.4.refs_8_ = f32[1536,128]{1,0:T(8,128)} custom-call(s32[1]{0:T(128)} %bitcast.11.role_ref, f32[768,128]{1,0:T(8,128)} %copy-done.1, f32[768,128]{1,0:T(8,128)} %copy-done.13, f32[768,128]{1,0:T(8,128)} %copy-done.17, f32[768,128]{1,0:T(8,128)} %copy-done.15, f32[768,128]{1,0:T(8,128)} %copy-done, f32[768,128]{1,0:T(8,128)} %collective-permute-done.11.refs_5_, ...), custom_call_target="tpu_custom_call" | custom-call | tf_op jit(solution)/shard_map/pick/pallas_call | solution.py:55
  128.7 24.9 %pick.5.refs_9_ = f32[1536,128]{1,0:T(8,128)} custom-call(s32[1]{0:T(128)} %bitcast.11.role_ref, f32[768,128]{1,0:T(8,128)} %copy-done.4, f32[768,128]{1,0:T(8,128)} %collective-permute-done.12.refs_1_, f32[768,128]{1,0:T(8,128)} %collective-permute-done.14.refs_2_, f32[768,128]{1,0:T(8,128)} %copy-done.16, f32[768,128]{1,0:T(8,128)} %copy-done.3, ...), custom_call_target="tpu_custom_call" | custom-call | tf_op jit(solution)/shard_map/pick/pallas_call | solution.py:55
  153.8 25.0 %pick.6.refs_10_ = f32[1536,128]{1,0:T(8,128)} custom-call(s32[1]{0:T(128)} %bitcast.11.role_ref, f32[768,128]{1,0:T(8,128)} %copy-done.6, f32[768,128]{1,0:T(8,128)} %collective-permute-done.18.refs_1_, f32[768,128]{1,0:T(8,128)} %collective-permute-done.20.refs_2_, f32[768,128]{1,0:T(8,128)} %collective-permute-done.19.refs_3_, f32[768,128]{1,0:T(8,128)} %copy-done.5, ...), custom_call_target="tpu_custom_call" | custom-call | tf_op jit(solution)/shard_map/pick/pallas_call | solution.py:55
  179.3 25.0 %pick.7.refs_11_ = f32[1536,128]{1,0:T(8,128)} custom-call(s32[1]{0:T(128)} %bitcast.11.role_ref, f32[768,128]{1,0:T(8,128)} %collective-permute-done.4.refs_0_.refs_6_, f32[768,128]{1,0:T(8,128)} %collective-permute-done.24.refs_1_, f32[768,128]{1,0:T(8,128)} %collective-permute-done.26.refs_2_, f32[768,128]{1,0:T(8,128)} %collective-permute-done.25.refs_3_, ...), custom_call_target="tpu_custom_call" | custom-call | tf_op jit(solution)/shard_map/pick/pallas_call | solution.py:55
  207.7 36.8 %front.1 = (f32[1536,3072]{1,0:T(8,128)}, f32[1536,128]{1,0:T(8,128)}) custom-call(s32[7]{0:T(128)} %pad_add_fusion.1.place_ref, s32[3,16]{1,0:T(4,128)} %multiply_reduce_fusion.entry_ref, s32[13]{0:T(128)} %convert_reduce_fusion.1.start_ref, f32[512,512]{1,0:T(8,128)} %d_ref.1, f32[512,512]{1,0:T(8,128)} %bitcast.14, f32[104,8,128]{2,1,0:T(8,128)} %copy-done.2, ...), custom_call_target="tpu_custom_call" | custom-call | tf_op jit(solution)/shard_map/front/pallas_call | solution.py:177
  (111 shorter events, 30.9 us)
Async XLA Ops:
  4.0 17.9 %collective-permute-start = (f32[768,128]{1,0:T(8,128)S(1)}, f32[768,128]{1,0:T(8,128)S(1)}, u32[]{:S(2)}, u32[]{:S(2)}) collective-permute-start(f32[768,128]{1,0:T(8,128)S(1)} %get-tuple-element.5.refs_0_), channel_id=1, source_target_pairs={{0,1},{1,3},{3,2},{2,0},{4,5},{5,7},{7,6},{6,4},{8,9},{9,11},{11,1... | collective-permute-start | bytes 1179656 | tf_op jit(solution)/shard_map/ppermute | solution.py:272
  6.0 18.1 %collective-permute-start.10 = (f32[768,128]{1,0:T(8,128)S(1)}, f32[768,128]{1,0:T(8,128)}, u32[]{:S(2)}, u32[]{:S(2)}) collective-permute-start(f32[768,128]{1,0:T(8,128)S(1)} %collective-permute-done.9.refs_6_), channel_id=1, source_target_pairs={{16,24},{20,28},{25,17},{29,21},{2,10},{6,14},{11,3},{15,7}} | collective-permute-start | bytes 1179656 | tf_op jit(solution)/shard_map/ppermute | solution.py:33
  14.1 16.2 %collective-permute-start.3 = (f32[768,128]{1,0:T(8,128)S(1)}, f32[768,128]{1,0:T(8,128)S(1)}, u32[]{:S(2)}, u32[]{:S(2)}) collective-permute-start(f32[768,128]{1,0:T(8,128)S(1)} %collective-permute-done.1.refs_4_.refs_3_), channel_id=1, source_target_pairs={{0,1},{1,3},{3,2},{2,0},{4,5},{5,7},{7,6},{6,4},{8,9},{9,11},{11,1... | collective-permute-start | bytes 1179656 | tf_op jit(solution)/shard_map/ppermute | solution.py:272
  17.3 14.3 %collective-permute-start.7 = (f32[768,128]{1,0:T(8,128)S(1)}, f32[768,128]{1,0:T(8,128)S(1)}, u32[]{:S(2)}, u32[]{:S(2)}) collective-permute-start(f32[768,128]{1,0:T(8,128)S(1)} %collective-permute-done.6.refs_1_), channel_id=1, source_target_pairs={{8,24},{12,28},{1,17},{5,21},{26,10},{30,14},{19,3},{23,7}} | collective-permute-start | bytes 1179656 | tf_op jit(solution)/shard_map/ppermute | solution.py:33
  24.2 14.6 %collective-permute-start.2 = (f32[768,128]{1,0:T(8,128)S(1)}, f32[768,128]{1,0:T(8,128)S(1)}, u32[]{:S(2)}, u32[]{:S(2)}) collective-permute-start(f32[768,128]{1,0:T(8,128)S(1)} %collective-permute-done.refs_0_.refs_2_), channel_id=1, source_target_pairs={{0,1},{1,3},{3,2},{2,0},{4,5},{5,7},{7,6},{6,4},{8,9},{9,11},{11,1... | collective-permute-start | bytes 1179656 | tf_op jit(solution)/shard_map/ppermute | solution.py:272
  24.2 14.6 %collective-permute-start.11 = (f32[768,128]{1,0:T(8,128)}, f32[768,128]{1,0:T(8,128)}, u32[]{:S(2)}, u32[]{:S(2)}) collective-permute-start(f32[768,128]{1,0:T(8,128)} %collective-permute-done.10.refs_7_), channel_id=1, source_target_pairs={{24,8},{28,12},{17,1},{21,5},{10,26},{14,30},{3,19},{7,23}} | collective-permute-start | bytes 1179656 | tf_op jit(solution)/shard_map/ppermute | solution.py:33
  38.7 17.0 %collective-permute-start.4 = (f32[768,128]{1,0:T(8,128)S(1)}, f32[768,128]{1,0:T(8,128)}, u32[]{:S(2)}, u32[]{:S(2)}) collective-permute-start(f32[768,128]{1,0:T(8,128)S(1)} %collective-permute-done.2.refs_0_.refs_4_), channel_id=1, source_target_pairs={{0,1},{1,3},{3,2},{2,0},{4,5},{5,7},{7,6},{6,4},{8,9},{9,11},{11,1... | collective-permute-start | bytes 1179656 | tf_op jit(solution)/shard_map/ppermute | solution.py:272
  38.8 39.4 %collective-permute-start.18 = (f32[768,128]{1,0:T(8,128)S(1)}, f32[768,128]{1,0:T(8,128)}, u32[]{:S(2)}, u32[]{:S(2)}) collective-permute-start(f32[768,128]{1,0:T(8,128)S(1)} %collective-permute-done.2.refs_0_.refs_4_), channel_id=1, source_target_pairs={{0,8},{4,12},{9,1},{13,5},{18,26},{22,30},{27,19},{31,23}} | collective-permute-start | bytes 1179656 | tf_op jit(solution)/shard_map/ppermute | solution.py:33
  40.2 34.6 %collective-permute-start.8 = (f32[768,128]{1,0:T(8,128)}, f32[768,128]{1,0:T(8,128)S(1)}, u32[]{:S(2)}, u32[]{:S(2)}) collective-permute-start(f32[768,128]{1,0:T(8,128)} %copy-done.15), channel_id=1, source_target_pairs={{24,16},{28,20},{17,25},{21,29},{10,2},{14,6},{3,11},{7,15}} | collective-permute-start | bytes 1179656 | tf_op jit(solution)/shard_map/ppermute | solution.py:33
  43.9 32.9 %collective-permute-start.13 = (f32[768,128]{1,0:T(8,128)}, f32[768,128]{1,0:T(8,128)S(1)}, u32[]{:S(2)}, u32[]{:S(2)}) collective-permute-start(f32[768,128]{1,0:T(8,128)} %collective-permute-done.12.refs_1_), channel_id=1, source_target_pairs={{8,24},{12,28},{1,17},{5,21},{26,10},{30,14},{19,3},{23,7}} | collective-permute-start | bytes 1179656 | tf_op jit(solution)/shard_map/ppermute | solution.py:33
  47.2 32.3 %collective-permute-start.27 = (f32[768,128]{1,0:T(8,128)S(1)}, f32[768,128]{1,0:T(8,128)}, u32[]{:S(2)}, u32[]{:S(2)}) collective-permute-start(f32[768,128]{1,0:T(8,128)S(1)} %collective-permute-done.5.refs_4_.refs_7_), channel_id=1, source_target_pairs={{0,16},{4,20},{9,25},{13,29},{18,2},{22,6},{27,11},{31,15}} | collective-permute-start | bytes 1179656 | tf_op jit(solution)/shard_map/ppermute | solution.py:33
  55.7 25.1 %collective-permute-start.24 = (f32[768,128]{1,0:T(8,128)}, f32[768,128]{1,0:T(8,128)}, u32[]{:S(2)}, u32[]{:S(2)}) collective-permute-start(f32[768,128]{1,0:T(8,128)} %collective-permute-done.4.refs_0_.refs_6_), channel_id=1, source_target_pairs={{0,8},{4,12},{9,1},{13,5},{18,26},{22,30},{27,19},{31,23}} | collective-permute-start | bytes 1179656 | tf_op jit(solution)/shard_map/ppermute | solution.py:33
  76.8 15.6 %collective-permute-start.22 = (f32[768,128]{1,0:T(8,128)}, f32[768,128]{1,0:T(8,128)}, u32[]{:S(2)}, u32[]{:S(2)}) collective-permute-start(f32[768,128]{1,0:T(8,128)} %collective-permute-done.21.refs_6_), channel_id=1, source_target_pairs={{16,24},{20,28},{25,17},{29,21},{2,10},{6,14},{11,3},{15,7}} | collective-permute-start | bytes 1179656 | tf_op jit(solution)/shard_map/ppermute | solution.py:33
  78.1 16.3 %collective-permute-start.19 = (f32[768,128]{1,0:T(8,128)}, f32[768,128]{1,0:T(8,128)}, u32[]{:S(2)}, u32[]{:S(2)}) collective-permute-start(f32[768,128]{1,0:T(8,128)} %collective-permute-done.18.refs_1_), channel_id=1, source_target_pairs={{8,24},{12,28},{1,17},{5,21},{26,10},{30,14},{19,3},{23,7}} | collective-permute-start | bytes 1179656 | tf_op jit(solution)/shard_map/ppermute | solution.py:33
  79.4 18.6 %collective-permute-start.28 = (f32[768,128]{1,0:T(8,128)}, f32[768,128]{1,0:T(8,128)}, u32[]{:S(2)}, u32[]{:S(2)}) collective-permute-start(f32[768,128]{1,0:T(8,128)} %collective-permute-done.27.refs_6_), channel_id=1, source_target_pairs={{16,24},{20,28},{25,17},{29,21},{2,10},{6,14},{11,3},{15,7}} | collective-permute-start | bytes 1179656 | tf_op jit(solution)/shard_map/ppermute | solution.py:33
  80.8 19.3 %collective-permute-start.25 = (f32[768,128]{1,0:T(8,128)}, f32[768,128]{1,0:T(8,128)}, u32[]{:S(2)}, u32[]{:S(2)}) collective-permute-start(f32[768,128]{1,0:T(8,128)} %collective-permute-done.24.refs_1_), channel_id=1, source_target_pairs={{8,24},{12,28},{1,17},{5,21},{26,10},{30,14},{19,3},{23,7}} | collective-permute-start | bytes 1179656 | tf_op jit(solution)/shard_map/ppermute | solution.py:33
  86.0 41.7 %collective-permute-start.14 = (f32[768,128]{1,0:T(8,128)}, f32[768,128]{1,0:T(8,128)}, u32[]{:S(2)}, u32[]{:S(2)}) collective-permute-start(f32[768,128]{1,0:T(8,128)} %copy-done.16), channel_id=1, source_target_pairs={{24,16},{28,20},{17,25},{21,29},{10,2},{14,6},{3,11},{7,15}} | collective-permute-start | bytes 1179656 | tf_op jit(solution)/shard_map/ppermute | solution.py:33
  92.4 61.3 %collective-permute-start.23 = (f32[768,128]{1,0:T(8,128)}, f32[768,128]{1,0:T(8,128)}, u32[]{:S(2)}, u32[]{:S(2)}) collective-permute-start(f32[768,128]{1,0:T(8,128)} %collective-permute-done.22.refs_7_), channel_id=1, source_target_pairs={{24,8},{28,12},{17,1},{21,5},{10,26},{14,30},{3,19},{7,23}} | collective-permute-start | bytes 1179656 | tf_op jit(solution)/shard_map/ppermute | solution.py:33
  94.4 59.4 %collective-permute-start.20 = (f32[768,128]{1,0:T(8,128)}, f32[768,128]{1,0:T(8,128)}, u32[]{:S(2)}, u32[]{:S(2)}) collective-permute-start(f32[768,128]{1,0:T(8,128)} %collective-permute-done.19.refs_3_), channel_id=1, source_target_pairs={{24,16},{28,20},{17,25},{21,29},{10,2},{14,6},{3,11},{7,15}} | collective-permute-start | bytes 1179656 | tf_op jit(solution)/shard_map/ppermute | solution.py:33
  98.0 81.3 %collective-permute-start.29 = (f32[768,128]{1,0:T(8,128)}, f32[768,128]{1,0:T(8,128)}, u32[]{:S(2)}, u32[]{:S(2)}) collective-permute-start(f32[768,128]{1,0:T(8,128)} %collective-permute-done.28.refs_7_), channel_id=1, source_target_pairs={{24,8},{28,12},{17,1},{21,5},{10,26},{14,30},{3,19},{7,23}} | collective-permute-start | bytes 1179656 | tf_op jit(solution)/shard_map/ppermute | solution.py:33
  100.1 79.3 %collective-permute-start.26 = (f32[768,128]{1,0:T(8,128)}, f32[768,128]{1,0:T(8,128)}, u32[]{:S(2)}, u32[]{:S(2)}) collective-permute-start(f32[768,128]{1,0:T(8,128)} %collective-permute-done.25.refs_3_), channel_id=1, source_target_pairs={{24,16},{28,20},{17,25},{21,29},{10,2},{14,6},{3,11},{7,15}} | collective-permute-start | bytes 1179656 | tf_op jit(solution)/shard_map/ppermute | solution.py:33
  127.7 78.4 %collective-permute-start.30 = (f32[1536,128]{1,0:T(8,128)}, f32[1536,128]{1,0:T(8,128)S(1)}, u32[]{:S(2)}, u32[]{:S(2)}) collective-permute-start(f32[1536,128]{1,0:T(8,128)} %pick.4.refs_8_), channel_id=1, source_target_pairs={{0,4},{4,0},{8,12},{12,8},{16,20},{20,16},{24,28},{28,24},{1,5},{5... | collective-permute-start | bytes 2359304 | tf_op jit(solution)/shard_map/ppermute | solution.py:284
  153.7 52.4 %collective-permute-start.31 = (f32[1536,128]{1,0:T(8,128)}, f32[1536,128]{1,0:T(8,128)S(1)}, u32[]{:S(2)}, u32[]{:S(2)}) collective-permute-start(f32[1536,128]{1,0:T(8,128)} %pick.5.refs_9_), channel_id=1, source_target_pairs={{0,4},{4,0},{8,12},{12,8},{16,20},{20,16},{24,28},{28,24},{1,5},{5... | collective-permute-start | bytes 2359304 | tf_op jit(solution)/shard_map/ppermute | solution.py:284
  178.8 27.3 %collective-permute-start.32 = (f32[1536,128]{1,0:T(8,128)}, f32[1536,128]{1,0:T(8,128)S(1)}, u32[]{:S(2)}, u32[]{:S(2)}) collective-permute-start(f32[1536,128]{1,0:T(8,128)} %pick.6.refs_10_), channel_id=1, source_target_pairs={{0,4},{4,0},{8,12},{12,8},{16,20},{20,16},{24,28},{28,24},{1,5},{5... | collective-permute-start | bytes 2359304 | tf_op jit(solution)/shard_map/ppermute | solution.py:284
  (28 other events, 1130.2 us)

commit v2 on v0

v2 whole, which is shorter than its diff:
```python
import functools

import jax
import jax.numpy as jnp
from jax import lax
from jax.experimental import pallas as pl
from jax.experimental.pallas import tpu as pltpu
from jax.sharding import PartitionSpec as P

TILE_ROWS = 8
TILE_COLS = 128
CAP = 2
NEXT = {0: 1, 1: 3, 3: 2, 2: 0}
PREV = {v: k for k, v in NEXT.items()}
NN = (((1,), (0,)), ((), ()))
NT = (((1,), (1,)), ((), ()))


def split(x):
    hi = x.astype(jnp.bfloat16)
    lo = (x - hi.astype(jnp.float32)).astype(jnp.bfloat16)
    return hi, lo


def own_kernel(plan, rows_step, place_ref, d_ref, *refs):
    pieces = refs[: len(plan)]
    halves_ref, block_ref, stage, dtcat, full_ref, sem = refs[len(plan) :]
    width = d_ref.shape[0]
    part = stage.shape[1] // 4
    todo = []
    for n, (s, row, rows) in enumerate(plan):
        lanes = pl.ds(pl.multiple_of(place_ref[s] * part, part), part)
        todo.append(
            pltpu.make_async_copy(pieces[n], stage.at[pl.ds(row, rows), lanes], sem.at[n])
        )
    for c in todo:
        c.start()
    hi, lo = split(d_ref[...].T)
    dtcat[0:width, :] = hi
    dtcat[width : 2 * width, :] = hi
    dtcat[2 * width :, :] = lo
    for c in todo:
        c.wait()
    mine = pl.ds(pl.multiple_of(place_ref[4] * part, part), part)

    def body(n, carry):
        at = pl.ds(pl.multiple_of(n * rows_step, rows_step), rows_step)
        hi, lo = split(stage[at, :])
        lhs = jnp.concatenate([hi, lo, hi], axis=1)
        full = lax.dot_general(lhs, dtcat[...], NN, preferred_element_type=jnp.float32)
        full_ref[...] = full
        block_ref[at, :] = full_ref[:, mine]
        hi, lo = split(full)
        halves_ref[at, 0:width] = hi
        halves_ref[at, width:] = lo
        return carry

    lax.fori_loop(0, stage.shape[0] // rows_step, body, 0)


def own_factor(place, d, pieces, plan, rows, rows_step):
    width = d.shape[0]
    part = width // 4
    whole = pl.BlockSpec(memory_space=pltpu.VMEM)
    return pl.pallas_call(
        functools.partial(own_kernel, plan, rows_step),
        out_shape=(
            jax.ShapeDtypeStruct((rows, 2 * width), jnp.bfloat16),
            jax.ShapeDtypeStruct((rows, part), jnp.float32),
        ),
        in_specs=[pl.BlockSpec(memory_space=pltpu.SMEM), whole]
        + [pl.BlockSpec(memory_space=pl.ANY)] * len(pieces),
        out_specs=(whole, whole),
        scratch_shapes=[
            pltpu.VMEM((rows, width), jnp.float32),
            pltpu.VMEM((3 * width, width), jnp.bfloat16),
            pltpu.VMEM((rows_step, width), jnp.float32),
            pltpu.SemaphoreType.DMA((len(pieces),)),
        ],
        compiler_params=pltpu.CompilerParams(vmem_limit_bytes=40 << 20),
        cost_estimate=pl.CostEstimate(
            flops=6 * rows * width * width, bytes_accessed=10 * rows * width, transcendentals=0
        ),
        name="own_factor",
    )(place, d, *pieces)


def front_kernel(
    first, entry_ref, start_ref, d_ref, agg_ref, pair_ref, own_ref, trail_ref, *refs
):
    out_ref, dcat, pair_cat = refs[-3:]
    j, i = pl.program_id(0), pl.program_id(1)
    n_i = pl.num_programs(1)
    bm, bn = out_ref.shape
    width = d_ref.shape[0]
    part = width // 4

    @pl.when((i == 0) & (j == 0))
    def _():
        hi, lo = split(d_ref[...])
        dcat[:, 0:width] = hi
        dcat[:, width : 2 * width] = hi
        dcat[:, 2 * width :] = lo

    @pl.when(i == 0)
    def _():
        panel = jnp.concatenate([pair_ref[:, s].reshape(bn, part) for s in range(4)], axis=1)
        hi, lo = split(panel)
        rhs = jnp.concatenate([hi, lo, hi], axis=1)
        turned = lax.dot_general(dcat[...], rhs, NT, preferred_element_type=jnp.float32)
        hi, lo = split(turned)
        pair_cat[0:width, :] = hi
        pair_cat[width : 2 * width, :] = lo
        pair_cat[2 * width :, :] = hi

    rows = pl.ds(pl.multiple_of(i * bm, bm), bm)
    hi, lo = own_ref[rows, 0:width], own_ref[rows, width:]
    lhs = jnp.concatenate([hi, hi, lo], axis=1)
    product = lax.dot_general(lhs, pair_cat[...], NN, preferred_element_type=jnp.float32)
    out_ref[...] = trail_ref[...] - product
    step = (first + j) * n_i + i

    def add(e, carry):
        r = pl.multiple_of(entry_ref[1, e], TILE_ROWS)
        c = pl.multiple_of(entry_ref[2, e], TILE_COLS)
        here = (pl.ds(r, TILE_ROWS), pl.ds(c, TILE_COLS))
        out_ref[here] = out_ref[here] + agg_ref[entry_ref[0, e]]
        return carry

    lax.fori_loop(start_ref[step], start_ref[step + 1], add, 0)


def front(entries, starts, d, agg, pair, own, trailing, before, first, n_j, bm, bn):
    rows, cols = trailing.shape
    width = d.shape[0]
    part = width // 4
    piece = pair.shape[2]
    if piece < bn:
        pair_block = pl.BlockSpec((bn // piece, 4, piece, part), lambda j, i: (j, 0, 0, 0))
    else:
        pair_block = pl.BlockSpec((1, 4, bn, part), lambda j, i: (0, 0, j, 0))
    whole = pl.BlockSpec(memory_space=pltpu.VMEM)
    smem = pl.BlockSpec(memory_space=pltpu.SMEM)
    block = pl.BlockSpec((bm, bn), lambda j, i: (i, first + j))
    operands = [entries, starts, d, agg, pair, own, trailing]
    specs = [smem, smem, whole, whole, pair_block, whole, block]
    aliases = {}
    if before is not None:
        aliases = {len(operands): 0}
        operands.append(before)
        specs.append(pl.BlockSpec(memory_space=pl.ANY))
    done = n_j * bn
    return pl.pallas_call(
        functools.partial(front_kernel, first),
        grid=(n_j, rows // bm),
        out_shape=jax.ShapeDtypeStruct((rows, cols), jnp.float32),
        in_specs=specs,
        out_specs=block,
        scratch_shapes=[
            pltpu.VMEM((width, 3 * width), jnp.bfloat16),
            pltpu.VMEM((3 * width, bn), jnp.bfloat16),
        ],
        input_output_aliases=aliases,
        compiler_params=pltpu.CompilerParams(vmem_limit_bytes=44 << 20),
        cost_estimate=pl.CostEstimate(
            flops=6 * (rows + width) * width * done,
            bytes_accessed=8 * rows * done + 4 * width * done,
            transcendentals=0,
        ),
        name="front",
    )(*operands)


def exchange_tiles(agg_vals, agg_dest, agg_tile, tiles_dev):
    row_devices = lax.axis_size("row")
    agg = agg_vals.shape[2]
    targets = agg_dest.reshape(-1)
    tile_ids = agg_tile.reshape(-1)
    slots = row_devices * CAP
    order = jnp.arange(agg, dtype=jnp.int32)
    earlier = (targets[None, :] == targets[:, None]) & (order[None, :] < order[:, None])
    position = targets * CAP + jnp.sum(earlier.astype(jnp.int32), axis=1)
    hit = position[None, :] == jnp.arange(slots, dtype=jnp.int32)[:, None]
    send_ids = tiles_dev + jnp.sum(jnp.where(hit, tile_ids[None, :] - tiles_dev, 0), axis=1)
    values = agg_vals.reshape(agg, TILE_ROWS, TILE_COLS)
    send = jnp.zeros((slots, TILE_ROWS, TILE_COLS), jnp.float32).at[position].set(values)
    send = send.reshape(row_devices, CAP, TILE_ROWS, TILE_COLS)
    numbers = send_ids.astype(jnp.float32).reshape(row_devices, 1, 1, CAP)
    numbers = jnp.pad(numbers, ((0, 0), (0, 0), (0, TILE_ROWS - 1), (0, TILE_COLS - CAP)))
    got = lax.all_to_all(
        jnp.concatenate([send, numbers], axis=1), "row", split_axis=0, concat_axis=0, tiled=True
    )
    landing = got[:, CAP, 0, :CAP].astype(jnp.int32)
    landing = jnp.pad(landing, ((0, 0), (0, 1)), constant_values=tiles_dev)
    return got.reshape(-1, TILE_ROWS, TILE_COLS), landing.reshape(-1)


def order_tiles(landing, slots, tiles_dev, tile_cols, bm, bn, n_i, n_j):
    row = (landing // tile_cols) * TILE_ROWS
    col = (landing % tile_cols) * TILE_COLS
    count = landing.shape[0]
    number = jnp.arange(count, dtype=jnp.int32)
    step = jnp.where(landing < tiles_dev, (col // bn) * n_i + row // bm, n_i * n_j)
    key = step * count + number
    rank = jnp.sum((key[None, :] < key[:, None]).astype(jnp.int32), axis=1)
    hit = (rank[None, :] == jnp.arange(slots, dtype=jnp.int32)[:, None]).astype(jnp.int32)
    fields = jnp.stack([number, row % bm, col % bn])
    entries = jnp.sum(hit[None] * fields[:, None, :], axis=2)
    edges = jnp.arange(n_i * n_j + 1, dtype=jnp.int32)
    starts = jnp.sum((step[None, :] < edges[:, None]).astype(jnp.int32), axis=1)
    return entries, starts


def per_device(diag_inverse, panel, trailing, agg_vals, agg_dest, agg_tile):
    row_devices = lax.axis_size("row")
    col_devices = lax.axis_size("col")
    local_rows, local_cols = trailing.shape
    part = panel.shape[1]
    col_index = lax.axis_index("col")
    tile_cols = local_cols // TILE_COLS
    tiles_dev = (local_rows // TILE_ROWS) * tile_cols
    bm = 512 if local_rows % 512 == 0 else local_rows
    bn = 768
    n_i, n_j = local_rows // bm, local_cols // bn

    if row_devices == 2 * col_devices and local_rows % (16 * row_devices) == 0:
        eighth = local_rows // row_devices
        spread = lax.all_to_all(
            panel.reshape(row_devices, eighth, part),
            "row",
            split_axis=0,
            concat_axis=0,
            tiled=True,
        )
        wanted = lax.all_to_all(
            spread.reshape(col_devices, 2, eighth, part),
            "col",
            split_axis=0,
            concat_axis=0,
            tiled=True,
        )
        pairs = [lax.all_gather(wanted[:, k], "row", axis=0) for k in range(2)]
        half = local_rows // 2
        ring = list(NEXT.items())
        parts = [(panel[:half], panel[half:])]
        for _ in range(3):
            parts.append(tuple(lax.ppermute(x, "col", ring) for x in parts[-1]))
        sources = [jnp.arange(4, dtype=jnp.int32)]
        back = jnp.array([PREV[q] for q in range(4)], jnp.int32)
        for _ in range(3):
            sources.append(back[sources[-1]])
        order = jnp.stack(sources)[:, col_index]
        own = [panel] + [x for pieces in parts[1:] for x in pieces]
        own_plan = [(0, 0, local_rows)]
        own_plan += [(s, r * half, half) for s in range(1, 4) for r in range(2)]
    else:
        whole = lax.all_gather(panel, "col", axis=0)
        column = lax.all_gather(panel, "row", axis=0, tiled=True)
        column = column.reshape(col_devices, local_cols, part)
        partner = lax.all_to_all(column, "col", split_axis=0, concat_axis=0, tiled=True)
        pairs = [partner[None]]
        own = [whole[s] for s in range(col_devices)]
        own_plan = [(s, 0, local_rows) for s in range(col_devices)]
        order = jnp.arange(4, dtype=jnp.int32)

    agg, landing = exchange_tiles(agg_vals, agg_dest, agg_tile, tiles_dev)
    entries, starts = order_tiles(
        landing, row_devices * CAP, tiles_dev, tile_cols, bm, bn, n_i, n_j
    )
    place = jnp.concatenate([order, col_index.reshape(1)]).astype(jnp.int32)
    halves, own_block = own_factor(place, diag_inverse, own, own_plan, local_rows, bm)
    updated = None
    calls = len(pairs)
    for h, pair in enumerate(pairs):
        updated = front(
            entries,
            starts,
            diag_inverse,
            agg,
            pair,
            halves,
            trailing,
            updated,
            h * (n_j // calls),
            n_j // calls,
            bm,
            bn,
        )
    return updated, own_block


def solution(mesh):
    in_specs = (
        P(),
        P("row", "col"),
        P("row", "col"),
        P("row", "col", None, None),
        P("row", "col", None, None),
        P("row", "col", None),
    )
    out_specs = (P("row", "col"), P("row", "col"))
    return jax.shard_map(
        per_device, mesh=mesh, in_specs=in_specs, out_specs=out_specs, check_vma=False
    )
```

time: 337 us -> 172 us (0.51)
  waiting for transfers between devices: 237 us -> 47.8 us
  matrix products: 43.3 us -> 0 us
  blocking collectives: 0 us -> 41.9 us
  Pallas kernels: 0 us -> 36.1 us
  starting transfers between devices: 12.5 us -> 5.48 us
  local copies, waits for them, and re-layouts: 27.1 us -> 21 us
    all_to_all x3 -> x1, waiting for transfers between devices: 139 us -> 1.15 us  [exchange_tiles(): lax.all_to_all(jnp.concatenate([send, numbers], axis=1), 'row', split_axi...]
    all_gather x2, waiting for transfers between devices: 97.7 us -> 0.02 us  [per_device(): pairs = [lax.all_gather(wanted[:, k], 'row', axis=0) for k in range(2)]]
    ppermute x0 -> x6, waiting for transfers between devices: none -> 46 us  [per_device(): parts.append(tuple((lax.ppermute(x, 'col', ring) for x in parts[-1])))]
    dot_general x2 -> x0, matrix products: 43.3 us -> none  [the longest x1 36 us: per_device(): lax.dot_general(own_full, partner, contract_last, precision=lax.Precision...]
    all_to_all x0 -> x2, blocking collectives: none -> 41.9 us  [the longest x1 24.2 us: per_device(): lax.all_to_all(spread.reshape(col_devices, 2, eighth, part), 'col', split...]
    pallas_call x0 -> x3, Pallas kernels: none -> 36.1 us  [the longest x2 30.8 us: front(): pl.pallas_call(functools.partial(front_kernel, first), grid=(n_j, rows //...]
    all_to_all x3 -> x1, starting transfers between devices: 12.4 us -> 3.36 us  [exchange_tiles(): lax.all_to_all(jnp.concatenate([send, numbers], axis=1), 'row', split_axi...]
    reshape x2 -> x0, local copies, waits for them, and re-layouts: 6.61 us -> none  [the longest x1 6.56 us: per_device(): split_rows = column_all.reshape(col_devices, local_cols, part_width)]
  transfers between devices with their start and end apart: 5 -> 9, of which waited for: 4 -> 7; matrix products, arithmetic and copies ran while one was open for 3% -> 5% of each run, Pallas kernels for 0% -> 12%
where the time goes in v2:
time: 172 us; the launch traced here: 171 us
  waiting for transfers between devices  47.8 us (28%)
  blocking collectives  41.9 us (24%)
  Pallas kernels  36.1 us (21%)
  local copies, waits for them, and re-layouts  21 us (12%)
  between operations  14.1 us (8%)
  starting transfers between devices  5.48 us (3%)
  other arithmetic  4.29 us (2%)
    ppermute x6, waiting for transfers between devices, per_device(): parts.append(tuple((lax.ppermute(x, 'col', ring) for x in parts[-1])))  46 us
    pallas_call x2, Pallas kernels, front(): pl.pallas_call(functools.partial(front_kernel, first), grid=(n_j, rows //...  30.8 us
    all_to_all x1, blocking collectives, per_device(): lax.all_to_all(spread.reshape(col_devices, 2, eighth, part), 'col', split...  24.2 us
    all_to_all x1, blocking collectives, per_device(): lax.all_to_all(panel.reshape(row_devices, eighth, part), 'row', split_axi...  17.7 us
    unnamed x29, local copies, waits for them, and re-layouts  15.6 us
    pallas_call x1, Pallas kernels, own_factor(): pl.pallas_call(functools.partial(own_kernel, plan, rows_step), out_shape=...  5.35 us
  transfers between devices with their start and end apart: 9, of which 7 were waited for; matrix products, arithmetic and copies ran while one was open for 5% of the time, Pallas kernels for 12%

profile of v2, /device:TPU:0, one launch (start us, length us, event | category | flops | bytes accessed | tf_op | source)
XLA Modules:
  0.0 170.8 jit_solution(4432778211567138525)
XLA Ops:
  7.2 17.7 %all_to_all.15 = f32[8,192,128]{2,1,0:T(8,128)S(1)} all-to-all(f32[8,192,128]{2,1,0:T(8,128)} %bitcast.27), channel_id=1, replica_groups=mesh['row'=8,'col'=4] {'row'}, dimensions={0} | all-to-all | bytes 1572864 | tf_op jit(solution)/shard_map/all_to_all | solution.py:228
  24.9 24.2 %all_to_all.16 = f32[4,2,192,128]{3,2,1,0:T(8,128)S(1)} all-to-all(f32[4,2,192,128]{3,2,1,0:T(8,128)S(1)} %bitcast.31), channel_id=1, replica_groups=mesh['row'=8,'col'=4] {'col'}, dimensions={0} | all-to-all | bytes 1572864 | tf_op jit(solution)/shard_map/all_to_all | solution.py:235
  53.9 1.5 scatter_fusion
  56.1 3.4 %all-to-all-start = ((f32[8,3,8,128]{3,2,1,0:T(8,128)}), f32[8,3,8,128]{3,2,1,0:T(8,128)S(1)}, u32[]{:S(2)}, u32[]{:S(2)}) async-start(f32[8,3,8,128]{3,2,1,0:T(8,128)} %select_maximum_fusion), calls=%async_computation | async-start | bytes 196608 | tf_op jit(solution)/shard_map/all_to_all | solution.py:190
  59.5 1.2 fusion.9
  60.9 1.8 %collective-permute-start = (f32[768,128]{1,0:T(8,128)S(1)}, f32[768,128]{1,0:T(8,128)S(1)}, u32[]{:S(2)}, u32[]{:S(2)}) collective-permute-start(f32[768,128]{1,0:T(8,128)S(1)} %get-tuple-element.11), channel_id=1, source_target_pairs={{0,1},{1,3},{3,2},{2,0},{4,5},{5,7},{7,6},{6,4},{8,9},{9,11},{11,1... | collective-permute-start | bytes 1179656 | tf_op jit(solution)/shard_map/ppermute | solution.py:247
  63.5 1.2 all-to-all-done
  65.5 8.1 %collective-permute-done.1.refs_2_ = f32[768,128]{1,0:T(8,128)S(1)} collective-permute-done((f32[768,128]{1,0:T(8,128)S(1)}, f32[768,128]{1,0:T(8,128)S(1)}, u32[]{:S(2)}, u32[]{:S(2)}) %collective-permute-start.1) | collective-permute-done | bytes 393248 | tf_op jit(solution)/shard_map/ppermute | solution.py:247
  74.3 7.7 %collective-permute-done.refs_1_ = f32[768,128]{1,0:T(8,128)S(1)} collective-permute-done((f32[768,128]{1,0:T(8,128)S(1)}, f32[768,128]{1,0:T(8,128)S(1)}, u32[]{:S(2)}, u32[]{:S(2)}) %collective-permute-start) | collective-permute-done | bytes 393248 | tf_op jit(solution)/shard_map/ppermute | solution.py:247
  83.3 7.1 %collective-permute-done.3.refs_4_ = f32[768,128]{1,0:T(8,128)S(1)} collective-permute-done((f32[768,128]{1,0:T(8,128)S(1)}, f32[768,128]{1,0:T(8,128)S(1)}, u32[]{:S(2)}, u32[]{:S(2)}) %collective-permute-start.3) | collective-permute-done | bytes 393248 | tf_op jit(solution)/shard_map/ppermute | solution.py:247
  91.1 7.7 %collective-permute-done.2.refs_3_ = f32[768,128]{1,0:T(8,128)S(1)} collective-permute-done((f32[768,128]{1,0:T(8,128)S(1)}, f32[768,128]{1,0:T(8,128)S(1)}, u32[]{:S(2)}, u32[]{:S(2)}) %collective-permute-start.2) | collective-permute-done | bytes 393248 | tf_op jit(solution)/shard_map/ppermute | solution.py:247
  99.7 7.5 %collective-permute-done.5.refs_6_ = f32[768,128]{1,0:T(8,128)S(1)} collective-permute-done((f32[768,128]{1,0:T(8,128)S(1)}, f32[768,128]{1,0:T(8,128)S(1)}, u32[]{:S(2)}, u32[]{:S(2)}) %collective-permute-start.5) | collective-permute-done | bytes 393248 | tf_op jit(solution)/shard_map/ppermute | solution.py:247
  107.2 8.0 %collective-permute-done.4.refs_5_ = f32[768,128]{1,0:T(8,128)S(1)} collective-permute-done((f32[768,128]{1,0:T(8,128)S(1)}, f32[768,128]{1,0:T(8,128)S(1)}, u32[]{:S(2)}, u32[]{:S(2)}) %collective-permute-start.4) | collective-permute-done | bytes 393248 | tf_op jit(solution)/shard_map/ppermute | solution.py:247
  115.2 1.2 copy-done
  116.4 1.1 copy-done.4
  117.6 1.0 copy-done.7
  118.6 1.0 copy-done.9
  121.5 5.4 %own_factor.1 = (bf16[1536,1024]{1,0:T(8,128)(2,1)S(1)}, f32[1536,128]{1,0:T(8,128)}) custom-call(s32[5]{0:T(128)S(1)} %pad_add_fusion.1.place_ref, f32[512,512]{1,0:T(8,128)S(1)} %copy-done, f32[1536,128]{1,0:T(8,128)S(1)} %copy-done.4, f32[768,128]{1,0:T(8,128)S(1)} %copy-done.9, f32[768,128]{1,0:T(8,128)S(1)} %copy-done.7, f32[768,128]{1,0:T(8,128)S(1)} %copy-done.13, ...), custom_call_target="tpu_custom_call" | custom-call | flops 2415919104 | bytes 7864320 | tf_op jit(solution)/shard_map/own_factor/pallas_call | solution.py:65
  127.0 1.2 copy-done.1
  128.2 1.9 %copy-done.5 = f32[32,1,192,128]{3,2,1,0:T(8,128)S(1)} copy-done((f32[32,1,192,128]{3,2,1,0:T(8,128)S(1)}, f32[32,1,192,128]{3,2,1,0:T(8,128)}, u32[]{:S(2)}) %copy-start.5) | copy-done | bytes 3145752
  130.1 15.4 %front.2.refs_0_ = f32[1536,3072]{1,0:T(8,128)} custom-call(s32[3,16]{1,0:T(4,128)S(1)} %multiply_reduce_fusion.entry_ref, s32[13]{0:T(128)S(1)} %convert_reduce_fusion.1.start_ref, f32[512,512]{1,0:T(8,128)S(1)} %copy-done.1, f32[24,8,128]{2,1,0:T(8,128)S(1)} %bitcast.29, f32[8,4,192,128]{3,2,1,0:T(8,128)S(1)} %bitcast.28, ...), custom_call_target="tpu_custom_call" | custom-call | flops 9663676416 | bytes 22020096 | tf_op jit(solution)/shard_map/front/pallas_call | solution.py:153
  145.5 1.2 copy-done.2
  146.7 1.9 %copy-done.3 = f32[32,1,192,128]{3,2,1,0:T(8,128)S(1)} copy-done((f32[32,1,192,128]{3,2,1,0:T(8,128)S(1)}, f32[32,1,192,128]{3,2,1,0:T(8,128)}, u32[]{:S(2)}) %copy-start.3) | copy-done | bytes 3145752
  148.6 15.4 %front.3 = f32[1536,3072]{1,0:T(8,128)} custom-call(s32[3,16]{1,0:T(4,128)S(1)} %multiply_reduce_fusion.entry_ref, s32[13]{0:T(128)S(1)} %convert_reduce_fusion.1.start_ref, f32[512,512]{1,0:T(8,128)S(1)} %copy-done.2, f32[24,8,128]{2,1,0:T(8,128)S(1)} %bitcast.30, f32[8,4,192,128]{3,2,1,0:T(8,128)S(1)} %bitcast.26, ...), custom_call_target="tpu_custom_call", output_to_operand_aliasing={{}: (7, {})} | custom-call | flops 9663676416 | bytes 22020096 | tf_op jit(solution)/shard_map/front/pallas_call | solution.py:153
  (67 shorter events, 13.1 us)
Async XLA Ops:
  7.2 119.8 %all-gather.7.cloned.1.call-start = ((), (), s32[]{:S(2)}) async-start(), calls=%async_computation.4 | async-start | bytes 3538944 | tf_op jit(solution)/shard_map/all_gather | solution.py:242
  50.1 95.4 %all-gather.5.cloned.1.call-start = ((), (), s32[]{:S(2)}) async-start(), calls=%async_computation.3 | async-start | bytes 3538944 | tf_op jit(solution)/shard_map/all_gather | solution.py:242
  56.1 8.5 %all-to-all-start = ((f32[8,3,8,128]{3,2,1,0:T(8,128)}), f32[8,3,8,128]{3,2,1,0:T(8,128)S(1)}, u32[]{:S(2)}, u32[]{:S(2)}) async-start(f32[8,3,8,128]{3,2,1,0:T(8,128)} %select_maximum_fusion), calls=%async_computation | async-start | bytes 196608 | tf_op jit(solution)/shard_map/all_to_all | solution.py:190
  60.7 12.9 %collective-permute-start.1 = (f32[768,128]{1,0:T(8,128)S(1)}, f32[768,128]{1,0:T(8,128)S(1)}, u32[]{:S(2)}, u32[]{:S(2)}) collective-permute-start(f32[768,128]{1,0:T(8,128)S(1)} %get-tuple-element.10), channel_id=1, source_target_pairs={{0,1},{1,3},{3,2},{2,0},{4,5},{5,7},{7,6},{6,4},{8,9},{9,11},{11,1... | collective-permute-start | bytes 1179656 | tf_op jit(solution)/shard_map/ppermute | solution.py:247
  60.9 21.0 %collective-permute-start = (f32[768,128]{1,0:T(8,128)S(1)}, f32[768,128]{1,0:T(8,128)S(1)}, u32[]{:S(2)}, u32[]{:S(2)}) collective-permute-start(f32[768,128]{1,0:T(8,128)S(1)} %get-tuple-element.11), channel_id=1, source_target_pairs={{0,1},{1,3},{3,2},{2,0},{4,5},{5,7},{7,6},{6,4},{8,9},{9,11},{11,1... | collective-permute-start | bytes 1179656 | tf_op jit(solution)/shard_map/ppermute | solution.py:247
  73.5 16.9 %collective-permute-start.3 = (f32[768,128]{1,0:T(8,128)S(1)}, f32[768,128]{1,0:T(8,128)S(1)}, u32[]{:S(2)}, u32[]{:S(2)}) collective-permute-start(f32[768,128]{1,0:T(8,128)S(1)} %collective-permute-done.1.refs_2_), channel_id=1, source_target_pairs={{0,1},{1,3},{3,2},{2,0},{4,5},{5,7},{7,6},{6,4},{8,9},{9,11},{11,1... | collective-permute-start | bytes 1179656 | tf_op jit(solution)/shard_map/ppermute | solution.py:247
  73.5 0.8 copy-start.6
  82.0 16.9 %collective-permute-start.2 = (f32[768,128]{1,0:T(8,128)S(1)}, f32[768,128]{1,0:T(8,128)S(1)}, u32[]{:S(2)}, u32[]{:S(2)}) collective-permute-start(f32[768,128]{1,0:T(8,128)S(1)} %collective-permute-done.refs_1_), channel_id=1, source_target_pairs={{0,1},{1,3},{3,2},{2,0},{4,5},{5,7},{7,6},{6,4},{8,9},{9,11},{11,1... | collective-permute-start | bytes 1179656 | tf_op jit(solution)/shard_map/ppermute | solution.py:247
  82.0 0.7 copy-start.8
  90.4 16.9 %collective-permute-start.5 = (f32[768,128]{1,0:T(8,128)S(1)}, f32[768,128]{1,0:T(8,128)S(1)}, u32[]{:S(2)}, u32[]{:S(2)}) collective-permute-start(f32[768,128]{1,0:T(8,128)S(1)} %collective-permute-done.3.refs_4_), channel_id=1, source_target_pairs={{0,1},{1,3},{3,2},{2,0},{4,5},{5,7},{7,6},{6,4},{8,9},{9,11},{11,1... | collective-permute-start | bytes 1179656 | tf_op jit(solution)/shard_map/ppermute | solution.py:247
  90.4 0.8 copy-start.10
  98.8 16.4 %collective-permute-start.4 = (f32[768,128]{1,0:T(8,128)S(1)}, f32[768,128]{1,0:T(8,128)S(1)}, u32[]{:S(2)}, u32[]{:S(2)}) collective-permute-start(f32[768,128]{1,0:T(8,128)S(1)} %collective-permute-done.2.refs_3_), channel_id=1, source_target_pairs={{0,1},{1,3},{3,2},{2,0},{4,5},{5,7},{7,6},{6,4},{8,9},{9,11},{11,1... | collective-permute-start | bytes 1179656 | tf_op jit(solution)/shard_map/ppermute | solution.py:247
  98.8 0.7 copy-start.12
  115.2 1.2 copy-start
  116.4 1.1 copy-start.4
  117.6 1.0 copy-start.7
  118.6 1.0 copy-start.9
  119.6 1.0 copy-start.11
  120.6 1.0 copy-start.13
  126.9 1.2 copy-start.1
  128.2 1.9 %copy-start.5 = (f32[32,1,192,128]{3,2,1,0:T(8,128)S(1)}, f32[32,1,192,128]{3,2,1,0:T(8,128)}, u32[]{:S(2)}) copy-start(f32[32,1,192,128]{3,2,1,0:T(8,128)} %all-gather.7.cloned.1.call-done) | copy-start | bytes 9437188
  145.5 1.2 copy-start.2
  146.7 1.9 %copy-start.3 = (f32[32,1,192,128]{3,2,1,0:T(8,128)S(1)}, f32[32,1,192,128]{3,2,1,0:T(8,128)}, u32[]{:S(2)}) copy-start(f32[32,1,192,128]{3,2,1,0:T(8,128)} %all-gather.5.cloned.1.call-done) | copy-start | bytes 9437188
Sparse Core Ops, SparseCore 0:
  50.2 31.3 all-gather.6
  83.5 32.3 all-gather.4

commit v3 on v2

--- a/solution.py
+++ b/solution.py
@@ -10,10 +10,10 @@
 TILE_ROWS = 8
 TILE_COLS = 128
 CAP = 2
+VMEM_LIMIT = 58 << 20
 NEXT = {0: 1, 1: 3, 3: 2, 2: 0}
 PREV = {v: k for k, v in NEXT.items()}
 NN = (((1,), (0,)), ((), ()))
-NT = (((1,), (1,)), ((), ()))
 
 
 def split(x):
@@ -77,7 +77,7 @@
             pltpu.VMEM((rows_step, width), jnp.float32),
             pltpu.SemaphoreType.DMA((len(pieces),)),
         ],
-        compiler_params=pltpu.CompilerParams(vmem_limit_bytes=40 << 20),
+        compiler_params=pltpu.CompilerParams(vmem_limit_bytes=VMEM_LIMIT),
         cost_estimate=pl.CostEstimate(
             flops=6 * rows * width * width, bytes_accessed=10 * rows * width, transcendentals=0
         ),
@@ -86,28 +86,41 @@
 
 
 def front_kernel(
-    first, entry_ref, start_ref, d_ref, agg_ref, pair_ref, own_ref, trail_ref, *refs
+    plan, place_ref, entry_ref, start_ref, d_ref, agg_ref, own_ref, trail_ref, *refs
 ):
-    out_ref, dcat, pair_cat = refs[-3:]
+    pieces = refs[: len(plan)]
+    out_ref, stage, dcat, pair_cat, sem = refs[len(plan) :]
     j, i = pl.program_id(0), pl.program_id(1)
     n_i = pl.num_programs(1)
     bm, bn = out_ref.shape
     width = d_ref.shape[0]
-    part = width // 4
 
     @pl.when((i == 0) & (j == 0))
     def _():
+        todo = []
+        for n, (where, half) in enumerate(plan):
+            _, depth, cols = pieces[n].shape
+            at = pl.ds(pl.multiple_of(place_ref[where] * depth, 8), depth)
+            todo.append(
+                pltpu.make_async_copy(
+                    pieces[n], stage.at[:, at, pl.ds(half * cols, cols)], sem.at[n]
+                )
+            )
+        for c in todo:
+            c.start()
         hi, lo = split(d_ref[...])
         dcat[:, 0:width] = hi
         dcat[:, width : 2 * width] = hi
         dcat[:, 2 * width :] = lo
+        for c in todo:
+            c.wait()
 
     @pl.when(i == 0)
     def _():
-        panel = jnp.concatenate([pair_ref[:, s].reshape(bn, part) for s in range(4)], axis=1)
-        hi, lo = split(panel)
-        rhs = jnp.concatenate([hi, lo, hi], axis=1)
-        turned = lax.dot_general(dcat[...], rhs, NT, preferred_element_type=jnp.float32)
+        cols = pl.ds(pl.multiple_of(j * bn, bn), bn)
+        hi, lo = split(stage[:, :, cols].reshape(width, bn))
+        rhs = jnp.concatenate([hi, lo, hi], axis=0)
+        turned = lax.dot_general(dcat[...], rhs, NN, preferred_element_type=jnp.float32)
         hi, lo = split(turned)
         pair_cat[0:width, :] = hi
         pair_cat[width : 2 * width, :] = lo
@@ -118,7 +131,7 @@
     lhs = jnp.concatenate([hi, hi, lo], axis=1)
     product = lax.dot_general(lhs, pair_cat[...], NN, preferred_element_type=jnp.float32)
     out_ref[...] = trail_ref[...] - product
-    step = (first + j) * n_i + i
+    step = j * n_i + i
 
     def add(e, carry):
         r = pl.multiple_of(entry_ref[1, e], TILE_ROWS)
@@ -130,45 +143,33 @@
     lax.fori_loop(start_ref[step], start_ref[step + 1], add, 0)
 
 
-def front(entries, starts, d, agg, pair, own, trailing, before, first, n_j, bm, bn):
+def front(place, entries, starts, d, agg, own, trailing, pieces, plan, bm, bn):
     rows, cols = trailing.shape
     width = d.shape[0]
-    part = width // 4
-    piece = pair.shape[2]
-    if piece < bn:
-        pair_block = pl.BlockSpec((bn // piece, 4, piece, part), lambda j, i: (j, 0, 0, 0))
-    else:
-        pair_block = pl.BlockSpec((1, 4, bn, part), lambda j, i: (0, 0, j, 0))
     whole = pl.BlockSpec(memory_space=pltpu.VMEM)
     smem = pl.BlockSpec(memory_space=pltpu.SMEM)
-    block = pl.BlockSpec((bm, bn), lambda j, i: (i, first + j))
-    operands = [entries, starts, d, agg, pair, own, trailing]
-    specs = [smem, smem, whole, whole, pair_block, whole, block]
-    aliases = {}
-    if before is not None:
-        aliases = {len(operands): 0}
-        operands.append(before)
-        specs.append(pl.BlockSpec(memory_space=pl.ANY))
-    done = n_j * bn
+    block = pl.BlockSpec((bm, bn), lambda j, i: (i, j))
     return pl.pallas_call(
-        functools.partial(front_kernel, first),
-        grid=(n_j, rows // bm),
+        functools.partial(front_kernel, plan),
+        grid=(cols // bn, rows // bm),
         out_shape=jax.ShapeDtypeStruct((rows, cols), jnp.float32),
-        in_specs=specs,
+        in_specs=[smem, smem, smem, whole, whole, whole, block]
+        + [pl.BlockSpec(memory_space=pl.ANY)] * len(pieces),
         out_specs=block,
         scratch_shapes=[
+            pltpu.VMEM((4, width // 4, cols), jnp.float32),
             pltpu.VMEM((width, 3 * width), jnp.bfloat16),
             pltpu.VMEM((3 * width, bn), jnp.bfloat16),
+            pltpu.SemaphoreType.DMA((len(pieces),)),
         ],
-        input_output_aliases=aliases,
-        compiler_params=pltpu.CompilerParams(vmem_limit_bytes=44 << 20),
+        compiler_params=pltpu.CompilerParams(vmem_limit_bytes=VMEM_LIMIT),
         cost_estimate=pl.CostEstimate(
-            flops=6 * (rows + width) * width * done,
-            bytes_accessed=8 * rows * done + 4 * width * done,
+            flops=6 * (rows + width) * width * cols,
+            bytes_accessed=8 * rows * cols + 4 * width * cols,
             transcendentals=0,
         ),
         name="front",
-    )(*operands)
+    )(place, entries, starts, d, agg, own, trailing, *pieces)
 
 
 def exchange_tiles(agg_vals, agg_dest, agg_tile, tiles_dev):
@@ -223,34 +224,52 @@
     bn = 768
     n_i, n_j = local_rows // bm, local_cols // bn
 
-    if row_devices == 2 * col_devices and local_rows % (16 * row_devices) == 0:
-        eighth = local_rows // row_devices
+    if row_devices == 8 and col_devices == 4:
+        row_index = lax.axis_index("row")
+        chip, core = row_index // 2, row_index % 2
+        half = local_rows // 2
+        ring = list(NEXT.items())
+        parts = [(panel[:half], panel[half:])]
+        parts.append(tuple(lax.ppermute(x, "col", ring) for x in parts[-1]))
+        depth = part // row_devices
         spread = lax.all_to_all(
-            panel.reshape(row_devices, eighth, part),
+            panel.T.reshape(row_devices, depth, local_rows),
             "row",
             split_axis=0,
             concat_axis=0,
             tiled=True,
         )
+        spread, parts[1] = lax.optimization_barrier((spread, parts[1]))
         wanted = lax.all_to_all(
-            spread.reshape(col_devices, 2, eighth, part),
+            spread.reshape(col_devices, 2, depth, local_rows),
             "col",
             split_axis=0,
             concat_axis=0,
             tiled=True,
         )
-        pairs = [lax.all_gather(wanted[:, k], "row", axis=0) for k in range(2)]
-        half = local_rows // 2
-        ring = list(NEXT.items())
-        parts = [(panel[:half], panel[half:])]
+        wanted, parts[1], agg_vals, agg_dest, agg_tile = lax.optimization_barrier(
+            (wanted, parts[1], agg_vals, agg_dest, agg_tile)
+        )
+        for _ in range(2):
+            parts.append(tuple(lax.ppermute(x, "col", ring) for x in parts[-1]))
+        siblings = [(p, p ^ 1) for p in range(row_devices)]
+        following = jnp.array([NEXT[c] for c in range(4)], jnp.int32)
+        previous = jnp.array([PREV[c] for c in range(4)], jnp.int32)
+        places, pieces, plan = [], [], []
+        for k, (step, back) in enumerate(((NEXT, previous), (PREV, following))):
+            turn = [(2 * c + m, 2 * step[c] + m) for c in range(4) for m in range(2)]
+            piece, source = wanted[:, k], chip
+            for n in range(4):
+                if n > 0:
+                    piece, source = lax.ppermute(piece, "row", turn), back[source]
+                plan += [(5 + len(places), k), (6 + len(places), k)]
+                places += [2 * source + core, 2 * source + 1 - core]
+                pieces += [piece, lax.ppermute(piece, "row", siblings)]
+        sources = [jnp.arange(4, dtype=jnp.int32)]
         for _ in range(3):
-            parts.append(tuple(lax.ppermute(x, "col", ring) for x in parts[-1]))
-        sources = [jnp.arange(4, dtype=jnp.int32)]
-        back = jnp.array([PREV[q] for q in range(4)], jnp.int32)
-        for _ in range(3):
-            sources.append(back[sources[-1]])
+            sources.append(previous[sources[-1]])
         order = jnp.stack(sources)[:, col_index]
-        own = [panel] + [x for pieces in parts[1:] for x in pieces]
+        own = [panel] + [x for halves in parts[1:] for x in halves]
         own_plan = [(0, 0, local_rows)]
         own_plan += [(s, r * half, half) for s in range(1, 4) for r in range(2)]
     else:
@@ -258,7 +277,7 @@
         column = lax.all_gather(panel, "row", axis=0, tiled=True)
         column = column.reshape(col_devices, local_cols, part)
         partner = lax.all_to_all(column, "col", split_axis=0, concat_axis=0, tiled=True)
-        pairs = [partner[None]]
+        places, pieces, plan = [jnp.int32(0)], [jnp.swapaxes(partner, 1, 2)], [(5, 0)]
         own = [whole[s] for s in range(col_devices)]
         own_plan = [(s, 0, local_rows) for s in range(col_devices)]
         order = jnp.arange(4, dtype=jnp.int32)
@@ -267,25 +286,11 @@
     entries, starts = order_tiles(
         landing, row_devices * CAP, tiles_dev, tile_cols, bm, bn, n_i, n_j
     )
-    place = jnp.concatenate([order, col_index.reshape(1)]).astype(jnp.int32)
+    place = jnp.concatenate([order, jnp.stack([col_index] + places)]).astype(jnp.int32)
     halves, own_block = own_factor(place, diag_inverse, own, own_plan, local_rows, bm)
-    updated = None
-    calls = len(pairs)
-    for h, pair in enumerate(pairs):
-        updated = front(
-            entries,
-            starts,
-            diag_inverse,
-            agg,
-            pair,
-            halves,
-            trailing,
-            updated,
-            h * (n_j // calls),
-            n_j // calls,
-            bm,
-            bn,
-        )
+    updated = front(
+        place, entries, starts, diag_inverse, agg, halves, trailing, pieces, plan, bm, bn
+    )
     return updated, own_block
 
 

time: 172 us -> 156 us (0.907)
  blocking collectives: 41.9 us -> 0 us
  starting transfers between devices: 5.48 us -> 33.1 us
  local copies, waits for them, and re-layouts: 21 us -> 15.2 us
  Pallas kernels: 36.1 us -> 40.4 us
  between operations: 14.1 us -> 11.9 us
    all_to_all x2 -> x0, blocking collectives: 41.9 us -> none  [the longest x1 24.2 us: per_device(): lax.all_to_all(spread.reshape(col_devices, 2, eighth, part), 'col', split...]
    unnamed x29 -> x34, local copies, waits for them, and re-layouts: 15.6 us -> 2.43 us
    all_to_all x0 -> x2, starting transfers between devices: none -> 10.1 us  [the longest x1 5.17 us: per_device(): lax.all_to_all(panel.T.reshape(row_devices, depth, local_rows), 'row', sp...]
    ppermute x6, starting transfers between devices: 2.04 us -> 11.4 us  [per_device(): parts.append(tuple((lax.ppermute(x, 'col', ring) for x in parts[-1])))]
    ppermute x0 -> x14, starting transfers between devices: none -> 7.72 us  [the longest x6 6.37 us: per_device(): piece, source = (lax.ppermute(piece, 'row', turn), back[source])]
    dynamic_slice x0 -> x6, local copies, waits for them, and re-layouts: none -> 7.61 us  [per_device(): piece, source = (lax.ppermute(piece, 'row', turn), back[source])]
    pallas_call x1, Pallas kernels: 5.35 us -> 8.1 us  [own_factor(): pl.pallas_call(functools.partial(own_kernel, plan, rows_step), out_shape=...]
    ppermute x6, waiting for transfers between devices: 46 us -> 48.4 us  [per_device(): parts.append(tuple((lax.ppermute(x, 'col', ring) for x in parts[-1])))]
  transfers between devices with their start and end apart: 9 -> 23, of which waited for: 7 -> 7; matrix products, arithmetic and copies ran while one was open for 5% -> 8% of each run, Pallas kernels for 12% -> 5%
where the time goes in v3:
time: 156 us; the launch traced here: 155 us
  waiting for transfers between devices  49 us (31%)
  Pallas kernels  40.4 us (26%)
  starting transfers between devices  33.1 us (21%)
  local copies, waits for them, and re-layouts  15.2 us (10%)
  between operations  11.9 us (8%)
  other arithmetic  5.35 us (3%)
    ppermute x6, waiting for transfers between devices, per_device(): parts.append(tuple((lax.ppermute(x, 'col', ring) for x in parts[-1])))  48.4 us
    pallas_call x1, Pallas kernels, front(): pl.pallas_call(functools.partial(front_kernel, plan), grid=(cols // bn, r...  32.3 us
    ppermute x6, starting transfers between devices, per_device(): parts.append(tuple((lax.ppermute(x, 'col', ring) for x in parts[-1])))  11.4 us
    pallas_call x1, Pallas kernels, own_factor(): pl.pallas_call(functools.partial(own_kernel, plan, rows_step), out_shape=...  8.1 us
    dynamic_slice x6, local copies, waits for them, and re-layouts, per_device(): piece, source = (lax.ppermute(piece, 'row', turn), back[source])  7.61 us
    ppermute x6, starting transfers between devices, per_device(): piece, source = (lax.ppermute(piece, 'row', turn), back[source])  6.37 us
    all_to_all x1, starting transfers between devices, per_device(): lax.all_to_all(panel.T.reshape(row_devices, depth, local_rows), 'row', sp...  5.17 us
    all_to_all x1, starting transfers between devices, per_device(): lax.all_to_all(spread.reshape(col_devices, 2, depth, local_rows), 'col',...  4.92 us
  transfers between devices with their start and end apart: 23, of which 7 were waited for; matrix products, arithmetic and copies ran while one was open for 8% of the time, Pallas kernels for 5%

profile of v3, /device:TPU:0, one launch (start us, length us, event | category | flops | bytes accessed | tf_op | source)
XLA Modules:
  0.0 155.0 jit_solution(5457137360240222664)
XLA Ops:
  0.6 2.3 %copy.67 = f32[1536,128]{0,1:T(8,128)} copy(f32[1536,128]{1,0:T(8,128)} %refs_0_.1) | data formatting | bytes 1572864 | tf_op args[1]
  2.9 5.2 %all-to-all-start = ((f32[8,16,1536]{2,1,0:T(8,128)}), f32[8,16,1536]{2,1,0:T(8,128)}, u32[]{:S(2)}, u32[]{:S(2)}) async-start(f32[8,16,1536]{2,1,0:T(8,128)} %bitcast.23), calls=%async_computation | async-start | bytes 1572864 | tf_op jit(solution)/shard_map/all_to_all | solution.py:235
  9.3 2.1 %collective-permute-start.1 = (f32[768,128]{1,0:T(8,128)S(1)}, f32[768,128]{1,0:T(8,128)S(1)}, u32[]{:S(2)}, u32[]{:S(2)}) collective-permute-start(f32[768,128]{1,0:T(8,128)S(1)} %get-tuple-element.28), channel_id=1, source_target_pairs={{0,1},{1,3},{3,2},{2,0},{4,5},{5,7},{7,6},{6,4},{8,9},{9,11},{11,1... | collective-permute-start | bytes 1179656 | tf_op jit(solution)/shard_map/ppermute | solution.py:233
  11.4 2.6 %collective-permute-start = (f32[768,128]{1,0:T(8,128)S(1)}, f32[768,128]{1,0:T(8,128)S(1)}, u32[]{:S(2)}, u32[]{:S(2)}) collective-permute-start(f32[768,128]{1,0:T(8,128)S(1)} %get-tuple-element.29), channel_id=1, source_target_pairs={{0,1},{1,3},{3,2},{2,0},{4,5},{5,7},{7,6},{6,4},{8,9},{9,11},{11,1... | collective-permute-start | bytes 1179656 | tf_op jit(solution)/shard_map/ppermute | solution.py:233
  14.0 8.4 %collective-permute-done.1.refs_2_ = f32[768,128]{1,0:T(8,128)S(1)} collective-permute-done((f32[768,128]{1,0:T(8,128)S(1)}, f32[768,128]{1,0:T(8,128)S(1)}, u32[]{:S(2)}, u32[]{:S(2)}) %collective-permute-start.1) | collective-permute-done | bytes 393248 | tf_op jit(solution)/shard_map/ppermute | solution.py:233
  22.4 8.1 %collective-permute-done.refs_1_ = f32[768,128]{1,0:T(8,128)S(1)} collective-permute-done((f32[768,128]{1,0:T(8,128)S(1)}, f32[768,128]{1,0:T(8,128)S(1)}, u32[]{:S(2)}, u32[]{:S(2)}) %collective-permute-start) | collective-permute-done | bytes 393248 | tf_op jit(solution)/shard_map/ppermute | solution.py:233
  30.5 4.9 %all-to-all-start.1 = ((f32[4,2,16,1536]{3,2,1,0:T(8,128)}), f32[4,2,16,1536]{3,2,1,0:T(8,128)S(1)}, u32[]{:S(2)}, u32[]{:S(2)}) async-start(f32[4,2,16,1536]{3,2,1,0:T(8,128)} %bitcast.24), calls=%async_computation.1 | async-start | bytes 1572864 | tf_op jit(solution)/shard_map/all_to_all | solution.py:243
  35.4 1.3 dynamic_slice.22
  41.6 1.3 dynamic_slice.24
  44.7 1.3 dynamic_slice.25
  50.9 1.3 dynamic_slice.27
  58.6 1.5 scatter_fusion
  60.7 3.9 %all-to-all-start.2 = ((f32[8,3,8,128]{3,2,1,0:T(8,128)}), f32[8,3,8,128]{3,2,1,0:T(8,128)S(1)}, u32[]{:S(2)}, u32[]{:S(2)}) async-start(f32[8,3,8,128]{3,2,1,0:T(8,128)} %select_maximum_fusion), calls=%async_computation.2 | async-start | bytes 196608 | tf_op jit(solution)/shard_map/all_to_all | solution.py:191
  64.7 2.1 %collective-permute-start.14 = (f32[4,16,1536]{2,1,0:T(8,128)S(1)}, f32[4,16,1536]{2,1,0:T(8,128)S(1)}, u32[]{:S(2)}, u32[]{:S(2)}) collective-permute-start(f32[4,16,1536]{2,1,0:T(8,128)S(1)} %get-tuple-element.26.refs_8_), channel_id=1, source_target_pairs={{0,16},{4,20},{8,0},{12,4},{16,24},{20,28},{24,8},{28,12},{1,17},{... | collective-permute-start | bytes 1179656 | tf_op jit(solution)/shard_map/ppermute | solution.py:264
  67.3 2.0 %collective-permute-start.2 = (f32[768,128]{1,0:T(8,128)S(1)}, f32[768,128]{1,0:T(8,128)}, u32[]{:S(2)}, u32[]{:S(2)}) collective-permute-start(f32[768,128]{1,0:T(8,128)S(1)} %collective-permute-done.refs_1_), channel_id=1, source_target_pairs={{0,1},{1,3},{3,2},{2,0},{4,5},{5,7},{7,6},{6,4},{8,9},{9,11},{11,1... | collective-permute-start | bytes 1179656 | tf_op jit(solution)/shard_map/ppermute | solution.py:254
  70.9 8.9 %collective-permute-done.2.refs_3_ = f32[768,128]{1,0:T(8,128)} collective-permute-done((f32[768,128]{1,0:T(8,128)S(1)}, f32[768,128]{1,0:T(8,128)}, u32[]{:S(2)}, u32[]{:S(2)}) %collective-permute-start.2) | collective-permute-done | bytes 393248 | tf_op jit(solution)/shard_map/ppermute | solution.py:254
  80.7 1.8 %collective-permute-start.16 = (f32[4,16,1536]{2,1,0:T(8,128)S(1)}, f32[4,16,1536]{2,1,0:T(8,128)S(1)}, u32[]{:S(2)}, u32[]{:S(2)}) collective-permute-start(f32[4,16,1536]{2,1,0:T(8,128)S(1)} %collective-permute-done.14.refs_10_), channel_id=1, source_target_pairs={{0,16},{4,20},{8,0},{12,4},{16,24},{20,28},{24,8},{28,12},{1,17},{... | collective-permute-start | bytes 1179656 | tf_op jit(solution)/shard_map/ppermute | solution.py:264
  82.7 8.7 %collective-permute-done.3.refs_4_ = f32[768,128]{1,0:T(8,128)S(1)} collective-permute-done((f32[768,128]{1,0:T(8,128)S(1)}, f32[768,128]{1,0:T(8,128)S(1)}, u32[]{:S(2)}, u32[]{:S(2)}) %collective-permute-start.3) | collective-permute-done | bytes 393248 | tf_op jit(solution)/shard_map/ppermute | solution.py:254
  92.0 3.4 %collective-permute-start.5 = (f32[768,128]{1,0:T(8,128)S(1)}, f32[768,128]{1,0:T(8,128)S(1)}, u32[]{:S(2)}, u32[]{:S(2)}) collective-permute-start(f32[768,128]{1,0:T(8,128)S(1)} %collective-permute-done.3.refs_4_), channel_id=1, source_target_pairs={{0,1},{1,3},{3,2},{2,0},{4,5},{5,7},{7,6},{6,4},{8,9},{9,11},{11,1... | collective-permute-start | bytes 1179656 | tf_op jit(solution)/shard_map/ppermute | solution.py:254
  95.3 1.8 %collective-permute-start.18 = (f32[4,16,1536]{2,1,0:T(8,128)S(1)}, f32[4,16,1536]{2,1,0:T(8,128)S(1)}, u32[]{:S(2)}, u32[]{:S(2)}) collective-permute-start(f32[4,16,1536]{2,1,0:T(8,128)S(1)} %collective-permute-done.16.refs_12_), channel_id=1, source_target_pairs={{0,16},{4,20},{8,0},{12,4},{16,24},{20,28},{24,8},{28,12},{1,17},{... | collective-permute-start | bytes 1179656 | tf_op jit(solution)/shard_map/ppermute | solution.py:264
  98.3 6.3 %collective-permute-done.4.refs_5_ = f32[768,128]{1,0:T(8,128)S(1)} collective-permute-done((f32[768,128]{1,0:T(8,128)}, f32[768,128]{1,0:T(8,128)S(1)}, u32[]{:S(2)}, u32[]{:S(2)}) %collective-permute-start.4) | collective-permute-done | bytes 393248 | tf_op jit(solution)/shard_map/ppermute | solution.py:254
  104.6 8.0 %collective-permute-done.5.refs_6_ = f32[768,128]{1,0:T(8,128)S(1)} collective-permute-done((f32[768,128]{1,0:T(8,128)S(1)}, f32[768,128]{1,0:T(8,128)S(1)}, u32[]{:S(2)}, u32[]{:S(2)}) %collective-permute-start.5) | collective-permute-done | bytes 393248 | tf_op jit(solution)/shard_map/ppermute | solution.py:254
  114.4 8.1 %own_factor.1 = (bf16[1536,1024]{1,0:T(8,128)(2,1)}, f32[1536,128]{1,0:T(8,128)}) custom-call(s32[21]{0:T(128)} %concatenate.6.place_ref, f32[512,512]{1,0:T(8,128)} %d_ref.3, f32[1536,128]{1,0:T(8,128)} %refs_0_.1, f32[768,128]{1,0:T(8,128)} %copy-done.4, f32[768,128]{1,0:T(8,128)} %copy-done.3, f32[768,128]{1,0:T(8,128)} %collective-permute-done.2.refs_3_, ...), custom_call_target="tpu_custom_call" | custom-call | flops 2415919104 | bytes 7864320 | tf_op jit(solution)/shard_map/own_factor/pallas_call | solution.py:65
  122.7 32.3 %front.1 = f32[1536,3072]{1,0:T(8,128)} custom-call(s32[21]{0:T(128)} %concatenate.6.place_ref, s32[3,16]{1,0:T(4,128)} %multiply_reduce_fusion.entry_ref, s32[13]{0:T(128)} %convert_reduce_fusion.1.start_ref, f32[512,512]{1,0:T(8,128)} %d_ref.3, f32[24,8,128]{2,1,0:T(8,128)} %bitcast.51, bf16[1536,1024]{1,0:T(8,128)(2,1)} %get-tuple-element.21.own_ref, ...), custom_call_target="tpu_custom_call" | custom-call | flops 19327352832 | bytes 44040192 | tf_op jit(solution)/shard_map/front/pallas_call | solution.py:152
  (101 shorter events, 15.5 us)
Async XLA Ops:
  2.9 27.6 %all-to-all-start = ((f32[8,16,1536]{2,1,0:T(8,128)}), f32[8,16,1536]{2,1,0:T(8,128)}, u32[]{:S(2)}, u32[]{:S(2)}) async-start(f32[8,16,1536]{2,1,0:T(8,128)} %bitcast.23), calls=%async_computation | async-start | bytes 1572864 | tf_op jit(solution)/shard_map/all_to_all | solution.py:235
  9.3 13.1 %collective-permute-start.1 = (f32[768,128]{1,0:T(8,128)S(1)}, f32[768,128]{1,0:T(8,128)S(1)}, u32[]{:S(2)}, u32[]{:S(2)}) collective-permute-start(f32[768,128]{1,0:T(8,128)S(1)} %get-tuple-element.28), channel_id=1, source_target_pairs={{0,1},{1,3},{3,2},{2,0},{4,5},{5,7},{7,6},{6,4},{8,9},{9,11},{11,1... | collective-permute-start | bytes 1179656 | tf_op jit(solution)/shard_map/ppermute | solution.py:233
  11.4 19.1 %collective-permute-start = (f32[768,128]{1,0:T(8,128)S(1)}, f32[768,128]{1,0:T(8,128)S(1)}, u32[]{:S(2)}, u32[]{:S(2)}) collective-permute-start(f32[768,128]{1,0:T(8,128)S(1)} %get-tuple-element.29), channel_id=1, source_target_pairs={{0,1},{1,3},{3,2},{2,0},{4,5},{5,7},{7,6},{6,4},{8,9},{9,11},{11,1... | collective-permute-start | bytes 1179656 | tf_op jit(solution)/shard_map/ppermute | solution.py:233
  22.4 92.0 %copy-start.3 = (f32[768,128]{1,0:T(8,128)}, f32[768,128]{1,0:T(8,128)S(1)}, u32[]{:S(2)}) copy-start(f32[768,128]{1,0:T(8,128)S(1)} %collective-permute-done.1.refs_2_) | copy-start | bytes 1179652
  30.5 25.0 %all-to-all-start.1 = ((f32[4,2,16,1536]{3,2,1,0:T(8,128)}), f32[4,2,16,1536]{3,2,1,0:T(8,128)S(1)}, u32[]{:S(2)}, u32[]{:S(2)}) async-start(f32[4,2,16,1536]{3,2,1,0:T(8,128)} %bitcast.24), calls=%async_computation.1 | async-start | bytes 1572864 | tf_op jit(solution)/shard_map/all_to_all | solution.py:243
  60.7 9.1 %all-to-all-start.2 = ((f32[8,3,8,128]{3,2,1,0:T(8,128)}), f32[8,3,8,128]{3,2,1,0:T(8,128)S(1)}, u32[]{:S(2)}, u32[]{:S(2)}) async-start(f32[8,3,8,128]{3,2,1,0:T(8,128)} %select_maximum_fusion), calls=%async_computation.2 | async-start | bytes 196608 | tf_op jit(solution)/shard_map/all_to_all | solution.py:191
  64.7 16.0 %collective-permute-start.14 = (f32[4,16,1536]{2,1,0:T(8,128)S(1)}, f32[4,16,1536]{2,1,0:T(8,128)S(1)}, u32[]{:S(2)}, u32[]{:S(2)}) collective-permute-start(f32[4,16,1536]{2,1,0:T(8,128)S(1)} %get-tuple-element.26.refs_8_), channel_id=1, source_target_pairs={{0,16},{4,20},{8,0},{12,4},{16,24},{20,28},{24,8},{28,12},{1,17},{... | collective-permute-start | bytes 1179656 | tf_op jit(solution)/shard_map/ppermute | solution.py:264
  66.8 24.7 %collective-permute-start.13 = (f32[4,16,1536]{2,1,0:T(8,128)S(1)}, f32[4,16,1536]{2,1,0:T(8,128)S(1)}, u32[]{:S(2)}, u32[]{:S(2)}) collective-permute-start(f32[4,16,1536]{2,1,0:T(8,128)S(1)} %get-tuple-element.26.refs_8_), channel_id=1, source_target_pairs={{0,4},{4,0},{8,12},{12,8},{16,20},{20,16},{24,28},{28,24},{1,5},{5... | collective-permute-start | bytes 1179656 | tf_op jit(solution)/shard_map/ppermute | solution.py:267
  66.8 15.7 %collective-permute-start.7 = (f32[4,16,1536]{2,1,0:T(8,128)S(1)}, f32[4,16,1536]{2,1,0:T(8,128)S(1)}, u32[]{:S(2)}, u32[]{:S(2)}) collective-permute-start(f32[4,16,1536]{2,1,0:T(8,128)S(1)} %get-tuple-element.27.refs_0_), channel_id=1, source_target_pairs={{0,8},{4,12},{8,24},{12,28},{16,0},{20,4},{24,16},{28,20},{1,9},{5... | collective-permute-start | bytes 1179656 | tf_op jit(solution)/shard_map/ppermute | solution.py:264
  67.0 24.9 %collective-permute-start.6 = (f32[4,16,1536]{2,1,0:T(8,128)S(1)}, f32[4,16,1536]{2,1,0:T(8,128)}, u32[]{:S(2)}, u32[]{:S(2)}) collective-permute-start(f32[4,16,1536]{2,1,0:T(8,128)S(1)} %get-tuple-element.27.refs_0_), channel_id=1, source_target_pairs={{0,4},{4,0},{8,12},{12,8},{16,20},{20,16},{24,28},{28,24},{1,5},{5... | collective-permute-start | bytes 1179656 | tf_op jit(solution)/shard_map/ppermute | solution.py:267
  67.3 12.5 %collective-permute-start.2 = (f32[768,128]{1,0:T(8,128)S(1)}, f32[768,128]{1,0:T(8,128)}, u32[]{:S(2)}, u32[]{:S(2)}) collective-permute-start(f32[768,128]{1,0:T(8,128)S(1)} %collective-permute-done.refs_1_), channel_id=1, source_target_pairs={{0,1},{1,3},{3,2},{2,0},{4,5},{5,7},{7,6},{6,4},{8,9},{9,11},{11,1... | collective-permute-start | bytes 1179656 | tf_op jit(solution)/shard_map/ppermute | solution.py:254
  79.8 11.7 %collective-permute-start.3 = (f32[768,128]{1,0:T(8,128)S(1)}, f32[768,128]{1,0:T(8,128)S(1)}, u32[]{:S(2)}, u32[]{:S(2)}) collective-permute-start(f32[768,128]{1,0:T(8,128)S(1)} %collective-permute-done.1.refs_2_), channel_id=1, source_target_pairs={{0,1},{1,3},{3,2},{2,0},{4,5},{5,7},{7,6},{6,4},{8,9},{9,11},{11,1... | collective-permute-start | bytes 1179656 | tf_op jit(solution)/shard_map/ppermute | solution.py:254
  80.7 14.7 %collective-permute-start.16 = (f32[4,16,1536]{2,1,0:T(8,128)S(1)}, f32[4,16,1536]{2,1,0:T(8,128)S(1)}, u32[]{:S(2)}, u32[]{:S(2)}) collective-permute-start(f32[4,16,1536]{2,1,0:T(8,128)S(1)} %collective-permute-done.14.refs_10_), channel_id=1, source_target_pairs={{0,16},{4,20},{8,0},{12,4},{16,24},{20,28},{24,8},{28,12},{1,17},{... | collective-permute-start | bytes 1179656 | tf_op jit(solution)/shard_map/ppermute | solution.py:264
  82.5 14.7 %collective-permute-start.9 = (f32[4,16,1536]{2,1,0:T(8,128)S(1)}, f32[4,16,1536]{2,1,0:T(8,128)S(1)}, u32[]{:S(2)}, u32[]{:S(2)}) collective-permute-start(f32[4,16,1536]{2,1,0:T(8,128)S(1)} %collective-permute-done.7.refs_2_), channel_id=1, source_target_pairs={{0,8},{4,12},{8,24},{12,28},{16,0},{20,4},{24,16},{28,20},{1,9},{5... | collective-permute-start | bytes 1179656 | tf_op jit(solution)/shard_map/ppermute | solution.py:264
  91.5 21.1 %collective-permute-start.15 = (f32[4,16,1536]{2,1,0:T(8,128)S(1)}, f32[4,16,1536]{2,1,0:T(8,128)S(1)}, u32[]{:S(2)}, u32[]{:S(2)}) collective-permute-start(f32[4,16,1536]{2,1,0:T(8,128)S(1)} %collective-permute-done.14.refs_10_), channel_id=1, source_target_pairs={{0,4},{4,0},{8,12},{12,8},{16,20},{20,16},{24,28},{28,24},{1,5},{5... | collective-permute-start | bytes 1179656 | tf_op jit(solution)/shard_map/ppermute | solution.py:267
  91.5 13.1 %collective-permute-start.4 = (f32[768,128]{1,0:T(8,128)}, f32[768,128]{1,0:T(8,128)S(1)}, u32[]{:S(2)}, u32[]{:S(2)}) collective-permute-start(f32[768,128]{1,0:T(8,128)} %collective-permute-done.2.refs_3_), channel_id=1, source_target_pairs={{0,1},{1,3},{3,2},{2,0},{4,5},{5,7},{7,6},{6,4},{8,9},{9,11},{11,1... | collective-permute-start | bytes 1179656 | tf_op jit(solution)/shard_map/ppermute | solution.py:254
  92.0 20.6 %collective-permute-start.5 = (f32[768,128]{1,0:T(8,128)S(1)}, f32[768,128]{1,0:T(8,128)S(1)}, u32[]{:S(2)}, u32[]{:S(2)}) collective-permute-start(f32[768,128]{1,0:T(8,128)S(1)} %collective-permute-done.3.refs_4_), channel_id=1, source_target_pairs={{0,1},{1,3},{3,2},{2,0},{4,5},{5,7},{7,6},{6,4},{8,9},{9,11},{11,1... | collective-permute-start | bytes 1179656 | tf_op jit(solution)/shard_map/ppermute | solution.py:254
  95.3 17.7 %collective-permute-start.18 = (f32[4,16,1536]{2,1,0:T(8,128)S(1)}, f32[4,16,1536]{2,1,0:T(8,128)S(1)}, u32[]{:S(2)}, u32[]{:S(2)}) collective-permute-start(f32[4,16,1536]{2,1,0:T(8,128)S(1)} %collective-permute-done.16.refs_12_), channel_id=1, source_target_pairs={{0,16},{4,20},{8,0},{12,4},{16,24},{20,28},{24,8},{28,12},{1,17},{... | collective-permute-start | bytes 1179656 | tf_op jit(solution)/shard_map/ppermute | solution.py:264
  97.2 16.0 %collective-permute-start.11 = (f32[4,16,1536]{2,1,0:T(8,128)S(1)}, f32[4,16,1536]{2,1,0:T(8,128)S(1)}, u32[]{:S(2)}, u32[]{:S(2)}) collective-permute-start(f32[4,16,1536]{2,1,0:T(8,128)S(1)} %collective-permute-done.9.refs_4_), channel_id=1, source_target_pairs={{0,8},{4,12},{8,24},{12,28},{16,0},{20,4},{24,16},{28,20},{1,9},{5... | collective-permute-start | bytes 1179656 | tf_op jit(solution)/shard_map/ppermute | solution.py:264
  104.6 17.9 %collective-permute-start.8 = (f32[4,16,1536]{2,1,0:T(8,128)S(1)}, f32[4,16,1536]{2,1,0:T(8,128)}, u32[]{:S(2)}, u32[]{:S(2)}) collective-permute-start(f32[4,16,1536]{2,1,0:T(8,128)S(1)} %collective-permute-done.7.refs_2_), channel_id=1, source_target_pairs={{0,4},{4,0},{8,12},{12,8},{16,20},{20,16},{24,28},{28,24},{1,5},{5... | collective-permute-start | bytes 1179656 | tf_op jit(solution)/shard_map/ppermute | solution.py:267
  112.6 10.0 %collective-permute-start.17 = (f32[4,16,1536]{2,1,0:T(8,128)S(1)}, f32[4,16,1536]{2,1,0:T(8,128)}, u32[]{:S(2)}, u32[]{:S(2)}) collective-permute-start(f32[4,16,1536]{2,1,0:T(8,128)S(1)} %collective-permute-done.16.refs_12_), channel_id=1, source_target_pairs={{0,4},{4,0},{8,12},{12,8},{16,20},{20,16},{24,28},{28,24},{1,5},{5... | collective-permute-start | bytes 1179656 | tf_op jit(solution)/shard_map/ppermute | solution.py:267
  112.6 10.0 %collective-permute-start.10 = (f32[4,16,1536]{2,1,0:T(8,128)S(1)}, f32[4,16,1536]{2,1,0:T(8,128)}, u32[]{:S(2)}, u32[]{:S(2)}) collective-permute-start(f32[4,16,1536]{2,1,0:T(8,128)S(1)} %collective-permute-done.9.refs_4_), channel_id=1, source_target_pairs={{0,4},{4,0},{8,12},{12,8},{16,20},{20,16},{24,28},{28,24},{1,5},{5... | collective-permute-start | bytes 1179656 | tf_op jit(solution)/shard_map/ppermute | solution.py:267
  113.1 9.5 %collective-permute-start.19 = (f32[4,16,1536]{2,1,0:T(8,128)S(1)}, f32[4,16,1536]{2,1,0:T(8,128)}, u32[]{:S(2)}, u32[]{:S(2)}) collective-permute-start(f32[4,16,1536]{2,1,0:T(8,128)S(1)} %collective-permute-done.18.refs_14_), channel_id=1, source_target_pairs={{0,4},{4,0},{8,12},{12,8},{16,20},{20,16},{24,28},{28,24},{1,5},{5... | collective-permute-start | bytes 1179656 | tf_op jit(solution)/shard_map/ppermute | solution.py:267
  113.2 9.4 %collective-permute-start.12 = (f32[4,16,1536]{2,1,0:T(8,128)S(1)}, f32[4,16,1536]{2,1,0:T(8,128)}, u32[]{:S(2)}, u32[]{:S(2)}) collective-permute-start(f32[4,16,1536]{2,1,0:T(8,128)S(1)} %collective-permute-done.11.refs_6_), channel_id=1, source_target_pairs={{0,4},{4,0},{8,12},{12,8},{16,20},{20,16},{24,28},{28,24},{1,5},{5... | collective-permute-start | bytes 1179656 | tf_op jit(solution)/shard_map/ppermute | solution.py:267
  (15 other events, 480.3 us)

commit v4 on v3

--- a/solution.py
+++ b/solution.py
@@ -14,6 +14,7 @@
 NEXT = {0: 1, 1: 3, 3: 2, 2: 0}
 PREV = {v: k for k, v in NEXT.items()}
 NN = (((1,), (0,)), ((), ()))
+NT = (((1,), (1,)), ((), ()))
 
 
 def split(x):
@@ -22,14 +23,20 @@
     return hi, lo
 
 
-def own_kernel(plan, rows_step, place_ref, d_ref, *refs):
+def ring_place(index, steps):
+    at = (index ^ (index >> 1)) - steps & 3
+    return at ^ (at >> 1)
+
+
+def own_kernel(ringed, plan, rows_step, place_ref, d_ref, *refs):
     pieces = refs[: len(plan)]
     halves_ref, block_ref, stage, dtcat, full_ref, sem = refs[len(plan) :]
     width = d_ref.shape[0]
     part = stage.shape[1] // 4
     todo = []
     for n, (s, row, rows) in enumerate(plan):
-        lanes = pl.ds(pl.multiple_of(place_ref[s] * part, part), part)
+        source = ring_place(place_ref[1], s) if ringed else s
+        lanes = pl.ds(pl.multiple_of(source * part, part), part)
         todo.append(
             pltpu.make_async_copy(pieces[n], stage.at[pl.ds(row, rows), lanes], sem.at[n])
         )
@@ -41,7 +48,7 @@
     dtcat[2 * width :, :] = lo
     for c in todo:
         c.wait()
-    mine = pl.ds(pl.multiple_of(place_ref[4] * part, part), part)
+    mine = pl.ds(pl.multiple_of(place_ref[1] * part, part), part)
 
     def body(n, carry):
         at = pl.ds(pl.multiple_of(n * rows_step, rows_step), rows_step)
@@ -58,12 +65,12 @@
     lax.fori_loop(0, stage.shape[0] // rows_step, body, 0)
 
 
-def own_factor(place, d, pieces, plan, rows, rows_step):
+def own_factor(place, d, pieces, plan, ringed, rows, rows_step):
     width = d.shape[0]
     part = width // 4
     whole = pl.BlockSpec(memory_space=pltpu.VMEM)
     return pl.pallas_call(
-        functools.partial(own_kernel, plan, rows_step),
+        functools.partial(own_kernel, ringed, plan, rows_step),
         out_shape=(
             jax.ShapeDtypeStruct((rows, 2 * width), jnp.bfloat16),
             jax.ShapeDtypeStruct((rows, part), jnp.float32),
@@ -85,43 +92,71 @@
     )(place, d, *pieces)
 
 
+def pair_kernel(d_ref, panel_ref, top_ref, low_ref):
+    width = d_ref.shape[0]
+    half = width // 2
+    d_hi, d_lo = split(d_ref[...])
+    hi, lo = split(jnp.concatenate([panel_ref[s] for s in range(4)], axis=1))
+    for ref, rows, upto in ((top_ref, slice(0, half), half), (low_ref, slice(half, width), width)):
+        d_rows = d_hi[rows, :upto]
+        lhs = jnp.concatenate([d_rows, d_rows, d_lo[rows, :upto]], axis=1)
+        rhs = jnp.concatenate([hi[:, :upto], lo[:, :upto], hi[:, :upto]], axis=1)
+        ref[...] = lax.dot_general(lhs, rhs, NT, preferred_element_type=jnp.float32)
+
+
+def pair_factor(d, panel, rows_step):
+    width = d.shape[0]
+    parts, rows, part = panel.shape
+    out = jax.ShapeDtypeStruct((width // 2, rows), jnp.float32)
+    out_block = pl.BlockSpec((width // 2, rows_step), lambda n: (0, n))
+    return pl.pallas_call(
+        pair_kernel,
+        grid=(rows // rows_step,),
+        out_shape=(out, out),
+        in_specs=[
+            pl.BlockSpec((width, width), lambda n: (0, 0)),
+            pl.BlockSpec((parts, rows_step, part), lambda n: (0, n, 0)),
+        ],
+        out_specs=(out_block, out_block),
+        compiler_params=pltpu.CompilerParams(vmem_limit_bytes=32 << 20),
+        cost_estimate=pl.CostEstimate(
+            flops=6 * rows * width * width, bytes_accessed=8 * rows * width, transcendentals=0
+        ),
+        name="pair_factor",
+    )(d, panel)
+
+
 def front_kernel(
-    plan, place_ref, entry_ref, start_ref, d_ref, agg_ref, own_ref, trail_ref, *refs
+    ringed, plan, place_ref, entry_ref, start_ref, agg_ref, own_ref, trail_ref, *refs
 ):
     pieces = refs[: len(plan)]
-    out_ref, stage, dcat, pair_cat, sem = refs[len(plan) :]
+    out_ref, stage, pair_cat, sem = refs[len(plan) :]
     j, i = pl.program_id(0), pl.program_id(1)
     n_i = pl.num_programs(1)
     bm, bn = out_ref.shape
-    width = d_ref.shape[0]
+    width = stage.shape[0]
 
     @pl.when((i == 0) & (j == 0))
     def _():
         todo = []
-        for n, (where, half) in enumerate(plan):
-            _, depth, cols = pieces[n].shape
-            at = pl.ds(pl.multiple_of(place_ref[where] * depth, 8), depth)
-            todo.append(
-                pltpu.make_async_copy(
-                    pieces[n], stage.at[:, at, pl.ds(half * cols, cols)], sem.at[n]
-                )
-            )
+        for n, (half, steps, swap) in enumerate(plan):
+            depth, cols = pieces[n].shape
+            block = 0
+            if ringed:
+                chip = ring_place(place_ref[0] // 2, steps)
+                block = (place_ref[0] % 2 ^ swap) * 4 + chip
+            at = pl.ds(pl.multiple_of(block * cols, TILE_COLS), cols)
+            rows = pl.ds(half * depth, depth)
+            todo.append(pltpu.make_async_copy(pieces[n], stage.at[rows, at], sem.at[n]))
         for c in todo:
             c.start()
-        hi, lo = split(d_ref[...])
-        dcat[:, 0:width] = hi
-        dcat[:, width : 2 * width] = hi
-        dcat[:, 2 * width :] = lo
         for c in todo:
             c.wait()
 
     @pl.when(i == 0)
     def _():
         cols = pl.ds(pl.multiple_of(j * bn, bn), bn)
-        hi, lo = split(stage[:, :, cols].reshape(width, bn))
-        rhs = jnp.concatenate([hi, lo, hi], axis=0)
-        turned = lax.dot_general(dcat[...], rhs, NN, preferred_element_type=jnp.float32)
-        hi, lo = split(turned)
+        hi, lo = split(stage[:, cols])
         pair_cat[0:width, :] = hi
         pair_cat[width : 2 * width, :] = lo
         pair_cat[2 * width :, :] = hi
@@ -143,33 +178,32 @@
     lax.fori_loop(start_ref[step], start_ref[step + 1], add, 0)
 
 
-def front(place, entries, starts, d, agg, own, trailing, pieces, plan, bm, bn):
+def front(place, entries, starts, agg, own, trailing, pieces, plan, ringed, bm, bn):
     rows, cols = trailing.shape
-    width = d.shape[0]
+    width = own.shape[1] // 2
     whole = pl.BlockSpec(memory_space=pltpu.VMEM)
     smem = pl.BlockSpec(memory_space=pltpu.SMEM)
     block = pl.BlockSpec((bm, bn), lambda j, i: (i, j))
     return pl.pallas_call(
-        functools.partial(front_kernel, plan),
+        functools.partial(front_kernel, ringed, plan),
         grid=(cols // bn, rows // bm),
         out_shape=jax.ShapeDtypeStruct((rows, cols), jnp.float32),
-        in_specs=[smem, smem, smem, whole, whole, whole, block]
+        in_specs=[smem, smem, smem, whole, whole, block]
         + [pl.BlockSpec(memory_space=pl.ANY)] * len(pieces),
         out_specs=block,
         scratch_shapes=[
-            pltpu.VMEM((4, width // 4, cols), jnp.float32),
-            pltpu.VMEM((width, 3 * width), jnp.bfloat16),
+            pltpu.VMEM((width, cols), jnp.float32),
             pltpu.VMEM((3 * width, bn), jnp.bfloat16),
             pltpu.SemaphoreType.DMA((len(pieces),)),
         ],
         compiler_params=pltpu.CompilerParams(vmem_limit_bytes=VMEM_LIMIT),
         cost_estimate=pl.CostEstimate(
-            flops=6 * (rows + width) * width * cols,
+            flops=6 * rows * width * cols,
             bytes_accessed=8 * rows * cols + 4 * width * cols,
             transcendentals=0,
         ),
         name="front",
-    )(place, entries, starts, d, agg, own, trailing, *pieces)
+    )(place, entries, starts, agg, own, trailing, *pieces)
 
 
 def exchange_tiles(agg_vals, agg_dest, agg_tile, tiles_dev):
@@ -220,56 +254,45 @@
     col_index = lax.axis_index("col")
     tile_cols = local_cols // TILE_COLS
     tiles_dev = (local_rows // TILE_ROWS) * tile_cols
-    bm = 512 if local_rows % 512 == 0 else local_rows
-    bn = 768
+    bm = 768 if local_rows % 768 == 0 else local_rows
+    bn = 1024
     n_i, n_j = local_rows // bm, local_cols // bn
 
-    if row_devices == 8 and col_devices == 4:
-        row_index = lax.axis_index("row")
-        chip, core = row_index // 2, row_index % 2
+    row_index = lax.axis_index("row")
+    place = jnp.stack([row_index, col_index]).astype(jnp.int32)
+    ringed = row_devices == 8 and col_devices == 4
+    if ringed:
         half = local_rows // 2
         ring = list(NEXT.items())
         parts = [(panel[:half], panel[half:])]
-        parts.append(tuple(lax.ppermute(x, "col", ring) for x in parts[-1]))
-        depth = part // row_devices
+        for _ in range(3):
+            parts.append(tuple(lax.ppermute(x, "col", ring) for x in parts[-1]))
+        quarter = local_rows // 4
         spread = lax.all_to_all(
-            panel.T.reshape(row_devices, depth, local_rows),
+            panel.reshape(4, quarter, part),
             "row",
             split_axis=0,
             concat_axis=0,
+            axis_index_groups=[[0, 2, 4, 6], [1, 3, 5, 7]],
             tiled=True,
         )
-        spread, parts[1] = lax.optimization_barrier((spread, parts[1]))
-        wanted = lax.all_to_all(
-            spread.reshape(col_devices, 2, depth, local_rows),
-            "col",
-            split_axis=0,
-            concat_axis=0,
-            tiled=True,
+        spread, first = lax.optimization_barrier((spread, parts[1]))
+        wanted = lax.all_to_all(spread, "col", split_axis=0, concat_axis=0, tiled=True)
+        wanted, second, agg_vals, agg_dest, agg_tile = lax.optimization_barrier(
+            (wanted, parts[2], agg_vals, agg_dest, agg_tile)
         )
-        wanted, parts[1], agg_vals, agg_dest, agg_tile = lax.optimization_barrier(
-            (wanted, parts[1], agg_vals, agg_dest, agg_tile)
-        )
-        for _ in range(2):
-            parts.append(tuple(lax.ppermute(x, "col", ring) for x in parts[-1]))
         siblings = [(p, p ^ 1) for p in range(row_devices)]
-        following = jnp.array([NEXT[c] for c in range(4)], jnp.int32)
-        previous = jnp.array([PREV[c] for c in range(4)], jnp.int32)
-        places, pieces, plan = [], [], []
-        for k, (step, back) in enumerate(((NEXT, previous), (PREV, following))):
+        pieces, plan = [], []
+        turns = ((NEXT, 1), (PREV, -1))
+        for h, piece in enumerate(pair_factor(diag_inverse, wanted, quarter)):
+            step, sign = turns[h]
             turn = [(2 * c + m, 2 * step[c] + m) for c in range(4) for m in range(2)]
-            piece, source = wanted[:, k], chip
             for n in range(4):
                 if n > 0:
-                    piece, source = lax.ppermute(piece, "row", turn), back[source]
-                plan += [(5 + len(places), k), (6 + len(places), k)]
-                places += [2 * source + core, 2 * source + 1 - core]
+                    piece = lax.ppermute(piece, "row", turn)
+                plan += [(h, sign * n, 0), (h, sign * n, 1)]
                 pieces += [piece, lax.ppermute(piece, "row", siblings)]
-        sources = [jnp.arange(4, dtype=jnp.int32)]
-        for _ in range(3):
-            sources.append(previous[sources[-1]])
-        order = jnp.stack(sources)[:, col_index]
-        own = [panel] + [x for halves in parts[1:] for x in halves]
+        own = [panel] + [x for halves in [first, second, parts[3]] for x in halves]
         own_plan = [(0, 0, local_rows)]
         own_plan += [(s, r * half, half) for s in range(1, 4) for r in range(2)]
     else:
@@ -277,19 +300,20 @@
         column = lax.all_gather(panel, "row", axis=0, tiled=True)
         column = column.reshape(col_devices, local_cols, part)
         partner = lax.all_to_all(column, "col", split_axis=0, concat_axis=0, tiled=True)
-        places, pieces, plan = [jnp.int32(0)], [jnp.swapaxes(partner, 1, 2)], [(5, 0)]
+        pieces, plan = pair_factor(diag_inverse, partner, 768), [(0, 0, 0), (1, 0, 0)]
         own = [whole[s] for s in range(col_devices)]
         own_plan = [(s, 0, local_rows) for s in range(col_devices)]
-        order = jnp.arange(4, dtype=jnp.int32)
 
     agg, landing = exchange_tiles(agg_vals, agg_dest, agg_tile, tiles_dev)
     entries, starts = order_tiles(
         landing, row_devices * CAP, tiles_dev, tile_cols, bm, bn, n_i, n_j
     )
-    place = jnp.concatenate([order, jnp.stack([col_index] + places)]).astype(jnp.int32)
-    halves, own_block = own_factor(place, diag_inverse, own, own_plan, local_rows, bm)
+    rows_step = 512 if local_rows % 512 == 0 else local_rows
+    halves, own_block = own_factor(
+        place, diag_inverse, own, own_plan, ringed, local_rows, rows_step
+    )
     updated = front(
-        place, entries, starts, diag_inverse, agg, halves, trailing, pieces, plan, bm, bn
+        place, entries, starts, agg, halves, trailing, pieces, plan, ringed, bm, bn
     )
     return updated, own_block
 

time: 156 us -> 144 us (0.923)
  waiting for transfers between devices: 49 us -> 64.6 us
  between operations: 11.9 us -> 0.95 us
  local copies, waits for them, and re-layouts: 15.2 us -> 5.72 us
  Pallas kernels: 40.4 us -> 34.1 us
  starting transfers between devices: 33.1 us -> 31 us
    ppermute x6, waiting for transfers between devices: 0.02 us -> 13.6 us  [per_device(): piece = lax.ppermute(piece, 'row', turn)]
    dynamic_slice x6 -> x0, local copies, waits for them, and re-layouts: 7.61 us -> none  [per_device(): piece, source = (lax.ppermute(piece, 'row', turn), back[source])]
    pallas_call x2 -> x3, Pallas kernels: 40.4 us -> 34.1 us  [the longest x1 25.3 us: front(): pl.pallas_call(functools.partial(front_kernel, ringed, plan), grid=(cols...]
    ppermute x6, starting transfers between devices: 11.4 us -> 9.1 us  [per_device(): parts.append(tuple((lax.ppermute(x, 'col', ring) for x in parts[-1])))]
  transfers between devices with their start and end apart: 23 -> 23, of which waited for: 7 -> 9; matrix products, arithmetic and copies ran while one was open for 8% -> 7% of each run, Pallas kernels for 5% -> 6%
where the time goes in v4:
time: 144 us; the launch traced here: 142 us
  waiting for transfers between devices  64.6 us (45%)
  Pallas kernels  34.1 us (24%)
  starting transfers between devices  31 us (22%)
  other arithmetic  5.96 us (4%)
  local copies, waits for them, and re-layouts  5.72 us (4%)
    ppermute x6, waiting for transfers between devices, per_device(): parts.append(tuple((lax.ppermute(x, 'col', ring) for x in parts[-1])))  49.9 us
    pallas_call x1, Pallas kernels, front(): pl.pallas_call(functools.partial(front_kernel, ringed, plan), grid=(cols...  25.3 us
    ppermute x6, waiting for transfers between devices, per_device(): piece = lax.ppermute(piece, 'row', turn)  13.6 us
    ppermute x6, starting transfers between devices, per_device(): parts.append(tuple((lax.ppermute(x, 'col', ring) for x in parts[-1])))  9.1 us
    pallas_call x1, Pallas kernels, own_factor(): pl.pallas_call(functools.partial(own_kernel, ringed, plan, rows_step), ou...  8.1 us
    ppermute x6, starting transfers between devices, per_device(): piece = lax.ppermute(piece, 'row', turn)  7.75 us
    all_to_all x1, starting transfers between devices, per_device(): lax.all_to_all(panel.reshape(4, quarter, part), 'row', split_axis=0, conc...  5.18 us
    all_to_all x1, starting transfers between devices, per_device(): lax.all_to_all(spread, 'col', split_axis=0, concat_axis=0, tiled=True)  4.92 us
  transfers between devices with their start and end apart: 23, of which 9 were waited for; matrix products, arithmetic and copies ran while one was open for 7% of the time, Pallas kernels for 6%

profile of v4, /device:TPU:0, one launch (start us, length us, event | category | flops | bytes accessed | tf_op | source)
XLA Modules:
  0.0 142.5 jit_solution(4535732763355166590)
XLA Ops:
  0.6 5.2 %all-to-all-start = ((f32[4,384,128]{2,1,0:T(8,128)}), f32[4,384,128]{2,1,0:T(8,128)}, u32[]{:S(2)}, u32[]{:S(2)}) async-start(f32[4,384,128]{2,1,0:T(8,128)} %bitcast.22), calls=%async_computation | async-start | bytes 1572864 | tf_op jit(solution)/shard_map/all_to_all | solution.py:271
  5.8 1.2 fusion.7
  7.0 2.1 %collective-permute-start.1 = (f32[768,128]{1,0:T(8,128)S(1)}, f32[768,128]{1,0:T(8,128)S(1)}, u32[]{:S(2)}, u32[]{:S(2)}) collective-permute-start(f32[768,128]{1,0:T(8,128)S(1)} %get-tuple-element.30), channel_id=1, source_target_pairs={{0,1},{1,3},{3,2},{2,0},{4,5},{5,7},{7,6},{6,4},{8,9},{9,11},{11,1... | collective-permute-start | bytes 1179656 | tf_op jit(solution)/shard_map/ppermute | solution.py:269
  9.1 2.6 %collective-permute-start = (f32[768,128]{1,0:T(8,128)S(1)}, f32[768,128]{1,0:T(8,128)S(1)}, u32[]{:S(2)}, u32[]{:S(2)}) collective-permute-start(f32[768,128]{1,0:T(8,128)S(1)} %get-tuple-element.31), channel_id=1, source_target_pairs={{0,1},{1,3},{3,2},{2,0},{4,5},{5,7},{7,6},{6,4},{8,9},{9,11},{11,1... | collective-permute-start | bytes 1179656 | tf_op jit(solution)/shard_map/ppermute | solution.py:269
  11.7 8.4 %collective-permute-done.1.refs_2_ = f32[768,128]{1,0:T(8,128)S(1)} collective-permute-done((f32[768,128]{1,0:T(8,128)S(1)}, f32[768,128]{1,0:T(8,128)S(1)}, u32[]{:S(2)}, u32[]{:S(2)}) %collective-permute-start.1) | collective-permute-done | bytes 393248 | tf_op jit(solution)/shard_map/ppermute | solution.py:269
  20.1 7.6 %collective-permute-done.refs_1_ = f32[768,128]{1,0:T(8,128)S(1)} collective-permute-done((f32[768,128]{1,0:T(8,128)S(1)}, f32[768,128]{1,0:T(8,128)S(1)}, u32[]{:S(2)}, u32[]{:S(2)}) %collective-permute-start) | collective-permute-done | bytes 393248 | tf_op jit(solution)/shard_map/ppermute | solution.py:269
  27.7 4.9 %all-to-all-start.1 = ((f32[4,384,128]{2,1,0:T(8,128)}), f32[4,384,128]{2,1,0:T(8,128)S(1)}, u32[]{:S(2)}, u32[]{:S(2)}) async-start(f32[4,384,128]{2,1,0:T(8,128)} %all-to-all-done), calls=%async_computation.1 | async-start | bytes 1572864 | tf_op jit(solution)/shard_map/all_to_all | solution.py:280
  32.6 2.0 %collective-permute-start.3 = (f32[768,128]{1,0:T(8,128)S(1)}, f32[768,128]{1,0:T(8,128)S(1)}, u32[]{:S(2)}, u32[]{:S(2)}) collective-permute-start(f32[768,128]{1,0:T(8,128)S(1)} %collective-permute-done.1.refs_2_), channel_id=1, source_target_pairs={{0,1},{1,3},{3,2},{2,0},{4,5},{5,7},{7,6},{6,4},{8,9},{9,11},{11,1... | collective-permute-start | bytes 1179656 | tf_op jit(solution)/shard_map/ppermute | solution.py:269
  34.6 2.4 %collective-permute-start.2 = (f32[768,128]{1,0:T(8,128)S(1)}, f32[768,128]{1,0:T(8,128)}, u32[]{:S(2)}, u32[]{:S(2)}) collective-permute-start(f32[768,128]{1,0:T(8,128)S(1)} %collective-permute-done.refs_1_), channel_id=1, source_target_pairs={{0,1},{1,3},{3,2},{2,0},{4,5},{5,7},{7,6},{6,4},{8,9},{9,11},{11,1... | collective-permute-start | bytes 1179656 | tf_op jit(solution)/shard_map/ppermute | solution.py:269
  37.6 23.7 %collective-permute-done.3.refs_4_ = f32[768,128]{1,0:T(8,128)S(1)} collective-permute-done((f32[768,128]{1,0:T(8,128)S(1)}, f32[768,128]{1,0:T(8,128)S(1)}, u32[]{:S(2)}, u32[]{:S(2)}) %collective-permute-start.3) | collective-permute-done | bytes 393248 | tf_op jit(solution)/shard_map/ppermute | solution.py:269
  61.3 8.5 %collective-permute-done.2.refs_3_ = f32[768,128]{1,0:T(8,128)} collective-permute-done((f32[768,128]{1,0:T(8,128)S(1)}, f32[768,128]{1,0:T(8,128)}, u32[]{:S(2)}, u32[]{:S(2)}) %collective-permute-start.2) | collective-permute-done | bytes 393248 | tf_op jit(solution)/shard_map/ppermute | solution.py:269
  69.8 1.2 copy-done
  71.9 1.4 collective-permute-start.7
  76.4 1.5 %scatter_fusion = f32[16,8,128]{2,1,0:T(8,128)S(1)} fusion(f32[16,8,128]{2,1,0:T(8,128)S(1)} %broadcast_in_dim.18, s32[12]{0:T(128)S(1)} %fusion.6, f32[12,8,128]{2,1,0:T(8,128)} %bitcast.25), kind=kCustom, calls=%fused_computation | custom fusion | bytes 147504 | tf_op jit(solution)/shard_map/scatter | solution.py:221
  78.6 3.4 %all-to-all-start.2 = ((f32[8,3,8,128]{3,2,1,0:T(8,128)}), f32[8,3,8,128]{3,2,1,0:T(8,128)S(1)}, u32[]{:S(2)}, u32[]{:S(2)}) async-start(f32[8,3,8,128]{3,2,1,0:T(8,128)} %select_maximum_fusion), calls=%async_computation.2 | async-start | bytes 196608 | tf_op jit(solution)/shard_map/all_to_all | solution.py:225
  82.0 1.9 %collective-permute-start.14 = (f32[256,384]{1,0:T(8,128)S(1)}, f32[256,384]{1,0:T(8,128)S(1)}, u32[]{:S(2)}, u32[]{:S(2)}) collective-permute-start(f32[256,384]{1,0:T(8,128)S(1)} %get-tuple-element.26.refs_8_), channel_id=1, source_target_pairs={{0,16},{4,20},{8,0},{12,4},{16,24},{20,28},{24,8},{28,12},{1,17},{... | collective-permute-start | bytes 1179656 | tf_op jit(solution)/shard_map/ppermute | solution.py:292
  83.9 1.7 %collective-permute-done.4.refs_5_ = f32[768,128]{1,0:T(8,128)} collective-permute-done((f32[768,128]{1,0:T(8,128)}, f32[768,128]{1,0:T(8,128)}, u32[]{:S(2)}, u32[]{:S(2)}) %collective-permute-start.4) | collective-permute-done | bytes 393248 | tf_op jit(solution)/shard_map/ppermute | solution.py:269
  85.6 8.1 %own_factor.1 = (bf16[1536,1024]{1,0:T(8,128)(2,1)}, f32[1536,128]{1,0:T(8,128)}) custom-call(s32[2]{0:T(128)} %pad_add_fusion.1.place_ref, f32[512,512]{1,0:T(8,128)} %d_ref.3, f32[1536,128]{1,0:T(8,128)} %refs_0_.1, f32[768,128]{1,0:T(8,128)} %copy-done.11, f32[768,128]{1,0:T(8,128)} %copy-done.10, f32[768,128]{1,0:T(8,128)} %collective-permute-done.2.refs_3_, ...), custom_call_target="tpu_custom_call" | custom-call | flops 2415919104 | bytes 7864320 | tf_op jit(solution)/shard_map/own_factor/pallas_call | solution.py:72
  93.9 1.4 collective-permute-start.9
  96.8 7.2 %collective-permute-done.9.refs_4_ = f32[256,384]{1,0:T(8,128)S(1)} collective-permute-done((f32[256,384]{1,0:T(8,128)S(1)}, f32[256,384]{1,0:T(8,128)S(1)}, u32[]{:S(2)}, u32[]{:S(2)}) %collective-permute-start.9) | collective-permute-done | bytes 393248 | tf_op jit(solution)/shard_map/ppermute | solution.py:292
  104.0 1.4 collective-permute-start.11
  108.1 5.1 %collective-permute-done.11.refs_6_ = f32[256,384]{1,0:T(8,128)} collective-permute-done((f32[256,384]{1,0:T(8,128)S(1)}, f32[256,384]{1,0:T(8,128)}, u32[]{:S(2)}, u32[]{:S(2)}) %collective-permute-start.11) | collective-permute-done | bytes 393248 | tf_op jit(solution)/shard_map/ppermute | solution.py:292
  113.2 1.3 collective-permute-done.18.refs_14_
  117.2 25.3 %front.1 = f32[1536,3072]{1,0:T(8,128)} custom-call(s32[2]{0:T(128)} %pad_add_fusion.1.place_ref, s32[3,16]{1,0:T(4,128)} %multiply_reduce_fusion.entry_ref, s32[7]{0:T(128)} %convert_reduce_fusion.2.start_ref, f32[24,8,128]{2,1,0:T(8,128)} %bitcast.24, bf16[1536,1024]{1,0:T(8,128)(2,1)} %get-tuple-element.23.own_ref, f32[1536,3072]{1,0:T(8,128)} %trail_ref.1, ...), custom_call_target="tpu_custom_call" | custom-call | flops 14495514624 | bytes 44040192 | tf_op jit(solution)/shard_map/front/pallas_call | solution.py:187
  (97 shorter events, 12.0 us)
Async XLA Ops:
  0.6 27.0 %all-to-all-start = ((f32[4,384,128]{2,1,0:T(8,128)}), f32[4,384,128]{2,1,0:T(8,128)}, u32[]{:S(2)}, u32[]{:S(2)}) async-start(f32[4,384,128]{2,1,0:T(8,128)} %bitcast.22), calls=%async_computation | async-start | bytes 1572864 | tf_op jit(solution)/shard_map/all_to_all | solution.py:271
  7.0 13.1 %collective-permute-start.1 = (f32[768,128]{1,0:T(8,128)S(1)}, f32[768,128]{1,0:T(8,128)S(1)}, u32[]{:S(2)}, u32[]{:S(2)}) collective-permute-start(f32[768,128]{1,0:T(8,128)S(1)} %get-tuple-element.30), channel_id=1, source_target_pairs={{0,1},{1,3},{3,2},{2,0},{4,5},{5,7},{7,6},{6,4},{8,9},{9,11},{11,1... | collective-permute-start | bytes 1179656 | tf_op jit(solution)/shard_map/ppermute | solution.py:269
  9.1 18.6 %collective-permute-start = (f32[768,128]{1,0:T(8,128)S(1)}, f32[768,128]{1,0:T(8,128)S(1)}, u32[]{:S(2)}, u32[]{:S(2)}) collective-permute-start(f32[768,128]{1,0:T(8,128)S(1)} %get-tuple-element.31), channel_id=1, source_target_pairs={{0,1},{1,3},{3,2},{2,0},{4,5},{5,7},{7,6},{6,4},{8,9},{9,11},{11,1... | collective-permute-start | bytes 1179656 | tf_op jit(solution)/shard_map/ppermute | solution.py:269
  20.0 65.6 %copy-start.10 = (f32[768,128]{1,0:T(8,128)}, f32[768,128]{1,0:T(8,128)S(1)}, u32[]{:S(2)}) copy-start(f32[768,128]{1,0:T(8,128)S(1)} %collective-permute-done.1.refs_2_) | copy-start | bytes 1179652
  27.7 42.2 %all-to-all-start.1 = ((f32[4,384,128]{2,1,0:T(8,128)}), f32[4,384,128]{2,1,0:T(8,128)S(1)}, u32[]{:S(2)}, u32[]{:S(2)}) async-start(f32[4,384,128]{2,1,0:T(8,128)} %all-to-all-done), calls=%async_computation.1 | async-start | bytes 1572864 | tf_op jit(solution)/shard_map/all_to_all | solution.py:280
  32.6 28.7 %collective-permute-start.3 = (f32[768,128]{1,0:T(8,128)S(1)}, f32[768,128]{1,0:T(8,128)S(1)}, u32[]{:S(2)}, u32[]{:S(2)}) collective-permute-start(f32[768,128]{1,0:T(8,128)S(1)} %collective-permute-done.1.refs_2_), channel_id=1, source_target_pairs={{0,1},{1,3},{3,2},{2,0},{4,5},{5,7},{7,6},{6,4},{8,9},{9,11},{11,1... | collective-permute-start | bytes 1179656 | tf_op jit(solution)/shard_map/ppermute | solution.py:269
  34.6 35.2 %collective-permute-start.2 = (f32[768,128]{1,0:T(8,128)S(1)}, f32[768,128]{1,0:T(8,128)}, u32[]{:S(2)}, u32[]{:S(2)}) collective-permute-start(f32[768,128]{1,0:T(8,128)S(1)} %collective-permute-done.refs_1_), channel_id=1, source_target_pairs={{0,1},{1,3},{3,2},{2,0},{4,5},{5,7},{7,6},{6,4},{8,9},{9,11},{11,1... | collective-permute-start | bytes 1179656 | tf_op jit(solution)/shard_map/ppermute | solution.py:269
  61.3 22.6 %collective-permute-start.5 = (f32[768,128]{1,0:T(8,128)S(1)}, f32[768,128]{1,0:T(8,128)}, u32[]{:S(2)}, u32[]{:S(2)}) collective-permute-start(f32[768,128]{1,0:T(8,128)S(1)} %collective-permute-done.3.refs_4_), channel_id=1, source_target_pairs={{0,1},{1,3},{3,2},{2,0},{4,5},{5,7},{7,6},{6,4},{8,9},{9,11},{11,1... | collective-permute-start | bytes 1179656 | tf_op jit(solution)/shard_map/ppermute | solution.py:269
  69.8 15.8 %collective-permute-start.4 = (f32[768,128]{1,0:T(8,128)}, f32[768,128]{1,0:T(8,128)}, u32[]{:S(2)}, u32[]{:S(2)}) collective-permute-start(f32[768,128]{1,0:T(8,128)} %collective-permute-done.2.refs_3_), channel_id=1, source_target_pairs={{0,1},{1,3},{3,2},{2,0},{4,5},{5,7},{7,6},{6,4},{8,9},{9,11},{11,1... | collective-permute-start | bytes 1179656 | tf_op jit(solution)/shard_map/ppermute | solution.py:269
  71.9 22.0 %collective-permute-start.7 = (f32[256,384]{1,0:T(8,128)S(1)}, f32[256,384]{1,0:T(8,128)S(1)}, u32[]{:S(2)}, u32[]{:S(2)}) collective-permute-start(f32[256,384]{1,0:T(8,128)S(1)} %get-tuple-element.25.refs_0_), channel_id=1, source_target_pairs={{0,8},{4,12},{8,24},{12,28},{16,0},{20,4},{24,16},{28,20},{1,9},{5... | collective-permute-start | bytes 1179656 | tf_op jit(solution)/shard_map/ppermute | solution.py:292
  73.3 34.1 %collective-permute-start.6 = (f32[256,384]{1,0:T(8,128)S(1)}, f32[256,384]{1,0:T(8,128)S(1)}, u32[]{:S(2)}, u32[]{:S(2)}) collective-permute-start(f32[256,384]{1,0:T(8,128)S(1)} %get-tuple-element.25.refs_0_), channel_id=1, source_target_pairs={{0,4},{4,0},{8,12},{12,8},{16,20},{20,16},{24,28},{28,24},{1,5},{5... | collective-permute-start | bytes 1179656 | tf_op jit(solution)/shard_map/ppermute | solution.py:294
  78.6 15.1 %all-to-all-start.2 = ((f32[8,3,8,128]{3,2,1,0:T(8,128)}), f32[8,3,8,128]{3,2,1,0:T(8,128)S(1)}, u32[]{:S(2)}, u32[]{:S(2)}) async-start(f32[8,3,8,128]{3,2,1,0:T(8,128)} %select_maximum_fusion), calls=%async_computation.2 | async-start | bytes 196608 | tf_op jit(solution)/shard_map/all_to_all | solution.py:225
  82.0 13.3 %collective-permute-start.14 = (f32[256,384]{1,0:T(8,128)S(1)}, f32[256,384]{1,0:T(8,128)S(1)}, u32[]{:S(2)}, u32[]{:S(2)}) collective-permute-start(f32[256,384]{1,0:T(8,128)S(1)} %get-tuple-element.26.refs_8_), channel_id=1, source_target_pairs={{0,16},{4,20},{8,0},{12,4},{16,24},{20,28},{24,8},{28,12},{1,17},{... | collective-permute-start | bytes 1179656 | tf_op jit(solution)/shard_map/ppermute | solution.py:292
  83.9 23.6 %collective-permute-start.13 = (f32[256,384]{1,0:T(8,128)S(1)}, f32[256,384]{1,0:T(8,128)S(1)}, u32[]{:S(2)}, u32[]{:S(2)}) collective-permute-start(f32[256,384]{1,0:T(8,128)S(1)} %get-tuple-element.26.refs_8_), channel_id=1, source_target_pairs={{0,4},{4,0},{8,12},{12,8},{16,20},{20,16},{24,28},{28,24},{1,5},{5... | collective-permute-start | bytes 1179656 | tf_op jit(solution)/shard_map/ppermute | solution.py:294
  93.9 10.1 %collective-permute-start.9 = (f32[256,384]{1,0:T(8,128)S(1)}, f32[256,384]{1,0:T(8,128)S(1)}, u32[]{:S(2)}, u32[]{:S(2)}) collective-permute-start(f32[256,384]{1,0:T(8,128)S(1)} %collective-permute-done.7.refs_2_), channel_id=1, source_target_pairs={{0,8},{4,12},{8,24},{12,28},{16,0},{20,4},{24,16},{28,20},{1,9},{5... | collective-permute-start | bytes 1179656 | tf_op jit(solution)/shard_map/ppermute | solution.py:292
  95.3 10.1 %collective-permute-start.16 = (f32[256,384]{1,0:T(8,128)S(1)}, f32[256,384]{1,0:T(8,128)S(1)}, u32[]{:S(2)}, u32[]{:S(2)}) collective-permute-start(f32[256,384]{1,0:T(8,128)S(1)} %collective-permute-done.14.refs_10_), channel_id=1, source_target_pairs={{0,16},{4,20},{8,0},{12,4},{16,24},{20,28},{24,8},{28,12},{1,17},{... | collective-permute-start | bytes 1179656 | tf_op jit(solution)/shard_map/ppermute | solution.py:292
  96.7 11.3 %collective-permute-start.8 = (f32[256,384]{1,0:T(8,128)S(1)}, f32[256,384]{1,0:T(8,128)}, u32[]{:S(2)}, u32[]{:S(2)}) collective-permute-start(f32[256,384]{1,0:T(8,128)S(1)} %collective-permute-done.7.refs_2_), channel_id=1, source_target_pairs={{0,4},{4,0},{8,12},{12,8},{16,20},{20,16},{24,28},{28,24},{1,5},{5... | collective-permute-start | bytes 1179656 | tf_op jit(solution)/shard_map/ppermute | solution.py:294
  104.0 9.3 %collective-permute-start.11 = (f32[256,384]{1,0:T(8,128)S(1)}, f32[256,384]{1,0:T(8,128)}, u32[]{:S(2)}, u32[]{:S(2)}) collective-permute-start(f32[256,384]{1,0:T(8,128)S(1)} %collective-permute-done.9.refs_4_), channel_id=1, source_target_pairs={{0,8},{4,12},{8,24},{12,28},{16,0},{20,4},{24,16},{28,20},{1,9},{5... | collective-permute-start | bytes 1179656 | tf_op jit(solution)/shard_map/ppermute | solution.py:292
  105.4 9.1 %collective-permute-start.18 = (f32[256,384]{1,0:T(8,128)S(1)}, f32[256,384]{1,0:T(8,128)}, u32[]{:S(2)}, u32[]{:S(2)}) collective-permute-start(f32[256,384]{1,0:T(8,128)S(1)} %collective-permute-done.16.refs_12_), channel_id=1, source_target_pairs={{0,16},{4,20},{8,0},{12,4},{16,24},{20,28},{24,8},{28,12},{1,17},{... | collective-permute-start | bytes 1179656 | tf_op jit(solution)/shard_map/ppermute | solution.py:292
  107.4 7.9 %collective-permute-start.15 = (f32[256,384]{1,0:T(8,128)S(1)}, f32[256,384]{1,0:T(8,128)S(1)}, u32[]{:S(2)}, u32[]{:S(2)}) collective-permute-start(f32[256,384]{1,0:T(8,128)S(1)} %collective-permute-done.14.refs_10_), channel_id=1, source_target_pairs={{0,4},{4,0},{8,12},{12,8},{16,20},{20,16},{24,28},{28,24},{1,5},{5... | collective-permute-start | bytes 1179656 | tf_op jit(solution)/shard_map/ppermute | solution.py:294
  107.5 7.8 %collective-permute-start.10 = (f32[256,384]{1,0:T(8,128)S(1)}, f32[256,384]{1,0:T(8,128)S(1)}, u32[]{:S(2)}, u32[]{:S(2)}) collective-permute-start(f32[256,384]{1,0:T(8,128)S(1)} %collective-permute-done.9.refs_4_), channel_id=1, source_target_pairs={{0,4},{4,0},{8,12},{12,8},{16,20},{20,16},{24,28},{28,24},{1,5},{5... | collective-permute-start | bytes 1179656 | tf_op jit(solution)/shard_map/ppermute | solution.py:294
  108.0 7.3 %collective-permute-start.17 = (f32[256,384]{1,0:T(8,128)S(1)}, f32[256,384]{1,0:T(8,128)S(1)}, u32[]{:S(2)}, u32[]{:S(2)}) collective-permute-start(f32[256,384]{1,0:T(8,128)S(1)} %collective-permute-done.16.refs_12_), channel_id=1, source_target_pairs={{0,4},{4,0},{8,12},{12,8},{16,20},{20,16},{24,28},{28,24},{1,5},{5... | collective-permute-start | bytes 1179656 | tf_op jit(solution)/shard_map/ppermute | solution.py:294
  113.2 2.1 %collective-permute-start.12 = (f32[256,384]{1,0:T(8,128)}, f32[256,384]{1,0:T(8,128)S(1)}, u32[]{:S(2)}, u32[]{:S(2)}) collective-permute-start(f32[256,384]{1,0:T(8,128)} %collective-permute-done.11.refs_6_), channel_id=1, source_target_pairs={{0,4},{4,0},{8,12},{12,8},{16,20},{20,16},{24,28},{28,24},{1,5},{5... | collective-permute-start | bytes 1179656 | tf_op jit(solution)/shard_map/ppermute | solution.py:294
  114.5 1.9 %collective-permute-start.19 = (f32[256,384]{1,0:T(8,128)}, f32[256,384]{1,0:T(8,128)S(1)}, u32[]{:S(2)}, u32[]{:S(2)}) collective-permute-start(f32[256,384]{1,0:T(8,128)} %collective-permute-done.18.refs_14_), channel_id=1, source_target_pairs={{0,4},{4,0},{8,12},{12,8},{16,20},{20,16},{24,28},{28,24},{1,5},{5... | collective-permute-start | bytes 1179656 | tf_op jit(solution)/shard_map/ppermute | solution.py:294
  (17 other events, 284.9 us)

commit v5 on v4

--- a/solution.py
+++ b/solution.py
@@ -118,7 +118,7 @@
             pl.BlockSpec((parts, rows_step, part), lambda n: (0, n, 0)),
         ],
         out_specs=(out_block, out_block),
-        compiler_params=pltpu.CompilerParams(vmem_limit_bytes=32 << 20),
+        compiler_params=pltpu.CompilerParams(vmem_limit_bytes=VMEM_LIMIT),
         cost_estimate=pl.CostEstimate(
             flops=6 * rows * width * width, bytes_accessed=8 * rows * width, transcendentals=0
         ),
@@ -164,8 +164,10 @@
     rows = pl.ds(pl.multiple_of(i * bm, bm), bm)
     hi, lo = own_ref[rows, 0:width], own_ref[rows, width:]
     lhs = jnp.concatenate([hi, hi, lo], axis=1)
-    product = lax.dot_general(lhs, pair_cat[...], NN, preferred_element_type=jnp.float32)
-    out_ref[...] = trail_ref[...] - product
+    for n in range(0, bn, 256):
+        at = slice(n, n + 256)
+        product = lax.dot_general(lhs, pair_cat[:, at], NN, preferred_element_type=jnp.float32)
+        out_ref[:, at] = trail_ref[:, at] - product
     step = j * n_i + i
 
     def add(e, carry):
@@ -206,7 +208,7 @@
     )(place, entries, starts, agg, own, trailing, *pieces)
 
 
-def exchange_tiles(agg_vals, agg_dest, agg_tile, tiles_dev):
+def pack_tiles(agg_vals, agg_dest, agg_tile, tiles_dev):
     row_devices = lax.axis_size("row")
     agg = agg_vals.shape[2]
     targets = agg_dest.reshape(-1)
@@ -222,9 +224,11 @@
     send = send.reshape(row_devices, CAP, TILE_ROWS, TILE_COLS)
     numbers = send_ids.astype(jnp.float32).reshape(row_devices, 1, 1, CAP)
     numbers = jnp.pad(numbers, ((0, 0), (0, 0), (0, TILE_ROWS - 1), (0, TILE_COLS - CAP)))
-    got = lax.all_to_all(
-        jnp.concatenate([send, numbers], axis=1), "row", split_axis=0, concat_axis=0, tiled=True
-    )
+    return jnp.concatenate([send, numbers], axis=1)
+
+
+def exchange_tiles(send, tiles_dev):
+    got = lax.all_to_all(send, "row", split_axis=0, concat_axis=0, tiled=True)
     landing = got[:, CAP, 0, :CAP].astype(jnp.int32)
     landing = jnp.pad(landing, ((0, 0), (0, 1)), constant_values=tiles_dev)
     return got.reshape(-1, TILE_ROWS, TILE_COLS), landing.reshape(-1)
@@ -260,6 +264,7 @@
 
     row_index = lax.axis_index("row")
     place = jnp.stack([row_index, col_index]).astype(jnp.int32)
+    tiles = pack_tiles(agg_vals, agg_dest, agg_tile, tiles_dev)
     ringed = row_devices == 8 and col_devices == 4
     if ringed:
         half = local_rows // 2
@@ -276,13 +281,11 @@
             axis_index_groups=[[0, 2, 4, 6], [1, 3, 5, 7]],
             tiled=True,
         )
-        spread, first = lax.optimization_barrier((spread, parts[1]))
+        spread, first, tiles = lax.optimization_barrier((spread, parts[1][0], tiles))
         wanted = lax.all_to_all(spread, "col", split_axis=0, concat_axis=0, tiled=True)
-        wanted, second, agg_vals, agg_dest, agg_tile = lax.optimization_barrier(
-            (wanted, parts[2], agg_vals, agg_dest, agg_tile)
-        )
+        wanted, second = lax.optimization_barrier((wanted, parts[2][0]))
         siblings = [(p, p ^ 1) for p in range(row_devices)]
-        pieces, plan = [], []
+        pieces, plan, across = [], [], []
         turns = ((NEXT, 1), (PREV, -1))
         for h, piece in enumerate(pair_factor(diag_inverse, wanted, quarter)):
             step, sign = turns[h]
@@ -290,9 +293,13 @@
             for n in range(4):
                 if n > 0:
                     piece = lax.ppermute(piece, "row", turn)
+                if n == 2:
+                    across.append(piece)
                 plan += [(h, sign * n, 0), (h, sign * n, 1)]
                 pieces += [piece, lax.ppermute(piece, "row", siblings)]
-        own = [panel] + [x for halves in [first, second, parts[3]] for x in halves]
+        last, across = lax.optimization_barrier((parts[3], tuple(across)))
+        pieces[4], pieces[12] = across
+        own = [panel, first, parts[1][1], second, parts[2][1], *last]
         own_plan = [(0, 0, local_rows)]
         own_plan += [(s, r * half, half) for s in range(1, 4) for r in range(2)]
     else:
@@ -304,7 +311,7 @@
         own = [whole[s] for s in range(col_devices)]
         own_plan = [(s, 0, local_rows) for s in range(col_devices)]
 
-    agg, landing = exchange_tiles(agg_vals, agg_dest, agg_tile, tiles_dev)
+    agg, landing = exchange_tiles(tiles, tiles_dev)
     entries, starts = order_tiles(
         landing, row_devices * CAP, tiles_dev, tile_cols, bm, bn, n_i, n_j
     )

time: 144 us -> 143 us (level)
  blocking collectives: 0 us -> 8.85 us
  waiting for transfers between devices: 64.6 us -> 59.7 us
  starting transfers between devices: 31 us -> 26.2 us
  Pallas kernels: 34.1 us -> 36.4 us
    all_to_all x0 -> x1, blocking collectives: none -> 8.85 us  [exchange_tiles(): got = lax.all_to_all(send, 'row', split_axis=0, concat_axis=0, tiled=True)]
    all_to_all x1 -> x0, starting transfers between devices: 3.36 us -> none  [exchange_tiles(): lax.all_to_all(jnp.concatenate([send, numbers], axis=1), 'row', split_axi...]
    pallas_call x1, Pallas kernels: 0.78 us -> 2.97 us  [pair_factor(): pl.pallas_call(pair_kernel, grid=(rows // rows_step,), out_shape=(out, ou...]
    ppermute x6, waiting for transfers between devices: 49.9 us -> 47.7 us  [per_device(): parts.append(tuple((lax.ppermute(x, 'col', ring) for x in parts[-1])))]
    ppermute x6, waiting for transfers between devices: 13.6 us -> 11.9 us  [per_device(): piece = lax.ppermute(piece, 'row', turn)]
    ppermute x6, starting transfers between devices: 7.75 us -> 6.08 us  [per_device(): piece = lax.ppermute(piece, 'row', turn)]
  transfers between devices with their start and end apart: 23 -> 22, of which waited for: 9 -> 8; matrix products, arithmetic and copies ran while one was open for 7% -> 6% of each run, Pallas kernels for 6% -> 8%
where the time goes in v5:
time: 143 us; the launch traced here: 142 us
  waiting for transfers between devices  59.7 us (42%)
  Pallas kernels  36.4 us (25%)
  starting transfers between devices  26.2 us (18%)
  blocking collectives  8.85 us (6%)
  other arithmetic  5.36 us (4%)
  local copies, waits for them, and re-layouts  4.77 us (3%)
    ppermute x6, waiting for transfers between devices, per_device(): parts.append(tuple((lax.ppermute(x, 'col', ring) for x in parts[-1])))  47.7 us
    pallas_call x1, Pallas kernels, front(): pl.pallas_call(functools.partial(front_kernel, ringed, plan), grid=(cols...  25.3 us
    ppermute x6, waiting for transfers between devices, per_device(): piece = lax.ppermute(piece, 'row', turn)  11.9 us
    all_to_all x1, blocking collectives, exchange_tiles(): got = lax.all_to_all(send, 'row', split_axis=0, concat_axis=0, tiled=True)  8.85 us
    ppermute x6, starting transfers between devices, per_device(): parts.append(tuple((lax.ppermute(x, 'col', ring) for x in parts[-1])))  8.8 us
    pallas_call x1, Pallas kernels, own_factor(): pl.pallas_call(functools.partial(own_kernel, ringed, plan, rows_step), ou...  8.1 us
    ppermute x6, starting transfers between devices, per_device(): piece = lax.ppermute(piece, 'row', turn)  6.08 us
    all_to_all x1, starting transfers between devices, per_device(): lax.all_to_all(panel.reshape(4, quarter, part), 'row', split_axis=0, conc...  5.18 us
  transfers between devices with their start and end apart: 22, of which 8 were waited for; matrix products, arithmetic and copies ran while one was open for 6% of the time, Pallas kernels for 8%

profile of v5, /device:TPU:0, one launch (start us, length us, event | category | flops | bytes accessed | tf_op | source)
XLA Modules:
  0.0 142.1 jit_solution(9849824937214579271)
XLA Ops:
  0.6 5.2 %all-to-all-start = ((f32[4,384,128]{2,1,0:T(8,128)}), f32[4,384,128]{2,1,0:T(8,128)}, u32[]{:S(2)}, u32[]{:S(2)}) async-start(f32[4,384,128]{2,1,0:T(8,128)} %bitcast.22), calls=%async_computation | async-start | bytes 1572864 | tf_op jit(solution)/shard_map/all_to_all | solution.py:276
  5.8 1.2 fusion.7
  7.0 2.1 %collective-permute-start = (f32[768,128]{1,0:T(8,128)S(1)}, f32[768,128]{1,0:T(8,128)S(1)}, u32[]{:S(2)}, u32[]{:S(2)}) collective-permute-start(f32[768,128]{1,0:T(8,128)S(1)} %get-tuple-element.31), channel_id=1, source_target_pairs={{0,1},{1,3},{3,2},{2,0},{4,5},{5,7},{7,6},{6,4},{8,9},{9,11},{11,1... | collective-permute-start | bytes 1179656 | tf_op jit(solution)/shard_map/ppermute | solution.py:274
  9.1 0.9 convert_reduce_fusion.1
  12.2 1.5 %scatter_fusion = f32[16,8,128]{2,1,0:T(8,128)S(1)} fusion(f32[16,8,128]{2,1,0:T(8,128)S(1)} %broadcast_in_dim.18, s32[12]{0:T(128)S(1)} %fusion.6, f32[12,8,128]{2,1,0:T(8,128)} %bitcast.25), kind=kCustom, calls=%fused_computation | custom fusion | bytes 147504 | tf_op jit(solution)/shard_map/scatter | solution.py:223
  13.8 5.5 %collective-permute-done.refs_1_ = f32[768,128]{1,0:T(8,128)S(1)} collective-permute-done((f32[768,128]{1,0:T(8,128)S(1)}, f32[768,128]{1,0:T(8,128)S(1)}, u32[]{:S(2)}, u32[]{:S(2)}) %collective-permute-start) | collective-permute-done | bytes 393248 | tf_op jit(solution)/shard_map/ppermute | solution.py:274
  19.2 8.9 %all_to_all.15 = f32[8,3,8,128]{3,2,1,0:T(8,128)S(1)} all-to-all(f32[8,3,8,128]{3,2,1,0:T(8,128)S(1)} %select_maximum_fusion), channel_id=1, replica_groups=mesh['row'=8,'col'=4] {'row'}, dimensions={0} | all-to-all | bytes 196608 | tf_op jit(solution)/shard_map/all_to_all | solution.py:231
  28.1 4.9 %all-to-all-start.2 = ((f32[4,384,128]{2,1,0:T(8,128)}), f32[4,384,128]{2,1,0:T(8,128)S(1)}, u32[]{:S(2)}, u32[]{:S(2)}) async-start(f32[4,384,128]{2,1,0:T(8,128)} %all-to-all-done), calls=%async_computation.2 | async-start | bytes 1572864 | tf_op jit(solution)/shard_map/all_to_all | solution.py:285
  33.0 2.0 %collective-permute-start.1 = (f32[768,128]{1,0:T(8,128)S(1)}, f32[768,128]{1,0:T(8,128)S(1)}, u32[]{:S(2)}, u32[]{:S(2)}) collective-permute-start(f32[768,128]{1,0:T(8,128)S(1)} %get-tuple-element.30), channel_id=1, source_target_pairs={{0,1},{1,3},{3,2},{2,0},{4,5},{5,7},{7,6},{6,4},{8,9},{9,11},{11,1... | collective-permute-start | bytes 1179656 | tf_op jit(solution)/shard_map/ppermute | solution.py:274
  35.0 2.4 %collective-permute-start.2 = (f32[768,128]{1,0:T(8,128)S(1)}, f32[768,128]{1,0:T(8,128)S(1)}, u32[]{:S(2)}, u32[]{:S(2)}) collective-permute-start(f32[768,128]{1,0:T(8,128)S(1)} %collective-permute-done.refs_1_), channel_id=1, source_target_pairs={{0,1},{1,3},{3,2},{2,0},{4,5},{5,7},{7,6},{6,4},{8,9},{9,11},{11,1... | collective-permute-start | bytes 1179656 | tf_op jit(solution)/shard_map/ppermute | solution.py:274
  38.0 24.3 %collective-permute-done.1.refs_2_ = f32[768,128]{1,0:T(8,128)S(1)} collective-permute-done((f32[768,128]{1,0:T(8,128)S(1)}, f32[768,128]{1,0:T(8,128)S(1)}, u32[]{:S(2)}, u32[]{:S(2)}) %collective-permute-start.1) | collective-permute-done | bytes 393248 | tf_op jit(solution)/shard_map/ppermute | solution.py:274
  62.4 8.3 %collective-permute-done.2.refs_3_ = f32[768,128]{1,0:T(8,128)S(1)} collective-permute-done((f32[768,128]{1,0:T(8,128)S(1)}, f32[768,128]{1,0:T(8,128)S(1)}, u32[]{:S(2)}, u32[]{:S(2)}) %collective-permute-start.2) | collective-permute-done | bytes 393248 | tf_op jit(solution)/shard_map/ppermute | solution.py:274
  70.8 0.9 copy-done
  71.7 3.0 %pair_factor.1 = (f32[256,384]{1,0:T(8,128)}, f32[256,384]{1,0:T(8,128)}) custom-call(f32[512,512]{1,0:T(8,128)} %d_ref.3, f32[4,384,128]{2,1,0:T(8,128)} %copy-done), custom_call_target="tpu_custom_call" | custom-call | flops 603979776 | bytes 1572864 | tf_op jit(solution)/shard_map/pair_factor/pallas_call | solution.py:112
  75.5 1.2 collective-permute-start.8
  78.1 2.3 %collective-permute-start.5 = (f32[768,128]{1,0:T(8,128)S(1)}, f32[768,128]{1,0:T(8,128)S(1)}, u32[]{:S(2)}, u32[]{:S(2)}) collective-permute-start(f32[768,128]{1,0:T(8,128)S(1)} %collective-permute-done.3.refs_4_), channel_id=1, source_target_pairs={{0,1},{1,3},{3,2},{2,0},{4,5},{5,7},{7,6},{6,4},{8,9},{9,11},{11,1... | collective-permute-start | bytes 1179656 | tf_op jit(solution)/shard_map/ppermute | solution.py:274
  80.4 3.7 %collective-permute-done.6.refs_2_ = f32[256,384]{1,0:T(8,128)S(1)} collective-permute-done((f32[256,384]{1,0:T(8,128)}, f32[256,384]{1,0:T(8,128)S(1)}, u32[]{:S(2)}, u32[]{:S(2)}) %collective-permute-start.6) | collective-permute-done | bytes 393248 | tf_op jit(solution)/shard_map/ppermute | solution.py:295
  85.0 1.2 collective-permute-start.9
  86.3 9.2 %collective-permute-done.5.refs_6_ = f32[768,128]{1,0:T(8,128)S(1)} collective-permute-done((f32[768,128]{1,0:T(8,128)S(1)}, f32[768,128]{1,0:T(8,128)S(1)}, u32[]{:S(2)}, u32[]{:S(2)}) %collective-permute-start.5) | collective-permute-done | bytes 393248 | tf_op jit(solution)/shard_map/ppermute | solution.py:274
  96.0 0.9 collective-permute-start.13
  96.8 1.2 collective-permute-start.18
  99.6 7.6 %collective-permute-done.13.refs_6_ = f32[256,384]{1,0:T(8,128)} collective-permute-done((f32[256,384]{1,0:T(8,128)S(1)}, f32[256,384]{1,0:T(8,128)}, u32[]{:S(2)}, u32[]{:S(2)}) %collective-permute-start.13) | collective-permute-done | bytes 393248 | tf_op jit(solution)/shard_map/ppermute | solution.py:295
  108.6 8.1 %own_factor.1 = (bf16[1536,1024]{1,0:T(8,128)(2,1)}, f32[1536,128]{1,0:T(8,128)}) custom-call(s32[2]{0:T(128)} %pad_add_fusion.1.place_ref, f32[512,512]{1,0:T(8,128)} %d_ref.3, f32[1536,128]{1,0:T(8,128)} %refs_0_.1, f32[768,128]{1,0:T(8,128)} %copy-done.2, f32[768,128]{1,0:T(8,128)} %copy-done.3, f32[768,128]{1,0:T(8,128)} %copy-done.4, ...), custom_call_target="tpu_custom_call" | custom-call | flops 2415919104 | bytes 7864320 | tf_op jit(solution)/shard_map/own_factor/pallas_call | solution.py:72
  116.8 25.3 %front.1 = f32[1536,3072]{1,0:T(8,128)} custom-call(s32[2]{0:T(128)} %pad_add_fusion.1.place_ref, s32[3,16]{1,0:T(4,128)} %multiply_reduce_fusion.entry_ref, s32[7]{0:T(128)} %convert_reduce_fusion.2.start_ref, f32[24,8,128]{2,1,0:T(8,128)} %bitcast.24, bf16[1536,1024]{1,0:T(8,128)(2,1)} %get-tuple-element.24.own_ref, f32[1536,3072]{1,0:T(8,128)} %trail_ref.1, ...), custom_call_target="tpu_custom_call" | custom-call | flops 14495514624 | bytes 44040192 | tf_op jit(solution)/shard_map/front/pallas_call | solution.py:189
  (90 shorter events, 9.6 us)
Async XLA Ops:
  0.6 18.6 %all-to-all-start = ((f32[4,384,128]{2,1,0:T(8,128)}), f32[4,384,128]{2,1,0:T(8,128)}, u32[]{:S(2)}, u32[]{:S(2)}) async-start(f32[4,384,128]{2,1,0:T(8,128)} %bitcast.22), calls=%async_computation | async-start | bytes 1572864 | tf_op jit(solution)/shard_map/all_to_all | solution.py:276
  7.0 12.3 %collective-permute-start = (f32[768,128]{1,0:T(8,128)S(1)}, f32[768,128]{1,0:T(8,128)S(1)}, u32[]{:S(2)}, u32[]{:S(2)}) collective-permute-start(f32[768,128]{1,0:T(8,128)S(1)} %get-tuple-element.31), channel_id=1, source_target_pairs={{0,1},{1,3},{3,2},{2,0},{4,5},{5,7},{7,6},{6,4},{8,9},{9,11},{11,1... | collective-permute-start | bytes 1179656 | tf_op jit(solution)/shard_map/ppermute | solution.py:274
  19.2 89.3 %copy-start.2 = (f32[768,128]{1,0:T(8,128)}, f32[768,128]{1,0:T(8,128)S(1)}, u32[]{:S(2)}) copy-start(f32[768,128]{1,0:T(8,128)S(1)} %collective-permute-done.refs_1_) | copy-start | bytes 1179652
  28.1 88.7 %copy-start.1 = (f32[8,3,8,128]{3,2,1,0:T(8,128)}, f32[8,3,8,128]{3,2,1,0:T(8,128)S(1)}, u32[]{:S(2)}) copy-start(f32[8,3,8,128]{3,2,1,0:T(8,128)S(1)} %all_to_all.15) | copy-start | bytes 294916
  28.1 42.7 %all-to-all-start.2 = ((f32[4,384,128]{2,1,0:T(8,128)}), f32[4,384,128]{2,1,0:T(8,128)S(1)}, u32[]{:S(2)}, u32[]{:S(2)}) async-start(f32[4,384,128]{2,1,0:T(8,128)} %all-to-all-done), calls=%async_computation.2 | async-start | bytes 1572864 | tf_op jit(solution)/shard_map/all_to_all | solution.py:285
  33.0 29.3 %collective-permute-start.1 = (f32[768,128]{1,0:T(8,128)S(1)}, f32[768,128]{1,0:T(8,128)S(1)}, u32[]{:S(2)}, u32[]{:S(2)}) collective-permute-start(f32[768,128]{1,0:T(8,128)S(1)} %get-tuple-element.30), channel_id=1, source_target_pairs={{0,1},{1,3},{3,2},{2,0},{4,5},{5,7},{7,6},{6,4},{8,9},{9,11},{11,1... | collective-permute-start | bytes 1179656 | tf_op jit(solution)/shard_map/ppermute | solution.py:274
  35.0 35.7 %collective-permute-start.2 = (f32[768,128]{1,0:T(8,128)S(1)}, f32[768,128]{1,0:T(8,128)S(1)}, u32[]{:S(2)}, u32[]{:S(2)}) collective-permute-start(f32[768,128]{1,0:T(8,128)S(1)} %collective-permute-done.refs_1_), channel_id=1, source_target_pairs={{0,1},{1,3},{3,2},{2,0},{4,5},{5,7},{7,6},{6,4},{8,9},{9,11},{11,1... | collective-permute-start | bytes 1179656 | tf_op jit(solution)/shard_map/ppermute | solution.py:274
  62.3 15.8 %collective-permute-start.3 = (f32[768,128]{1,0:T(8,128)S(1)}, f32[768,128]{1,0:T(8,128)S(1)}, u32[]{:S(2)}, u32[]{:S(2)}) collective-permute-start(f32[768,128]{1,0:T(8,128)S(1)} %collective-permute-done.1.refs_2_), channel_id=1, source_target_pairs={{0,1},{1,3},{3,2},{2,0},{4,5},{5,7},{7,6},{6,4},{8,9},{9,11},{11,1... | collective-permute-start | bytes 1179656 | tf_op jit(solution)/shard_map/ppermute | solution.py:274
  74.7 9.5 %collective-permute-start.6 = (f32[256,384]{1,0:T(8,128)}, f32[256,384]{1,0:T(8,128)S(1)}, u32[]{:S(2)}, u32[]{:S(2)}) collective-permute-start(f32[256,384]{1,0:T(8,128)} %get-tuple-element.20.refs_0_), channel_id=1, source_target_pairs={{0,8},{4,12},{8,24},{12,28},{16,0},{20,4},{24,16},{28,20},{1,9},{5... | collective-permute-start | bytes 1179656 | tf_op jit(solution)/shard_map/ppermute | solution.py:295
  75.5 9.5 %collective-permute-start.8 = (f32[256,384]{1,0:T(8,128)}, f32[256,384]{1,0:T(8,128)S(1)}, u32[]{:S(2)}, u32[]{:S(2)}) collective-permute-start(f32[256,384]{1,0:T(8,128)} %get-tuple-element.21.refs_8_), channel_id=1, source_target_pairs={{0,16},{4,20},{8,0},{12,4},{16,24},{20,28},{24,8},{28,12},{1,17},{... | collective-permute-start | bytes 1179656 | tf_op jit(solution)/shard_map/ppermute | solution.py:295
  77.7 17.8 %collective-permute-start.4 = (f32[768,128]{1,0:T(8,128)S(1)}, f32[768,128]{1,0:T(8,128)S(1)}, u32[]{:S(2)}, u32[]{:S(2)}) collective-permute-start(f32[768,128]{1,0:T(8,128)S(1)} %collective-permute-done.2.refs_3_), channel_id=1, source_target_pairs={{0,1},{1,3},{3,2},{2,0},{4,5},{5,7},{7,6},{6,4},{8,9},{9,11},{11,1... | collective-permute-start | bytes 1179656 | tf_op jit(solution)/shard_map/ppermute | solution.py:274
  78.1 17.3 %collective-permute-start.5 = (f32[768,128]{1,0:T(8,128)S(1)}, f32[768,128]{1,0:T(8,128)S(1)}, u32[]{:S(2)}, u32[]{:S(2)}) collective-permute-start(f32[768,128]{1,0:T(8,128)S(1)} %collective-permute-done.3.refs_4_), channel_id=1, source_target_pairs={{0,1},{1,3},{3,2},{2,0},{4,5},{5,7},{7,6},{6,4},{8,9},{9,11},{11,1... | collective-permute-start | bytes 1179656 | tf_op jit(solution)/shard_map/ppermute | solution.py:274
  84.1 11.8 %collective-permute-start.7 = (f32[256,384]{1,0:T(8,128)S(1)}, f32[256,384]{1,0:T(8,128)S(1)}, u32[]{:S(2)}, u32[]{:S(2)}) collective-permute-start(f32[256,384]{1,0:T(8,128)S(1)} %collective-permute-done.6.refs_2_), channel_id=1, source_target_pairs={{0,8},{4,12},{8,24},{12,28},{16,0},{20,4},{24,16},{28,20},{1,9},{5... | collective-permute-start | bytes 1179656 | tf_op jit(solution)/shard_map/ppermute | solution.py:295
  85.0 11.9 %collective-permute-start.9 = (f32[256,384]{1,0:T(8,128)S(1)}, f32[256,384]{1,0:T(8,128)S(1)}, u32[]{:S(2)}, u32[]{:S(2)}) collective-permute-start(f32[256,384]{1,0:T(8,128)S(1)} %collective-permute-done.8.refs_10_), channel_id=1, source_target_pairs={{0,16},{4,20},{8,0},{12,4},{16,24},{20,28},{24,8},{28,12},{1,17},{... | collective-permute-start | bytes 1179656 | tf_op jit(solution)/shard_map/ppermute | solution.py:295
  86.2 12.7 %collective-permute-start.10 = (f32[256,384]{1,0:T(8,128)}, f32[256,384]{1,0:T(8,128)S(1)}, u32[]{:S(2)}, u32[]{:S(2)}) collective-permute-start(f32[256,384]{1,0:T(8,128)} %get-tuple-element.20.refs_0_), channel_id=1, source_target_pairs={{0,4},{4,0},{8,12},{12,8},{16,20},{20,16},{24,28},{28,24},{1,5},{5... | collective-permute-start | bytes 1179656 | tf_op jit(solution)/shard_map/ppermute | solution.py:299
  95.5 3.6 %collective-permute-start.15 = (f32[256,384]{1,0:T(8,128)}, f32[256,384]{1,0:T(8,128)S(1)}, u32[]{:S(2)}, u32[]{:S(2)}) collective-permute-start(f32[256,384]{1,0:T(8,128)} %get-tuple-element.21.refs_8_), channel_id=1, source_target_pairs={{0,4},{4,0},{8,12},{12,8},{16,20},{20,16},{24,28},{28,24},{1,5},{5... | collective-permute-start | bytes 1179656 | tf_op jit(solution)/shard_map/ppermute | solution.py:299
  95.5 4.0 %collective-permute-start.11 = (f32[256,384]{1,0:T(8,128)S(1)}, f32[256,384]{1,0:T(8,128)S(1)}, u32[]{:S(2)}, u32[]{:S(2)}) collective-permute-start(f32[256,384]{1,0:T(8,128)S(1)} %collective-permute-done.6.refs_2_), channel_id=1, source_target_pairs={{0,4},{4,0},{8,12},{12,8},{16,20},{20,16},{24,28},{28,24},{1,5},{5... | collective-permute-start | bytes 1179656 | tf_op jit(solution)/shard_map/ppermute | solution.py:299
  96.0 11.2 %collective-permute-start.13 = (f32[256,384]{1,0:T(8,128)S(1)}, f32[256,384]{1,0:T(8,128)}, u32[]{:S(2)}, u32[]{:S(2)}) collective-permute-start(f32[256,384]{1,0:T(8,128)S(1)} %collective-permute-done.7.refs_4_), channel_id=1, source_target_pairs={{0,8},{4,12},{8,24},{12,28},{16,0},{20,4},{24,16},{28,20},{1,9},{5... | collective-permute-start | bytes 1179656 | tf_op jit(solution)/shard_map/ppermute | solution.py:295
  96.8 10.9 %collective-permute-start.18 = (f32[256,384]{1,0:T(8,128)S(1)}, f32[256,384]{1,0:T(8,128)}, u32[]{:S(2)}, u32[]{:S(2)}) collective-permute-start(f32[256,384]{1,0:T(8,128)S(1)} %collective-permute-done.9.refs_12_), channel_id=1, source_target_pairs={{0,16},{4,20},{8,0},{12,4},{16,24},{20,28},{24,8},{28,12},{1,17},{... | collective-permute-start | bytes 1179656 | tf_op jit(solution)/shard_map/ppermute | solution.py:295
  98.9 17.7 %collective-permute-start.16 = (f32[256,384]{1,0:T(8,128)S(1)}, f32[256,384]{1,0:T(8,128)}, u32[]{:S(2)}, u32[]{:S(2)}) collective-permute-start(f32[256,384]{1,0:T(8,128)S(1)} %collective-permute-done.8.refs_10_), channel_id=1, source_target_pairs={{0,4},{4,0},{8,12},{12,8},{16,20},{20,16},{24,28},{28,24},{1,5},{5... | collective-permute-start | bytes 1179656 | tf_op jit(solution)/shard_map/ppermute | solution.py:299
  99.0 17.7 %collective-permute-start.12 = (f32[256,384]{1,0:T(8,128)S(1)}, f32[256,384]{1,0:T(8,128)}, u32[]{:S(2)}, u32[]{:S(2)}) collective-permute-start(f32[256,384]{1,0:T(8,128)S(1)} %collective-permute-done.7.refs_4_), channel_id=1, source_target_pairs={{0,4},{4,0},{8,12},{12,8},{16,20},{20,16},{24,28},{28,24},{1,5},{5... | collective-permute-start | bytes 1179656 | tf_op jit(solution)/shard_map/ppermute | solution.py:299
  99.5 17.2 %collective-permute-start.17 = (f32[256,384]{1,0:T(8,128)S(1)}, f32[256,384]{1,0:T(8,128)}, u32[]{:S(2)}, u32[]{:S(2)}) collective-permute-start(f32[256,384]{1,0:T(8,128)S(1)} %collective-permute-done.9.refs_12_), channel_id=1, source_target_pairs={{0,4},{4,0},{8,12},{12,8},{16,20},{20,16},{24,28},{28,24},{1,5},{5... | collective-permute-start | bytes 1179656 | tf_op jit(solution)/shard_map/ppermute | solution.py:299
  107.2 9.5 %collective-permute-start.14 = (f32[256,384]{1,0:T(8,128)}, f32[256,384]{1,0:T(8,128)}, u32[]{:S(2)}, u32[]{:S(2)}) collective-permute-start(f32[256,384]{1,0:T(8,128)} %collective-permute-done.13.refs_6_), channel_id=1, source_target_pairs={{0,4},{4,0},{8,12},{12,8},{16,20},{20,16},{24,28},{28,24},{1,5},{5... | collective-permute-start | bytes 1179656 | tf_op jit(solution)/shard_map/ppermute | solution.py:299
  107.8 9.0 %collective-permute-start.19 = (f32[256,384]{1,0:T(8,128)}, f32[256,384]{1,0:T(8,128)}, u32[]{:S(2)}, u32[]{:S(2)}) collective-permute-start(f32[256,384]{1,0:T(8,128)} %collective-permute-done.18.refs_14_), channel_id=1, source_target_pairs={{0,4},{4,0},{8,12},{12,8},{16,20},{20,16},{24,28},{28,24},{1,5},{5... | collective-permute-start | bytes 1179656 | tf_op jit(solution)/shard_map/ppermute | solution.py:299
  (13 other events, 299.5 us)

commit v6 on v5

--- a/solution.py
+++ b/solution.py
@@ -26,70 +26,6 @@
 def ring_place(index, steps):
     at = (index ^ (index >> 1)) - steps & 3
     return at ^ (at >> 1)
-
-
-def own_kernel(ringed, plan, rows_step, place_ref, d_ref, *refs):
-    pieces = refs[: len(plan)]
-    halves_ref, block_ref, stage, dtcat, full_ref, sem = refs[len(plan) :]
-    width = d_ref.shape[0]
-    part = stage.shape[1] // 4
-    todo = []
-    for n, (s, row, rows) in enumerate(plan):
-        source = ring_place(place_ref[1], s) if ringed else s
-        lanes = pl.ds(pl.multiple_of(source * part, part), part)
-        todo.append(
-            pltpu.make_async_copy(pieces[n], stage.at[pl.ds(row, rows), lanes], sem.at[n])
-        )
-    for c in todo:
-        c.start()
-    hi, lo = split(d_ref[...].T)
-    dtcat[0:width, :] = hi
-    dtcat[width : 2 * width, :] = hi
-    dtcat[2 * width :, :] = lo
-    for c in todo:
-        c.wait()
-    mine = pl.ds(pl.multiple_of(place_ref[1] * part, part), part)
-
-    def body(n, carry):
-        at = pl.ds(pl.multiple_of(n * rows_step, rows_step), rows_step)
-        hi, lo = split(stage[at, :])
-        lhs = jnp.concatenate([hi, lo, hi], axis=1)
-        full = lax.dot_general(lhs, dtcat[...], NN, preferred_element_type=jnp.float32)
-        full_ref[...] = full
-        block_ref[at, :] = full_ref[:, mine]
-        hi, lo = split(full)
-        halves_ref[at, 0:width] = hi
-        halves_ref[at, width:] = lo
-        return carry
-
-    lax.fori_loop(0, stage.shape[0] // rows_step, body, 0)
-
-
-def own_factor(place, d, pieces, plan, ringed, rows, rows_step):
-    width = d.shape[0]
-    part = width // 4
-    whole = pl.BlockSpec(memory_space=pltpu.VMEM)
-    return pl.pallas_call(
-        functools.partial(own_kernel, ringed, plan, rows_step),
-        out_shape=(
-            jax.ShapeDtypeStruct((rows, 2 * width), jnp.bfloat16),
-            jax.ShapeDtypeStruct((rows, part), jnp.float32),
-        ),
-        in_specs=[pl.BlockSpec(memory_space=pltpu.SMEM), whole]
-        + [pl.BlockSpec(memory_space=pl.ANY)] * len(pieces),
-        out_specs=(whole, whole),
-        scratch_shapes=[
-            pltpu.VMEM((rows, width), jnp.float32),
-            pltpu.VMEM((3 * width, width), jnp.bfloat16),
-            pltpu.VMEM((rows_step, width), jnp.float32),
-            pltpu.SemaphoreType.DMA((len(pieces),)),
-        ],
-        compiler_params=pltpu.CompilerParams(vmem_limit_bytes=VMEM_LIMIT),
-        cost_estimate=pl.CostEstimate(
-            flops=6 * rows * width * width, bytes_accessed=10 * rows * width, transcendentals=0
-        ),
-        name="own_factor",
-    )(place, d, *pieces)
 
 
 def pair_kernel(d_ref, panel_ref, top_ref, low_ref):
@@ -127,31 +63,63 @@
 
 
 def front_kernel(
-    ringed, plan, place_ref, entry_ref, start_ref, agg_ref, own_ref, trail_ref, *refs
+    ringed, own_plan, plan, place_ref, entry_ref, start_ref, d_ref, agg_ref, trail_ref, *refs
 ):
-    pieces = refs[: len(plan)]
-    out_ref, stage, pair_cat, sem = refs[len(plan) :]
+    n_own, n_pair = len(own_plan), len(plan)
+    own_pieces, pieces = refs[:n_own], refs[n_own : n_own + n_pair]
+    out_ref, block_ref = refs[n_own + n_pair : n_own + n_pair + 2]
+    own_stage, stage, dt_left, dt_right, own_cat, pair_cat, full, sem = refs[n_own + n_pair + 2 :]
     j, i = pl.program_id(0), pl.program_id(1)
     n_i = pl.num_programs(1)
     bm, bn = out_ref.shape
-    width = stage.shape[0]
+    width = d_ref.shape[0]
+    half = width // 2
+    part = width // 4
 
     @pl.when((i == 0) & (j == 0))
     def _():
         todo = []
-        for n, (half, steps, swap) in enumerate(plan):
+        for n, s in enumerate(own_plan):
+            source = ring_place(place_ref[1], s) if ringed else s
+            lanes = pl.ds(pl.multiple_of(source * part, part), part)
+            todo.append(pltpu.make_async_copy(own_pieces[n], own_stage.at[:, lanes], sem.at[n]))
+        for n, (upper, steps, swap) in enumerate(plan):
             depth, cols = pieces[n].shape
             block = 0
             if ringed:
                 chip = ring_place(place_ref[0] // 2, steps)
                 block = (place_ref[0] % 2 ^ swap) * 4 + chip
             at = pl.ds(pl.multiple_of(block * cols, TILE_COLS), cols)
-            rows = pl.ds(half * depth, depth)
-            todo.append(pltpu.make_async_copy(pieces[n], stage.at[rows, at], sem.at[n]))
+            rows = pl.ds(upper * depth, depth)
+            todo.append(
+                pltpu.make_async_copy(pieces[n], stage.at[rows, at], sem.at[n_own + n])
+            )
         for c in todo:
             c.start()
+        hi, lo = split(d_ref[...].T)
+        dt_left[...] = jnp.concatenate(
+            [hi[:half, :half], hi[:half, :half], lo[:half, :half]], axis=0
+        )
+        dt_right[...] = jnp.concatenate([hi[:, half:], hi[:, half:], lo[:, half:]], axis=0)
         for c in todo:
             c.wait()
+
+    rows = pl.ds(pl.multiple_of(i * bm, bm), bm)
+
+    @pl.when(j == 0)
+    def _():
+        hi, lo = split(own_stage[rows, :])
+        lhs = jnp.concatenate([hi[:, :half], lo[:, :half], hi[:, :half]], axis=1)
+        full[:, :half] = lax.dot_general(
+            lhs, dt_left[...], NN, preferred_element_type=jnp.float32
+        )
+        lhs = jnp.concatenate([hi, lo, hi], axis=1)
+        full[:, half:] = lax.dot_general(
+            lhs, dt_right[...], NN, preferred_element_type=jnp.float32
+        )
+        block_ref[...] = full[:, pl.ds(pl.multiple_of(place_ref[1] * part, part), part)]
+        hi, lo = split(full[...])
+        own_cat[rows, :] = jnp.concatenate([hi, hi, lo], axis=1)
 
     @pl.when(i == 0)
     def _():
@@ -161,12 +129,11 @@
         pair_cat[width : 2 * width, :] = lo
         pair_cat[2 * width :, :] = hi
 
-    rows = pl.ds(pl.multiple_of(i * bm, bm), bm)
-    hi, lo = own_ref[rows, 0:width], own_ref[rows, width:]
-    lhs = jnp.concatenate([hi, hi, lo], axis=1)
     for n in range(0, bn, 256):
         at = slice(n, n + 256)
-        product = lax.dot_general(lhs, pair_cat[:, at], NN, preferred_element_type=jnp.float32)
+        product = lax.dot_general(
+            own_cat[rows, :], pair_cat[:, at], NN, preferred_element_type=jnp.float32
+        )
         out_ref[:, at] = trail_ref[:, at] - product
     step = j * n_i + i
 
@@ -180,32 +147,46 @@
     lax.fori_loop(start_ref[step], start_ref[step + 1], add, 0)
 
 
-def front(place, entries, starts, agg, own, trailing, pieces, plan, ringed, bm, bn):
+def front(place, entries, starts, d, agg, trailing, own, own_plan, pieces, plan, ringed, bm, bn):
     rows, cols = trailing.shape
-    width = own.shape[1] // 2
+    width = d.shape[0]
+    half, part = width // 2, width // 4
+    n_i = rows // bm
     whole = pl.BlockSpec(memory_space=pltpu.VMEM)
     smem = pl.BlockSpec(memory_space=pltpu.SMEM)
     block = pl.BlockSpec((bm, bn), lambda j, i: (i, j))
+    operands = len(own) + len(pieces)
     return pl.pallas_call(
-        functools.partial(front_kernel, ringed, plan),
-        grid=(cols // bn, rows // bm),
-        out_shape=jax.ShapeDtypeStruct((rows, cols), jnp.float32),
+        functools.partial(front_kernel, ringed, own_plan, plan),
+        grid=(cols // bn, n_i),
+        out_shape=(
+            jax.ShapeDtypeStruct((rows, cols), jnp.float32),
+            jax.ShapeDtypeStruct((rows, part), jnp.float32),
+        ),
         in_specs=[smem, smem, smem, whole, whole, block]
-        + [pl.BlockSpec(memory_space=pl.ANY)] * len(pieces),
-        out_specs=block,
+        + [pl.BlockSpec(memory_space=pl.ANY)] * operands,
+        out_specs=(
+            block,
+            pl.BlockSpec((bm, part), lambda j, i: (jnp.where(j == 0, i, n_i - 1), 0)),
+        ),
         scratch_shapes=[
+            pltpu.VMEM((rows, width), jnp.float32),
             pltpu.VMEM((width, cols), jnp.float32),
+            pltpu.VMEM((3 * half, half), jnp.bfloat16),
+            pltpu.VMEM((3 * width, half), jnp.bfloat16),
+            pltpu.VMEM((rows, 3 * width), jnp.bfloat16),
             pltpu.VMEM((3 * width, bn), jnp.bfloat16),
-            pltpu.SemaphoreType.DMA((len(pieces),)),
+            pltpu.VMEM((bm, width), jnp.float32),
+            pltpu.SemaphoreType.DMA((operands,)),
         ],
         compiler_params=pltpu.CompilerParams(vmem_limit_bytes=VMEM_LIMIT),
         cost_estimate=pl.CostEstimate(
-            flops=6 * rows * width * cols,
+            flops=6 * rows * width * (cols + width),
             bytes_accessed=8 * rows * cols + 4 * width * cols,
             transcendentals=0,
         ),
         name="front",
-    )(place, entries, starts, agg, own, trailing, *pieces)
+    )(place, entries, starts, d, agg, trailing, *own, *pieces)
 
 
 def pack_tiles(agg_vals, agg_dest, agg_tile, tiles_dev):
@@ -267,12 +248,8 @@
     tiles = pack_tiles(agg_vals, agg_dest, agg_tile, tiles_dev)
     ringed = row_devices == 8 and col_devices == 4
     if ringed:
-        half = local_rows // 2
-        ring = list(NEXT.items())
-        parts = [(panel[:half], panel[half:])]
-        for _ in range(3):
-            parts.append(tuple(lax.ppermute(x, "col", ring) for x in parts[-1]))
         quarter = local_rows // 4
+        ring = functools.partial(lax.ppermute, axis_name="col", perm=list(NEXT.items()))
         spread = lax.all_to_all(
             panel.reshape(4, quarter, part),
             "row",
@@ -281,11 +258,12 @@
             axis_index_groups=[[0, 2, 4, 6], [1, 3, 5, 7]],
             tiled=True,
         )
-        spread, first, tiles = lax.optimization_barrier((spread, parts[1][0], tiles))
+        spread, first, tiles = lax.optimization_barrier((spread, ring(panel), tiles))
         wanted = lax.all_to_all(spread, "col", split_axis=0, concat_axis=0, tiled=True)
-        wanted, second = lax.optimization_barrier((wanted, parts[2][0]))
+        wanted, first, tiles = lax.optimization_barrier((wanted, first, tiles))
+        second = ring(first)
         siblings = [(p, p ^ 1) for p in range(row_devices)]
-        pieces, plan, across = [], [], []
+        pieces, plan = [], []
         turns = ((NEXT, 1), (PREV, -1))
         for h, piece in enumerate(pair_factor(diag_inverse, wanted, quarter)):
             step, sign = turns[h]
@@ -293,15 +271,9 @@
             for n in range(4):
                 if n > 0:
                     piece = lax.ppermute(piece, "row", turn)
-                if n == 2:
-                    across.append(piece)
                 plan += [(h, sign * n, 0), (h, sign * n, 1)]
                 pieces += [piece, lax.ppermute(piece, "row", siblings)]
-        last, across = lax.optimization_barrier((parts[3], tuple(across)))
-        pieces[4], pieces[12] = across
-        own = [panel, first, parts[1][1], second, parts[2][1], *last]
-        own_plan = [(0, 0, local_rows)]
-        own_plan += [(s, r * half, half) for s in range(1, 4) for r in range(2)]
+        own = [panel, first, second, ring(second)]
     else:
         whole = lax.all_gather(panel, "col", axis=0)
         column = lax.all_gather(panel, "row", axis=0, tiled=True)
@@ -309,20 +281,26 @@
         partner = lax.all_to_all(column, "col", split_axis=0, concat_axis=0, tiled=True)
         pieces, plan = pair_factor(diag_inverse, partner, 768), [(0, 0, 0), (1, 0, 0)]
         own = [whole[s] for s in range(col_devices)]
-        own_plan = [(s, 0, local_rows) for s in range(col_devices)]
 
     agg, landing = exchange_tiles(tiles, tiles_dev)
     entries, starts = order_tiles(
         landing, row_devices * CAP, tiles_dev, tile_cols, bm, bn, n_i, n_j
     )
-    rows_step = 512 if local_rows % 512 == 0 else local_rows
-    halves, own_block = own_factor(
-        place, diag_inverse, own, own_plan, ringed, local_rows, rows_step
+    return front(
+        place,
+        entries,
+        starts,
+        diag_inverse,
+        agg,
+        trailing,
+        own,
+        list(range(4)),
+        pieces,
+        plan,
+        ringed,
+        bm,
+        bn,
     )
-    updated = front(
-        place, entries, starts, agg, halves, trailing, pieces, plan, ringed, bm, bn
-    )
-    return updated, own_block
 
 
 def solution(mesh):

time: 143 us -> 123 us (0.86)
  waiting for transfers between devices: 59.7 us -> 38 us
  blocking collectives: 8.85 us -> 24 us
  starting transfers between devices: 26.2 us -> 19.2 us
  Pallas kernels: 36.4 us -> 30.7 us
    ppermute x6 -> x3, waiting for transfers between devices: 47.7 us -> 11.6 us  [the longest x1 7.16 us: per_device(): own = [panel, first, second, ring(second)]]
    all_to_all x1, blocking collectives: 8.85 us -> 24 us  [per_device(): lax.all_to_all(spread, 'col', split_axis=0, concat_axis=0, tiled=True)]
    pallas_call x2 -> x1, Pallas kernels: 33.4 us -> 27.7 us  [front(): pl.pallas_call(functools.partial(front_kernel, ringed, own_plan, plan), g...]
    all_to_all x1, waiting for transfers between devices: 0.01 us -> 5.28 us  [per_device(): lax.all_to_all(panel.reshape(4, quarter, part), 'row', split_axis=0, conc...]
    all_to_all x1, waiting for transfers between devices: 0.01 us -> 4.85 us  [exchange_tiles(): got = lax.all_to_all(send, 'row', split_axis=0, concat_axis=0, tiled=True)]
    ppermute x6 -> x3, starting transfers between devices: 8.8 us -> 4.05 us  [the longest x1 3.08 us: per_device(): ring(panel)]
    ppermute x6, waiting for transfers between devices: 11.9 us -> 15 us  [per_device(): piece = lax.ppermute(piece, 'row', turn)]
    all_to_all x1, starting transfers between devices: 5.18 us -> 3.72 us  [per_device(): lax.all_to_all(panel.reshape(4, quarter, part), 'row', split_axis=0, conc...]
  transfers between devices with their start and end apart: 22 -> 19, of which waited for: 8 -> 8; matrix products, arithmetic and copies ran while one was open for 6% -> 7% of each run, Pallas kernels for 8% -> 0%
where the time goes in v6:
time: 123 us; the launch traced here: 122 us
  waiting for transfers between devices  38 us (31%)
  Pallas kernels  30.7 us (25%)
  blocking collectives  24 us (20%)
  starting transfers between devices  19.2 us (16%)
  other arithmetic  5.99 us (5%)
  local copies, waits for them, and re-layouts  3.49 us (3%)
    pallas_call x1, Pallas kernels, front(): pl.pallas_call(functools.partial(front_kernel, ringed, own_plan, plan), g...  27.7 us
    all_to_all x1, blocking collectives, per_device(): lax.all_to_all(spread, 'col', split_axis=0, concat_axis=0, tiled=True)  24 us
    ppermute x6, waiting for transfers between devices, per_device(): piece = lax.ppermute(piece, 'row', turn)  15 us
    ppermute x1, waiting for transfers between devices, per_device(): own = [panel, first, second, ring(second)]  7.16 us
    ppermute x6, starting transfers between devices, per_device(): piece = lax.ppermute(piece, 'row', turn)  6.13 us
    all_to_all x1, waiting for transfers between devices, per_device(): lax.all_to_all(panel.reshape(4, quarter, part), 'row', split_axis=0, conc...  5.28 us
    all_to_all x1, waiting for transfers between devices, exchange_tiles(): got = lax.all_to_all(send, 'row', split_axis=0, concat_axis=0, tiled=True)  4.85 us
    ppermute x1, waiting for transfers between devices, per_device(): ring(panel)  4.47 us
  transfers between devices with their start and end apart: 19, of which 8 were waited for; matrix products, arithmetic and copies ran while one was open for 7% of the time, Pallas kernels for 0%

profile of v6, /device:TPU:0, one launch (start us, length us, event | category | flops | bytes accessed | tf_op | source)
XLA Modules:
  0.0 122.2 jit_solution(12081408738306486389)
XLA Ops:
  0.6 3.1 %collective-permute-start = (f32[1536,128]{1,0:T(8,128)}, f32[1536,128]{1,0:T(8,128)S(1)}, u32[]{:S(2)}, u32[]{:S(2)}) collective-permute-start(f32[1536,128]{1,0:T(8,128)} %refs_0_.1), channel_id=1, source_target_pairs={{0,1},{1,3},{3,2},{2,0},{4,5},{5,7},{7,6},{6,4},{8,9},{9,11},{11,1... | collective-permute-start | bytes 2359304 | tf_op jit(solution)/shard_map/ppermute | solution.py:261
  3.7 3.7 %all-to-all-start = ((f32[4,384,128]{2,1,0:T(8,128)}), f32[4,384,128]{2,1,0:T(8,128)S(1)}, u32[]{:S(2)}, u32[]{:S(2)}) async-start(f32[4,384,128]{2,1,0:T(8,128)} %bitcast.22), calls=%async_computation | async-start | bytes 1572864 | tf_op jit(solution)/shard_map/all_to_all | solution.py:253
  7.4 0.9 convert_reduce_fusion.1
  9.9 0.7 fusion.6
  10.5 1.5 %scatter_fusion = f32[16,8,128]{2,1,0:T(8,128)S(1)} fusion(f32[16,8,128]{2,1,0:T(8,128)S(1)} %broadcast_in_dim.18, s32[12]{0:T(128)S(1)} %fusion.6, f32[12,8,128]{2,1,0:T(8,128)} %bitcast.25), kind=kCustom, calls=%fused_computation | custom fusion | bytes 147504 | tf_op jit(solution)/shard_map/scatter | solution.py:204
  12.7 5.3 %all-to-all-done = f32[4,384,128]{2,1,0:T(8,128)S(1)} async-done(((f32[4,384,128]{2,1,0:T(8,128)}), f32[4,384,128]{2,1,0:T(8,128)S(1)}, u32[]{:S(2)}, u32[]{:S(2)}) %all-to-all-start) | async-done | bytes 786464 | tf_op jit(solution)/shard_map/all_to_all | solution.py:253
  18.0 4.5 %collective-permute-done.refs_1_ = f32[1536,128]{1,0:T(8,128)S(1)} collective-permute-done((f32[1536,128]{1,0:T(8,128)}, f32[1536,128]{1,0:T(8,128)S(1)}, u32[]{:S(2)}, u32[]{:S(2)}) %collective-permute-start) | collective-permute-done | bytes 786464 | tf_op jit(solution)/shard_map/ppermute | solution.py:261
  22.5 24.0 %all_to_all.15.panel_ref = f32[4,384,128]{2,1,0:T(8,128)} all-to-all(f32[4,384,128]{2,1,0:T(8,128)S(1)} %all-to-all-done), channel_id=1, replica_groups=mesh['row'=8,'col'=4] {'col'}, dimensions={0} | all-to-all | bytes 1572864 | tf_op jit(solution)/shard_map/all_to_all | solution.py:262
  46.5 3.0 %pair_factor.1 = (f32[256,384]{1,0:T(8,128)}, f32[256,384]{1,0:T(8,128)}) custom-call(f32[512,512]{1,0:T(8,128)} %d_ref.3, f32[4,384,128]{2,1,0:T(8,128)} %all_to_all.15.panel_ref), custom_call_target="tpu_custom_call" | custom-call | flops 603979776 | bytes 1572864 | tf_op jit(solution)/shard_map/pair_factor/pallas_call | solution.py:48
  49.5 1.5 %collective-permute-start.4 = (f32[256,384]{1,0:T(8,128)}, f32[256,384]{1,0:T(8,128)S(1)}, u32[]{:S(2)}, u32[]{:S(2)}) collective-permute-start(f32[256,384]{1,0:T(8,128)} %get-tuple-element.16.refs_4_), channel_id=1, source_target_pairs={{0,8},{4,12},{8,24},{12,28},{16,0},{20,4},{24,16},{28,20},{1,9},{5... | collective-permute-start | bytes 1179656 | tf_op jit(solution)/shard_map/ppermute | solution.py:273
  51.8 3.7 %all-to-all-start.2 = ((f32[8,3,8,128]{3,2,1,0:T(8,128)}), f32[8,3,8,128]{3,2,1,0:T(8,128)S(1)}, u32[]{:S(2)}, u32[]{:S(2)}) async-start(f32[8,3,8,128]{3,2,1,0:T(8,128)} %select_maximum_fusion), calls=%async_computation.2 | async-start | bytes 196608 | tf_op jit(solution)/shard_map/all_to_all | solution.py:212
  56.6 4.9 %all-to-all-done.2 = f32[8,3,8,128]{3,2,1,0:T(8,128)S(1)} async-done(((f32[8,3,8,128]{3,2,1,0:T(8,128)}), f32[8,3,8,128]{3,2,1,0:T(8,128)S(1)}, u32[]{:S(2)}, u32[]{:S(2)}) %all-to-all-start.2) | async-done | bytes 98336 | tf_op jit(solution)/shard_map/all_to_all | solution.py:212
  61.6 1.7 %collective-permute-start.6 = (f32[256,384]{1,0:T(8,128)S(1)}, f32[256,384]{1,0:T(8,128)}, u32[]{:S(2)}, u32[]{:S(2)}) collective-permute-start(f32[256,384]{1,0:T(8,128)S(1)} %collective-permute-done.4.refs_6_), channel_id=1, source_target_pairs={{0,8},{4,12},{8,24},{12,28},{16,0},{20,4},{24,16},{28,20},{1,9},{5... | collective-permute-start | bytes 1179656 | tf_op jit(solution)/shard_map/ppermute | solution.py:273
  65.0 7.6 %collective-permute-done.6.refs_8_ = f32[256,384]{1,0:T(8,128)} collective-permute-done((f32[256,384]{1,0:T(8,128)S(1)}, f32[256,384]{1,0:T(8,128)}, u32[]{:S(2)}, u32[]{:S(2)}) %collective-permute-start.6) | collective-permute-done | bytes 393248 | tf_op jit(solution)/shard_map/ppermute | solution.py:273
  72.6 1.8 %collective-permute-start.8 = (f32[256,384]{1,0:T(8,128)}, f32[256,384]{1,0:T(8,128)}, u32[]{:S(2)}, u32[]{:S(2)}) collective-permute-start(f32[256,384]{1,0:T(8,128)} %collective-permute-done.6.refs_8_), channel_id=1, source_target_pairs={{0,8},{4,12},{8,24},{12,28},{16,0},{20,4},{24,16},{28,20},{1,9},{5... | collective-permute-start | bytes 1179656 | tf_op jit(solution)/shard_map/ppermute | solution.py:273
  74.7 0.8 collective-permute-start.2
  75.9 0.7 convert_reduce_fusion.2.start_ref
  77.1 5.8 %collective-permute-done.8.refs_10_ = f32[256,384]{1,0:T(8,128)} collective-permute-done((f32[256,384]{1,0:T(8,128)}, f32[256,384]{1,0:T(8,128)}, u32[]{:S(2)}, u32[]{:S(2)}) %collective-permute-start.8) | collective-permute-done | bytes 393248 | tf_op jit(solution)/shard_map/ppermute | solution.py:273
  82.9 1.7 %collective-permute-done.15.refs_18_ = f32[256,384]{1,0:T(8,128)} collective-permute-done((f32[256,384]{1,0:T(8,128)}, f32[256,384]{1,0:T(8,128)}, u32[]{:S(2)}, u32[]{:S(2)}) %collective-permute-start.15) | collective-permute-done | bytes 393248 | tf_op jit(solution)/shard_map/ppermute | solution.py:273
  84.6 0.7 multiply_reduce_fusion.entry_ref
  85.4 1.1 collective-permute-done.16.refs_19_
  86.5 7.2 %collective-permute-done.2.refs_3_ = f32[1536,128]{1,0:T(8,128)S(1)} collective-permute-done((f32[1536,128]{1,0:T(8,128)S(1)}, f32[1536,128]{1,0:T(8,128)S(1)}, u32[]{:S(2)}, u32[]{:S(2)}) %collective-permute-start.2) | collective-permute-done | bytes 786464 | tf_op jit(solution)/shard_map/ppermute | solution.py:276
  93.8 0.8 copy-done.3
  94.6 27.7 %front.1 = (f32[1536,3072]{1,0:T(8,128)}, f32[1536,128]{1,0:T(8,128)}) custom-call(s32[2]{0:T(128)} %pad_add_fusion.1.place_ref, s32[3,16]{1,0:T(4,128)} %multiply_reduce_fusion.entry_ref, s32[7]{0:T(128)} %convert_reduce_fusion.2.start_ref, f32[512,512]{1,0:T(8,128)} %d_ref.3, f32[24,8,128]{2,1,0:T(8,128)} %bitcast.24, f32[1536,3072]{1,0:T(8,128)} %trail_ref.1, ...), custom_call_target="tpu_custom_call" | custom-call | flops 16911433728 | bytes 44040192 | tf_op jit(solution)/shard_map/front/pallas_call | solution.py:159
  (74 shorter events, 7.2 us)
Async XLA Ops:
  0.6 21.8 %collective-permute-start = (f32[1536,128]{1,0:T(8,128)}, f32[1536,128]{1,0:T(8,128)S(1)}, u32[]{:S(2)}, u32[]{:S(2)}) collective-permute-start(f32[1536,128]{1,0:T(8,128)} %refs_0_.1), channel_id=1, source_target_pairs={{0,1},{1,3},{3,2},{2,0},{4,5},{5,7},{7,6},{6,4},{8,9},{9,11},{11,1... | collective-permute-start | bytes 2359304 | tf_op jit(solution)/shard_map/ppermute | solution.py:261
  3.7 14.3 %all-to-all-start = ((f32[4,384,128]{2,1,0:T(8,128)}), f32[4,384,128]{2,1,0:T(8,128)S(1)}, u32[]{:S(2)}, u32[]{:S(2)}) async-start(f32[4,384,128]{2,1,0:T(8,128)} %bitcast.22), calls=%async_computation | async-start | bytes 1572864 | tf_op jit(solution)/shard_map/all_to_all | solution.py:253
  22.5 71.2 %copy-start.1 = (f32[1536,128]{1,0:T(8,128)}, f32[1536,128]{1,0:T(8,128)S(1)}, u32[]{:S(2)}) copy-start(f32[1536,128]{1,0:T(8,128)S(1)} %collective-permute-done.refs_1_) | copy-start | bytes 2359300
  49.5 12.1 %collective-permute-start.4 = (f32[256,384]{1,0:T(8,128)}, f32[256,384]{1,0:T(8,128)S(1)}, u32[]{:S(2)}, u32[]{:S(2)}) collective-permute-start(f32[256,384]{1,0:T(8,128)} %get-tuple-element.16.refs_4_), channel_id=1, source_target_pairs={{0,8},{4,12},{8,24},{12,28},{16,0},{20,4},{24,16},{28,20},{1,9},{5... | collective-permute-start | bytes 1179656 | tf_op jit(solution)/shard_map/ppermute | solution.py:273
  51.0 12.3 %collective-permute-start.11 = (f32[256,384]{1,0:T(8,128)}, f32[256,384]{1,0:T(8,128)}, u32[]{:S(2)}, u32[]{:S(2)}) collective-permute-start(f32[256,384]{1,0:T(8,128)} %get-tuple-element.17.refs_12_), channel_id=1, source_target_pairs={{0,16},{4,20},{8,0},{12,4},{16,24},{20,28},{24,8},{28,12},{1,17},{... | collective-permute-start | bytes 1179656 | tf_op jit(solution)/shard_map/ppermute | solution.py:273
  51.5 23.1 %collective-permute-start.1 = (f32[1536,128]{1,0:T(8,128)S(1)}, f32[1536,128]{1,0:T(8,128)S(1)}, u32[]{:S(2)}, u32[]{:S(2)}) collective-permute-start(f32[1536,128]{1,0:T(8,128)S(1)} %collective-permute-done.refs_1_), channel_id=1, source_target_pairs={{0,1},{1,3},{3,2},{2,0},{4,5},{5,7},{7,6},{6,4},{8,9},{9,11},{11,1... | collective-permute-start | bytes 2359304 | tf_op jit(solution)/shard_map/ppermute | solution.py:264
  51.8 9.7 %all-to-all-start.2 = ((f32[8,3,8,128]{3,2,1,0:T(8,128)}), f32[8,3,8,128]{3,2,1,0:T(8,128)S(1)}, u32[]{:S(2)}, u32[]{:S(2)}) async-start(f32[8,3,8,128]{3,2,1,0:T(8,128)} %select_maximum_fusion), calls=%async_computation.2 | async-start | bytes 196608 | tf_op jit(solution)/shard_map/all_to_all | solution.py:212
  56.1 8.3 %collective-permute-start.3 = (f32[256,384]{1,0:T(8,128)}, f32[256,384]{1,0:T(8,128)S(1)}, u32[]{:S(2)}, u32[]{:S(2)}) collective-permute-start(f32[256,384]{1,0:T(8,128)} %get-tuple-element.16.refs_4_), channel_id=1, source_target_pairs={{0,4},{4,0},{8,12},{12,8},{16,20},{20,16},{24,28},{28,24},{1,5},{5... | collective-permute-start | bytes 1179656 | tf_op jit(solution)/shard_map/ppermute | solution.py:275
  56.6 7.9 %collective-permute-start.10 = (f32[256,384]{1,0:T(8,128)}, f32[256,384]{1,0:T(8,128)S(1)}, u32[]{:S(2)}, u32[]{:S(2)}) collective-permute-start(f32[256,384]{1,0:T(8,128)} %get-tuple-element.17.refs_12_), channel_id=1, source_target_pairs={{0,4},{4,0},{8,12},{12,8},{16,20},{20,16},{24,28},{28,24},{1,5},{5... | collective-permute-start | bytes 1179656 | tf_op jit(solution)/shard_map/ppermute | solution.py:275
  61.5 32.2 %copy-start = (f32[8,3,8,128]{3,2,1,0:T(8,128)}, f32[8,3,8,128]{3,2,1,0:T(8,128)S(1)}, u32[]{:S(2)}) copy-start(f32[8,3,8,128]{3,2,1,0:T(8,128)S(1)} %all-to-all-done.2) | copy-start | bytes 294916
  61.6 32.1 %copy-start.4 = (f32[256,384]{1,0:T(8,128)}, f32[256,384]{1,0:T(8,128)S(1)}, u32[]{:S(2)}) copy-start(f32[256,384]{1,0:T(8,128)S(1)} %collective-permute-done.4.refs_6_) | copy-start | bytes 1179652
  61.6 11.0 %collective-permute-start.6 = (f32[256,384]{1,0:T(8,128)S(1)}, f32[256,384]{1,0:T(8,128)}, u32[]{:S(2)}, u32[]{:S(2)}) collective-permute-start(f32[256,384]{1,0:T(8,128)S(1)} %collective-permute-done.4.refs_6_), channel_id=1, source_target_pairs={{0,8},{4,12},{8,24},{12,28},{16,0},{20,4},{24,16},{28,20},{1,9},{5... | collective-permute-start | bytes 1179656 | tf_op jit(solution)/shard_map/ppermute | solution.py:273
  63.3 11.1 %collective-permute-start.13 = (f32[256,384]{1,0:T(8,128)}, f32[256,384]{1,0:T(8,128)}, u32[]{:S(2)}, u32[]{:S(2)}) collective-permute-start(f32[256,384]{1,0:T(8,128)} %collective-permute-done.11.refs_14_), channel_id=1, source_target_pairs={{0,16},{4,20},{8,0},{12,4},{16,24},{20,28},{24,8},{28,12},{1,17},{... | collective-permute-start | bytes 1179656 | tf_op jit(solution)/shard_map/ppermute | solution.py:273
  64.4 10.2 %copy-start.5 = (f32[256,384]{1,0:T(8,128)}, f32[256,384]{1,0:T(8,128)S(1)}, u32[]{:S(2)}) copy-start(f32[256,384]{1,0:T(8,128)S(1)} %collective-permute-done.3.refs_5_) | copy-start | bytes 1179652
  64.5 12.1 %collective-permute-start.5 = (f32[256,384]{1,0:T(8,128)S(1)}, f32[256,384]{1,0:T(8,128)}, u32[]{:S(2)}, u32[]{:S(2)}) collective-permute-start(f32[256,384]{1,0:T(8,128)S(1)} %collective-permute-done.4.refs_6_), channel_id=1, source_target_pairs={{0,4},{4,0},{8,12},{12,8},{16,20},{20,16},{24,28},{28,24},{1,5},{5... | collective-permute-start | bytes 1179656 | tf_op jit(solution)/shard_map/ppermute | solution.py:275
  64.6 12.1 %collective-permute-start.12 = (f32[256,384]{1,0:T(8,128)}, f32[256,384]{1,0:T(8,128)}, u32[]{:S(2)}, u32[]{:S(2)}) collective-permute-start(f32[256,384]{1,0:T(8,128)} %collective-permute-done.11.refs_14_), channel_id=1, source_target_pairs={{0,4},{4,0},{8,12},{12,8},{16,20},{20,16},{24,28},{28,24},{1,5},{5... | collective-permute-start | bytes 1179656 | tf_op jit(solution)/shard_map/ppermute | solution.py:275
  72.6 10.3 %collective-permute-start.8 = (f32[256,384]{1,0:T(8,128)}, f32[256,384]{1,0:T(8,128)}, u32[]{:S(2)}, u32[]{:S(2)}) collective-permute-start(f32[256,384]{1,0:T(8,128)} %collective-permute-done.6.refs_8_), channel_id=1, source_target_pairs={{0,8},{4,12},{8,24},{12,28},{16,0},{20,4},{24,16},{28,20},{1,9},{5... | collective-permute-start | bytes 1179656 | tf_op jit(solution)/shard_map/ppermute | solution.py:273
  74.4 10.2 %collective-permute-start.15 = (f32[256,384]{1,0:T(8,128)}, f32[256,384]{1,0:T(8,128)}, u32[]{:S(2)}, u32[]{:S(2)}) collective-permute-start(f32[256,384]{1,0:T(8,128)} %collective-permute-done.13.refs_16_), channel_id=1, source_target_pairs={{0,16},{4,20},{8,0},{12,4},{16,24},{20,28},{24,8},{28,12},{1,17},{... | collective-permute-start | bytes 1179656 | tf_op jit(solution)/shard_map/ppermute | solution.py:273
  74.7 19.1 %copy-start.2 = (f32[1536,128]{1,0:T(8,128)}, f32[1536,128]{1,0:T(8,128)S(1)}, u32[]{:S(2)}) copy-start(f32[1536,128]{1,0:T(8,128)S(1)} %collective-permute-done.1.refs_2_) | copy-start | bytes 2359300
  74.7 19.0 %collective-permute-start.2 = (f32[1536,128]{1,0:T(8,128)S(1)}, f32[1536,128]{1,0:T(8,128)S(1)}, u32[]{:S(2)}, u32[]{:S(2)}) collective-permute-start(f32[1536,128]{1,0:T(8,128)S(1)} %collective-permute-done.1.refs_2_), channel_id=1, source_target_pairs={{0,1},{1,3},{3,2},{2,0},{4,5},{5,7},{7,6},{6,4},{8,9},{9,11},{11,1... | collective-permute-start | bytes 2359304 | tf_op jit(solution)/shard_map/ppermute | solution.py:276
  76.6 8.8 %collective-permute-start.7 = (f32[256,384]{1,0:T(8,128)}, f32[256,384]{1,0:T(8,128)S(1)}, u32[]{:S(2)}, u32[]{:S(2)}) collective-permute-start(f32[256,384]{1,0:T(8,128)} %collective-permute-done.6.refs_8_), channel_id=1, source_target_pairs={{0,4},{4,0},{8,12},{12,8},{16,20},{20,16},{24,28},{28,24},{1,5},{5... | collective-permute-start | bytes 1179656 | tf_op jit(solution)/shard_map/ppermute | solution.py:275
  76.7 8.7 %collective-permute-start.14 = (f32[256,384]{1,0:T(8,128)}, f32[256,384]{1,0:T(8,128)S(1)}, u32[]{:S(2)}, u32[]{:S(2)}) collective-permute-start(f32[256,384]{1,0:T(8,128)} %collective-permute-done.13.refs_16_), channel_id=1, source_target_pairs={{0,4},{4,0},{8,12},{12,8},{16,20},{20,16},{24,28},{28,24},{1,5},{5... | collective-permute-start | bytes 1179656 | tf_op jit(solution)/shard_map/ppermute | solution.py:275
  82.9 2.4 %collective-permute-start.9 = (f32[256,384]{1,0:T(8,128)}, f32[256,384]{1,0:T(8,128)S(1)}, u32[]{:S(2)}, u32[]{:S(2)}) collective-permute-start(f32[256,384]{1,0:T(8,128)} %collective-permute-done.8.refs_10_), channel_id=1, source_target_pairs={{0,4},{4,0},{8,12},{12,8},{16,20},{20,16},{24,28},{28,24},{1,5},{5... | collective-permute-start | bytes 1179656 | tf_op jit(solution)/shard_map/ppermute | solution.py:275
  84.6 1.9 %collective-permute-start.16 = (f32[256,384]{1,0:T(8,128)}, f32[256,384]{1,0:T(8,128)S(1)}, u32[]{:S(2)}, u32[]{:S(2)}) collective-permute-start(f32[256,384]{1,0:T(8,128)} %collective-permute-done.15.refs_18_), channel_id=1, source_target_pairs={{0,4},{4,0},{8,12},{12,8},{16,20},{20,16},{24,28},{28,24},{1,5},{5... | collective-permute-start | bytes 1179656 | tf_op jit(solution)/shard_map/ppermute | solution.py:275
  (6 other events, 43.3 us)

commit v7 on v6

--- a/solution.py
+++ b/solution.py
@@ -258,21 +258,27 @@
             axis_index_groups=[[0, 2, 4, 6], [1, 3, 5, 7]],
             tiled=True,
         )
-        spread, first, tiles = lax.optimization_barrier((spread, ring(panel), tiles))
+        first = ring(panel)
+        spread, tiles = lax.optimization_barrier((spread, tiles))
         wanted = lax.all_to_all(spread, "col", split_axis=0, concat_axis=0, tiled=True)
         wanted, first, tiles = lax.optimization_barrier((wanted, first, tiles))
         second = ring(first)
         siblings = [(p, p ^ 1) for p in range(row_devices)]
+        turns = [
+            [(2 * c + m, 2 * step[c] + m) for c in range(4) for m in range(2)]
+            for step in (NEXT, PREV)
+        ]
+        held = list(pair_factor(diag_inverse, wanted, quarter))
         pieces, plan = [], []
-        turns = ((NEXT, 1), (PREV, -1))
-        for h, piece in enumerate(pair_factor(diag_inverse, wanted, quarter)):
-            step, sign = turns[h]
-            turn = [(2 * c + m, 2 * step[c] + m) for c in range(4) for m in range(2)]
-            for n in range(4):
-                if n > 0:
-                    piece = lax.ppermute(piece, "row", turn)
-                plan += [(h, sign * n, 0), (h, sign * n, 1)]
-                pieces += [piece, lax.ppermute(piece, "row", siblings)]
+        for n in range(4):
+            if n > 0:
+                held = [lax.ppermute(x, "row", turn) for x, turn in zip(held, turns)]
+            if n == 1:
+                *held, second = lax.optimization_barrier((*held, second))
+            for h, x in enumerate(held):
+                steps = n if h == 0 else -n
+                plan += [(h, steps, 0), (h, steps, 1)]
+                pieces += [x, lax.ppermute(x, "row", siblings)]
         own = [panel, first, second, ring(second)]
     else:
         whole = lax.all_gather(panel, "col", axis=0)

time: 123 us -> 132 us (1.073)
  waiting for transfers between devices: 38 us -> 65.6 us
  blocking collectives: 24 us -> 0 us
  starting transfers between devices: 19.2 us -> 23.4 us
  local copies, waits for them, and re-layouts: 3.49 us -> 4.87 us
    ppermute x15, waiting for transfers between devices: 20.7 us -> 45.7 us  [the longest x1 34.2 us: per_device(): first = ring(panel)]
    all_to_all x1 -> x0, blocking collectives: 24 us -> none  [per_device(): lax.all_to_all(spread, 'col', split_axis=0, concat_axis=0, tiled=True)]
    all_to_all x0 -> x1, starting transfers between devices: none -> 5.1 us  [per_device(): lax.all_to_all(spread, 'col', split_axis=0, concat_axis=0, tiled=True)]
    ppermute x1, waiting for transfers between devices: 0.01 us -> 3.19 us  [per_device(): second = ring(first)]
    ppermute x1, waiting for transfers between devices: 7.16 us -> 4.85 us  [per_device(): own = [panel, first, second, ring(second)]]
    all_to_all x1, starting transfers between devices: 3.72 us -> 5.18 us  [per_device(): lax.all_to_all(panel.reshape(4, quarter, part), 'row', split_axis=0, conc...]
    unnamed x23 -> x25, local copies, waits for them, and re-layouts: 0.93 us -> 2.31 us
  transfers between devices with their start and end apart: 19 -> 20, of which waited for: 8 -> 8; matrix products, arithmetic and copies ran while one was open for 7% -> 7% of each run, Pallas kernels for 0% -> 2%
where the time goes in v7:
time: 132 us; the launch traced here: 131 us
  waiting for transfers between devices  65.6 us (50%)
  Pallas kernels  30.7 us (23%)
  starting transfers between devices  23.4 us (18%)
  other arithmetic  5.9 us (4%)
  local copies, waits for them, and re-layouts  4.87 us (4%)
    ppermute x1, waiting for transfers between devices, per_device(): first = ring(panel)  34.2 us
    pallas_call x1, Pallas kernels, front(): pl.pallas_call(functools.partial(front_kernel, ringed, own_plan, plan), g...  27.7 us
    ppermute x6, waiting for transfers between devices, per_device(): held = [lax.ppermute(x, 'row', turn) for x, turn in zip(held, turns)]  11.5 us
    all_to_all x1, waiting for transfers between devices, per_device(): lax.all_to_all(panel.reshape(4, quarter, part), 'row', split_axis=0, conc...  6.13 us
    ppermute x6, starting transfers between devices, per_device(): held = [lax.ppermute(x, 'row', turn) for x, turn in zip(held, turns)]  6.08 us
    all_to_all x1, waiting for transfers between devices, exchange_tiles(): got = lax.all_to_all(send, 'row', split_axis=0, concat_axis=0, tiled=True)  5.75 us
    all_to_all x1, starting transfers between devices, per_device(): lax.all_to_all(panel.reshape(4, quarter, part), 'row', split_axis=0, conc...  5.18 us
    all_to_all x1, starting transfers between devices, per_device(): lax.all_to_all(spread, 'col', split_axis=0, concat_axis=0, tiled=True)  5.1 us
  transfers between devices with their start and end apart: 20, of which 8 were waited for; matrix products, arithmetic and copies ran while one was open for 7% of the time, Pallas kernels for 2%

profile of v7, /device:TPU:0, one launch (start us, length us, event | category | flops | bytes accessed | tf_op | source)
XLA Modules:
  0.0 131.3 jit_solution(12266239591653435855)
XLA Ops:
  0.6 5.2 %all-to-all-start = ((f32[4,384,128]{2,1,0:T(8,128)}), f32[4,384,128]{2,1,0:T(8,128)}, u32[]{:S(2)}, u32[]{:S(2)}) async-start(f32[4,384,128]{2,1,0:T(8,128)} %bitcast.22), calls=%async_computation | async-start | bytes 1572864 | tf_op jit(solution)/shard_map/all_to_all | solution.py:253
  5.8 0.9 convert_reduce_fusion.1
  8.9 1.5 %scatter_fusion = f32[16,8,128]{2,1,0:T(8,128)S(1)} fusion(f32[16,8,128]{2,1,0:T(8,128)S(1)} %broadcast_in_dim.18, s32[12]{0:T(128)S(1)} %fusion.6, f32[12,8,128]{2,1,0:T(8,128)} %bitcast.25), kind=kCustom, calls=%fused_computation | custom fusion | bytes 147504 | tf_op jit(solution)/shard_map/scatter | solution.py:204
  11.1 6.1 %all-to-all-done = f32[4,384,128]{2,1,0:T(8,128)} async-done(((f32[4,384,128]{2,1,0:T(8,128)}), f32[4,384,128]{2,1,0:T(8,128)}, u32[]{:S(2)}, u32[]{:S(2)}) %all-to-all-start) | async-done | bytes 786464 | tf_op jit(solution)/shard_map/all_to_all | solution.py:253
  17.2 5.1 %all-to-all-start.1 = ((f32[4,384,128]{2,1,0:T(8,128)}), f32[4,384,128]{2,1,0:T(8,128)S(1)}, u32[]{:S(2)}, u32[]{:S(2)}) async-start(f32[4,384,128]{2,1,0:T(8,128)} %all-to-all-done), calls=%async_computation.1 | async-start | bytes 1572864 | tf_op jit(solution)/shard_map/all_to_all | solution.py:263
  22.3 2.0 %collective-permute-start = (f32[1536,128]{1,0:T(8,128)}, f32[1536,128]{1,0:T(8,128)S(1)}, u32[]{:S(2)}, u32[]{:S(2)}) collective-permute-start(f32[1536,128]{1,0:T(8,128)} %refs_0_.1), channel_id=1, source_target_pairs={{0,1},{1,3},{3,2},{2,0},{4,5},{5,7},{7,6},{6,4},{8,9},{9,11},{11,1... | collective-permute-start | bytes 2359304 | tf_op jit(solution)/shard_map/ppermute | solution.py:261
  24.3 34.2 %collective-permute-done.refs_1_ = f32[1536,128]{1,0:T(8,128)S(1)} collective-permute-done((f32[1536,128]{1,0:T(8,128)}, f32[1536,128]{1,0:T(8,128)S(1)}, u32[]{:S(2)}, u32[]{:S(2)}) %collective-permute-start) | collective-permute-done | bytes 786464 | tf_op jit(solution)/shard_map/ppermute | solution.py:261
  58.6 0.8 copy-done
  59.4 3.0 %pair_factor.1 = (f32[256,384]{1,0:T(8,128)}, f32[256,384]{1,0:T(8,128)}) custom-call(f32[512,512]{1,0:T(8,128)} %d_ref.3, f32[4,384,128]{2,1,0:T(8,128)} %copy-done), custom_call_target="tpu_custom_call" | custom-call | flops 603979776 | bytes 1572864 | tf_op jit(solution)/shard_map/pair_factor/pallas_call | solution.py:48
  62.4 1.3 %collective-permute-start.1 = (f32[256,384]{1,0:T(8,128)}, f32[256,384]{1,0:T(8,128)S(1)}, u32[]{:S(2)}, u32[]{:S(2)}) collective-permute-start(f32[256,384]{1,0:T(8,128)} %get-tuple-element.17.refs_4_), channel_id=1, source_target_pairs={{0,8},{4,12},{8,24},{12,28},{16,0},{20,4},{24,16},{28,20},{1,9},{5... | collective-permute-start | bytes 1179656 | tf_op jit(solution)/shard_map/ppermute | solution.py:275
  63.7 0.7 collective-permute-start.2
  64.4 3.4 %all-to-all-start.2 = ((f32[8,3,8,128]{3,2,1,0:T(8,128)}), f32[8,3,8,128]{3,2,1,0:T(8,128)S(1)}, u32[]{:S(2)}, u32[]{:S(2)}) async-start(f32[8,3,8,128]{3,2,1,0:T(8,128)} %select_maximum_fusion), calls=%async_computation.2 | async-start | bytes 196608 | tf_op jit(solution)/shard_map/all_to_all | solution.py:212
  68.9 5.7 %all-to-all-done.2 = f32[8,3,8,128]{3,2,1,0:T(8,128)S(1)} async-done(((f32[8,3,8,128]{3,2,1,0:T(8,128)}), f32[8,3,8,128]{3,2,1,0:T(8,128)S(1)}, u32[]{:S(2)}, u32[]{:S(2)}) %all-to-all-start.2) | async-done | bytes 98336 | tf_op jit(solution)/shard_map/all_to_all | solution.py:212
  74.8 3.2 %collective-permute-done.3.refs_2_ = f32[1536,128]{1,0:T(8,128)S(1)} collective-permute-done((f32[1536,128]{1,0:T(8,128)S(1)}, f32[1536,128]{1,0:T(8,128)S(1)}, u32[]{:S(2)}, u32[]{:S(2)}) %collective-permute-start.3) | collective-permute-done | bytes 786464 | tf_op jit(solution)/shard_map/ppermute | solution.py:265
  78.0 1.3 %collective-permute-start.9 = (f32[256,384]{1,0:T(8,128)S(1)}, f32[256,384]{1,0:T(8,128)}, u32[]{:S(2)}, u32[]{:S(2)}) collective-permute-start(f32[256,384]{1,0:T(8,128)S(1)} %collective-permute-done.1.refs_8_), channel_id=1, source_target_pairs={{0,8},{4,12},{8,24},{12,28},{16,0},{20,4},{24,16},{28,20},{1,9},{5... | collective-permute-start | bytes 1179656 | tf_op jit(solution)/shard_map/ppermute | solution.py:275
  81.6 5.6 %collective-permute-done.9.refs_12_ = f32[256,384]{1,0:T(8,128)} collective-permute-done((f32[256,384]{1,0:T(8,128)S(1)}, f32[256,384]{1,0:T(8,128)}, u32[]{:S(2)}, u32[]{:S(2)}) %collective-permute-start.9) | collective-permute-done | bytes 393248 | tf_op jit(solution)/shard_map/ppermute | solution.py:275
  87.2 1.3 %collective-permute-start.13 = (f32[256,384]{1,0:T(8,128)}, f32[256,384]{1,0:T(8,128)}, u32[]{:S(2)}, u32[]{:S(2)}) collective-permute-start(f32[256,384]{1,0:T(8,128)} %collective-permute-done.9.refs_12_), channel_id=1, source_target_pairs={{0,8},{4,12},{8,24},{12,28},{16,0},{20,4},{24,16},{28,20},{1,9},{5... | collective-permute-start | bytes 1179656 | tf_op jit(solution)/shard_map/ppermute | solution.py:275
  88.5 0.7 collective-permute-start.15
  90.9 4.8 %collective-permute-done.13.refs_16_ = f32[256,384]{1,0:T(8,128)} collective-permute-done((f32[256,384]{1,0:T(8,128)}, f32[256,384]{1,0:T(8,128)}, u32[]{:S(2)}, u32[]{:S(2)}) %collective-permute-start.13) | collective-permute-done | bytes 393248 | tf_op jit(solution)/shard_map/ppermute | solution.py:275
  95.8 1.1 collective-permute-done.15.refs_18_
  96.8 0.7 multiply_reduce_fusion.entry_ref
  97.6 4.8 %collective-permute-done.4.refs_3_ = f32[1536,128]{1,0:T(8,128)S(1)} collective-permute-done((f32[1536,128]{1,0:T(8,128)S(1)}, f32[1536,128]{1,0:T(8,128)S(1)}, u32[]{:S(2)}, u32[]{:S(2)}) %collective-permute-start.4) | collective-permute-done | bytes 786464 | tf_op jit(solution)/shard_map/ppermute | solution.py:282
  102.5 0.8 copy-done.4
  103.6 27.7 %front.1 = (f32[1536,3072]{1,0:T(8,128)}, f32[1536,128]{1,0:T(8,128)}) custom-call(s32[2]{0:T(128)} %pad_add_fusion.1.place_ref, s32[3,16]{1,0:T(4,128)} %multiply_reduce_fusion.entry_ref, s32[7]{0:T(128)} %convert_reduce_fusion.2.start_ref, f32[512,512]{1,0:T(8,128)} %d_ref.3, f32[24,8,128]{2,1,0:T(8,128)} %bitcast.24, f32[1536,3072]{1,0:T(8,128)} %trail_ref.1, ...), custom_call_target="tpu_custom_call" | custom-call | flops 16911433728 | bytes 44040192 | tf_op jit(solution)/shard_map/front/pallas_call | solution.py:159
  (77 shorter events, 8.4 us)
Async XLA Ops:
  0.6 16.6 %all-to-all-start = ((f32[4,384,128]{2,1,0:T(8,128)}), f32[4,384,128]{2,1,0:T(8,128)}, u32[]{:S(2)}, u32[]{:S(2)}) async-start(f32[4,384,128]{2,1,0:T(8,128)} %bitcast.22), calls=%async_computation | async-start | bytes 1572864 | tf_op jit(solution)/shard_map/all_to_all | solution.py:253
  17.2 41.3 %all-to-all-start.1 = ((f32[4,384,128]{2,1,0:T(8,128)}), f32[4,384,128]{2,1,0:T(8,128)S(1)}, u32[]{:S(2)}, u32[]{:S(2)}) async-start(f32[4,384,128]{2,1,0:T(8,128)} %all-to-all-done), calls=%async_computation.1 | async-start | bytes 1572864 | tf_op jit(solution)/shard_map/all_to_all | solution.py:263
  22.3 36.2 %collective-permute-start = (f32[1536,128]{1,0:T(8,128)}, f32[1536,128]{1,0:T(8,128)S(1)}, u32[]{:S(2)}, u32[]{:S(2)}) collective-permute-start(f32[1536,128]{1,0:T(8,128)} %refs_0_.1), channel_id=1, source_target_pairs={{0,1},{1,3},{3,2},{2,0},{4,5},{5,7},{7,6},{6,4},{8,9},{9,11},{11,1... | collective-permute-start | bytes 2359304 | tf_op jit(solution)/shard_map/ppermute | solution.py:261
  58.5 43.9 %copy-start.2 = (f32[1536,128]{1,0:T(8,128)}, f32[1536,128]{1,0:T(8,128)S(1)}, u32[]{:S(2)}) copy-start(f32[1536,128]{1,0:T(8,128)S(1)} %collective-permute-done.refs_1_) | copy-start | bytes 2359300
  58.5 19.4 %collective-permute-start.3 = (f32[1536,128]{1,0:T(8,128)S(1)}, f32[1536,128]{1,0:T(8,128)S(1)}, u32[]{:S(2)}, u32[]{:S(2)}) collective-permute-start(f32[1536,128]{1,0:T(8,128)S(1)} %collective-permute-done.refs_1_), channel_id=1, source_target_pairs={{0,1},{1,3},{3,2},{2,0},{4,5},{5,7},{7,6},{6,4},{8,9},{9,11},{11,1... | collective-permute-start | bytes 2359304 | tf_op jit(solution)/shard_map/ppermute | solution.py:265
  62.4 12.4 %collective-permute-start.1 = (f32[256,384]{1,0:T(8,128)}, f32[256,384]{1,0:T(8,128)S(1)}, u32[]{:S(2)}, u32[]{:S(2)}) collective-permute-start(f32[256,384]{1,0:T(8,128)} %get-tuple-element.17.refs_4_), channel_id=1, source_target_pairs={{0,8},{4,12},{8,24},{12,28},{16,0},{20,4},{24,16},{28,20},{1,9},{5... | collective-permute-start | bytes 1179656 | tf_op jit(solution)/shard_map/ppermute | solution.py:275
  63.7 11.0 %collective-permute-start.2 = (f32[256,384]{1,0:T(8,128)}, f32[256,384]{1,0:T(8,128)S(1)}, u32[]{:S(2)}, u32[]{:S(2)}) collective-permute-start(f32[256,384]{1,0:T(8,128)} %get-tuple-element.18.refs_6_), channel_id=1, source_target_pairs={{0,16},{4,20},{8,0},{12,4},{16,24},{20,28},{24,8},{28,12},{1,17},{... | collective-permute-start | bytes 1179656 | tf_op jit(solution)/shard_map/ppermute | solution.py:275
  64.4 10.2 %all-to-all-start.2 = ((f32[8,3,8,128]{3,2,1,0:T(8,128)}), f32[8,3,8,128]{3,2,1,0:T(8,128)S(1)}, u32[]{:S(2)}, u32[]{:S(2)}) async-start(f32[8,3,8,128]{3,2,1,0:T(8,128)} %select_maximum_fusion), calls=%async_computation.2 | async-start | bytes 196608 | tf_op jit(solution)/shard_map/all_to_all | solution.py:212
  68.4 12.4 %collective-permute-start.5 = (f32[256,384]{1,0:T(8,128)}, f32[256,384]{1,0:T(8,128)S(1)}, u32[]{:S(2)}, u32[]{:S(2)}) collective-permute-start(f32[256,384]{1,0:T(8,128)} %get-tuple-element.17.refs_4_), channel_id=1, source_target_pairs={{0,4},{4,0},{8,12},{12,8},{16,20},{20,16},{24,28},{28,24},{1,5},{5... | collective-permute-start | bytes 1179656 | tf_op jit(solution)/shard_map/ppermute | solution.py:281
  68.8 12.8 %collective-permute-start.6 = (f32[256,384]{1,0:T(8,128)}, f32[256,384]{1,0:T(8,128)}, u32[]{:S(2)}, u32[]{:S(2)}) collective-permute-start(f32[256,384]{1,0:T(8,128)} %get-tuple-element.18.refs_6_), channel_id=1, source_target_pairs={{0,4},{4,0},{8,12},{12,8},{16,20},{20,16},{24,28},{28,24},{1,5},{5... | collective-permute-start | bytes 1179656 | tf_op jit(solution)/shard_map/ppermute | solution.py:281
  74.6 27.8 %copy-start.1 = (f32[8,3,8,128]{3,2,1,0:T(8,128)}, f32[8,3,8,128]{3,2,1,0:T(8,128)S(1)}, u32[]{:S(2)}) copy-start(f32[8,3,8,128]{3,2,1,0:T(8,128)S(1)} %all-to-all-done.2) | copy-start | bytes 294916
  74.7 27.7 %copy-start.5 = (f32[256,384]{1,0:T(8,128)}, f32[256,384]{1,0:T(8,128)S(1)}, u32[]{:S(2)}) copy-start(f32[256,384]{1,0:T(8,128)S(1)} %collective-permute-done.1.refs_8_) | copy-start | bytes 1179652
  74.8 27.7 %copy-start.6 = (f32[256,384]{1,0:T(8,128)}, f32[256,384]{1,0:T(8,128)S(1)}, u32[]{:S(2)}) copy-start(f32[256,384]{1,0:T(8,128)S(1)} %collective-permute-done.2.refs_10_) | copy-start | bytes 1179652
  78.0 9.3 %collective-permute-start.9 = (f32[256,384]{1,0:T(8,128)S(1)}, f32[256,384]{1,0:T(8,128)}, u32[]{:S(2)}, u32[]{:S(2)}) collective-permute-start(f32[256,384]{1,0:T(8,128)S(1)} %collective-permute-done.1.refs_8_), channel_id=1, source_target_pairs={{0,8},{4,12},{8,24},{12,28},{16,0},{20,4},{24,16},{28,20},{1,9},{5... | collective-permute-start | bytes 1179656 | tf_op jit(solution)/shard_map/ppermute | solution.py:275
  79.3 9.3 %collective-permute-start.11 = (f32[256,384]{1,0:T(8,128)S(1)}, f32[256,384]{1,0:T(8,128)}, u32[]{:S(2)}, u32[]{:S(2)}) collective-permute-start(f32[256,384]{1,0:T(8,128)S(1)} %collective-permute-done.2.refs_10_), channel_id=1, source_target_pairs={{0,16},{4,20},{8,0},{12,4},{16,24},{20,28},{24,8},{28,12},{1,17},{... | collective-permute-start | bytes 1179656 | tf_op jit(solution)/shard_map/ppermute | solution.py:275
  80.7 9.6 %collective-permute-start.7 = (f32[256,384]{1,0:T(8,128)S(1)}, f32[256,384]{1,0:T(8,128)}, u32[]{:S(2)}, u32[]{:S(2)}) collective-permute-start(f32[256,384]{1,0:T(8,128)S(1)} %collective-permute-done.1.refs_8_), channel_id=1, source_target_pairs={{0,4},{4,0},{8,12},{12,8},{16,20},{20,16},{24,28},{28,24},{1,5},{5... | collective-permute-start | bytes 1179656 | tf_op jit(solution)/shard_map/ppermute | solution.py:281
  80.8 9.6 %collective-permute-start.8 = (f32[256,384]{1,0:T(8,128)S(1)}, f32[256,384]{1,0:T(8,128)}, u32[]{:S(2)}, u32[]{:S(2)}) collective-permute-start(f32[256,384]{1,0:T(8,128)S(1)} %collective-permute-done.2.refs_10_), channel_id=1, source_target_pairs={{0,4},{4,0},{8,12},{12,8},{16,20},{20,16},{24,28},{28,24},{1,5},{5... | collective-permute-start | bytes 1179656 | tf_op jit(solution)/shard_map/ppermute | solution.py:281
  81.6 20.8 %collective-permute-start.4 = (f32[1536,128]{1,0:T(8,128)S(1)}, f32[1536,128]{1,0:T(8,128)S(1)}, u32[]{:S(2)}, u32[]{:S(2)}) collective-permute-start(f32[1536,128]{1,0:T(8,128)S(1)} %collective-permute-done.3.refs_2_), channel_id=1, source_target_pairs={{0,1},{1,3},{3,2},{2,0},{4,5},{5,7},{7,6},{6,4},{8,9},{9,11},{11,1... | collective-permute-start | bytes 2359304 | tf_op jit(solution)/shard_map/ppermute | solution.py:282
  87.2 8.5 %collective-permute-start.13 = (f32[256,384]{1,0:T(8,128)}, f32[256,384]{1,0:T(8,128)}, u32[]{:S(2)}, u32[]{:S(2)}) collective-permute-start(f32[256,384]{1,0:T(8,128)} %collective-permute-done.9.refs_12_), channel_id=1, source_target_pairs={{0,8},{4,12},{8,24},{12,28},{16,0},{20,4},{24,16},{28,20},{1,9},{5... | collective-permute-start | bytes 1179656 | tf_op jit(solution)/shard_map/ppermute | solution.py:275
  88.5 8.3 %collective-permute-start.15 = (f32[256,384]{1,0:T(8,128)}, f32[256,384]{1,0:T(8,128)}, u32[]{:S(2)}, u32[]{:S(2)}) collective-permute-start(f32[256,384]{1,0:T(8,128)} %collective-permute-done.11.refs_14_), channel_id=1, source_target_pairs={{0,16},{4,20},{8,0},{12,4},{16,24},{20,28},{24,8},{28,12},{1,17},{... | collective-permute-start | bytes 1179656 | tf_op jit(solution)/shard_map/ppermute | solution.py:275
  90.3 7.2 %collective-permute-start.10 = (f32[256,384]{1,0:T(8,128)}, f32[256,384]{1,0:T(8,128)S(1)}, u32[]{:S(2)}, u32[]{:S(2)}) collective-permute-start(f32[256,384]{1,0:T(8,128)} %collective-permute-done.9.refs_12_), channel_id=1, source_target_pairs={{0,4},{4,0},{8,12},{12,8},{16,20},{20,16},{24,28},{28,24},{1,5},{5... | collective-permute-start | bytes 1179656 | tf_op jit(solution)/shard_map/ppermute | solution.py:281
  90.4 7.1 %collective-permute-start.12 = (f32[256,384]{1,0:T(8,128)}, f32[256,384]{1,0:T(8,128)S(1)}, u32[]{:S(2)}, u32[]{:S(2)}) collective-permute-start(f32[256,384]{1,0:T(8,128)} %collective-permute-done.11.refs_14_), channel_id=1, source_target_pairs={{0,4},{4,0},{8,12},{12,8},{16,20},{20,16},{24,28},{28,24},{1,5},{5... | collective-permute-start | bytes 1179656 | tf_op jit(solution)/shard_map/ppermute | solution.py:281
  95.8 6.7 %collective-permute-start.14 = (f32[256,384]{1,0:T(8,128)}, f32[256,384]{1,0:T(8,128)S(1)}, u32[]{:S(2)}, u32[]{:S(2)}) collective-permute-start(f32[256,384]{1,0:T(8,128)} %collective-permute-done.13.refs_16_), channel_id=1, source_target_pairs={{0,4},{4,0},{8,12},{12,8},{16,20},{20,16},{24,28},{28,24},{1,5},{5... | collective-permute-start | bytes 1179656 | tf_op jit(solution)/shard_map/ppermute | solution.py:281
  96.8 5.6 %collective-permute-start.16 = (f32[256,384]{1,0:T(8,128)}, f32[256,384]{1,0:T(8,128)S(1)}, u32[]{:S(2)}, u32[]{:S(2)}) collective-permute-start(f32[256,384]{1,0:T(8,128)} %collective-permute-done.15.refs_18_), channel_id=1, source_target_pairs={{0,4},{4,0},{8,12},{12,8},{16,20},{20,16},{24,28},{28,24},{1,5},{5... | collective-permute-start | bytes 1179656 | tf_op jit(solution)/shard_map/ppermute | solution.py:281
  (8 other events, 39.1 us)

commit v8 on v7

--- a/solution.py
+++ b/solution.py
@@ -76,13 +76,13 @@
     half = width // 2
     part = width // 4
 
-    @pl.when((i == 0) & (j == 0))
-    def _():
-        todo = []
+    def own_copies():
         for n, s in enumerate(own_plan):
             source = ring_place(place_ref[1], s) if ringed else s
             lanes = pl.ds(pl.multiple_of(source * part, part), part)
-            todo.append(pltpu.make_async_copy(own_pieces[n], own_stage.at[:, lanes], sem.at[n]))
+            yield pltpu.make_async_copy(own_pieces[n], own_stage.at[:, lanes], sem.at[n])
+
+    def pair_copies():
         for n, (upper, steps, swap) in enumerate(plan):
             depth, cols = pieces[n].shape
             block = 0
@@ -90,18 +90,21 @@
                 chip = ring_place(place_ref[0] // 2, steps)
                 block = (place_ref[0] % 2 ^ swap) * 4 + chip
             at = pl.ds(pl.multiple_of(block * cols, TILE_COLS), cols)
-            rows = pl.ds(upper * depth, depth)
-            todo.append(
-                pltpu.make_async_copy(pieces[n], stage.at[rows, at], sem.at[n_own + n])
-            )
-        for c in todo:
+            target = stage.at[pl.ds(upper * depth, depth), at]
+            yield pltpu.make_async_copy(pieces[n], target, sem.at[n_own + n])
+
+    @pl.when((i == 0) & (j == 0))
+    def _():
+        for c in own_copies():
+            c.start()
+        for c in pair_copies():
             c.start()
         hi, lo = split(d_ref[...].T)
         dt_left[...] = jnp.concatenate(
             [hi[:half, :half], hi[:half, :half], lo[:half, :half]], axis=0
         )
         dt_right[...] = jnp.concatenate([hi[:, half:], hi[:, half:], lo[:, half:]], axis=0)
-        for c in todo:
+        for c in own_copies():
             c.wait()
 
     rows = pl.ds(pl.multiple_of(i * bm, bm), bm)
@@ -120,6 +123,11 @@
         block_ref[...] = full[:, pl.ds(pl.multiple_of(place_ref[1] * part, part), part)]
         hi, lo = split(full[...])
         own_cat[rows, :] = jnp.concatenate([hi, hi, lo], axis=1)
+
+    @pl.when((i == 0) & (j == 0))
+    def _():
+        for c in pair_copies():
+            c.wait()
 
     @pl.when(i == 0)
     def _():
@@ -258,8 +266,7 @@
             axis_index_groups=[[0, 2, 4, 6], [1, 3, 5, 7]],
             tiled=True,
         )
-        first = ring(panel)
-        spread, tiles = lax.optimization_barrier((spread, tiles))
+        spread, first, tiles = lax.optimization_barrier((spread, ring(panel), tiles))
         wanted = lax.all_to_all(spread, "col", split_axis=0, concat_axis=0, tiled=True)
         wanted, first, tiles = lax.optimization_barrier((wanted, first, tiles))
         second = ring(first)

time: 132 us -> 118 us (0.89)
  waiting for transfers between devices: 65.6 us -> 34.8 us
  blocking collectives: 0 us -> 24 us
  starting transfers between devices: 23.4 us -> 18.4 us
    ppermute x1, waiting for transfers between devices: 34.2 us -> 4.47 us  [per_device(): ring(panel)]
    all_to_all x0 -> x1, blocking collectives: none -> 24 us  [per_device(): lax.all_to_all(spread, 'col', split_axis=0, concat_axis=0, tiled=True)]
    all_to_all x1 -> x0, starting transfers between devices: 5.1 us -> none  [per_device(): lax.all_to_all(spread, 'col', split_axis=0, concat_axis=0, tiled=True)]
    all_to_all x1, starting transfers between devices: 5.18 us -> 3.72 us  [per_device(): lax.all_to_all(panel.reshape(4, quarter, part), 'row', split_axis=0, conc...]
  transfers between devices with their start and end apart: 20 -> 19, of which waited for: 8 -> 9; matrix products, arithmetic and copies ran while one was open for 7% -> 7% of each run, Pallas kernels for 2% -> 3%
where the time goes in v8:
time: 118 us
  waiting for transfers between devices  34.8 us (29%)
  Pallas kernels  29.6 us (25%)
  blocking collectives  24 us (20%)
  starting transfers between devices  18.4 us (16%)
  other arithmetic  6.03 us (5%)
  local copies, waits for them, and re-layouts  4.03 us (3%)
    pallas_call x1, Pallas kernels, front(): pl.pallas_call(functools.partial(front_kernel, ringed, own_plan, plan), g...  26.6 us
    all_to_all x1, blocking collectives, per_device(): lax.all_to_all(spread, 'col', split_axis=0, concat_axis=0, tiled=True)  24 us
    ppermute x6, waiting for transfers between devices, per_device(): held = [lax.ppermute(x, 'row', turn) for x, turn in zip(held, turns)]  11.4 us
    ppermute x6, starting transfers between devices, per_device(): held = [lax.ppermute(x, 'row', turn) for x, turn in zip(held, turns)]  6.08 us
    all_to_all x1, waiting for transfers between devices, per_device(): lax.all_to_all(panel.reshape(4, quarter, part), 'row', split_axis=0, conc...  5.28 us
    ppermute x1, waiting for transfers between devices, per_device(): own = [panel, first, second, ring(second)]  4.89 us
    all_to_all x1, waiting for transfers between devices, exchange_tiles(): got = lax.all_to_all(send, 'row', split_axis=0, concat_axis=0, tiled=True)  4.87 us
    ppermute x1, waiting for transfers between devices, per_device(): ring(panel)  4.47 us
  transfers between devices with their start and end apart: 19, of which 9 were waited for; matrix products, arithmetic and copies ran while one was open for 7% of the time, Pallas kernels for 3%

profile of v8, /device:TPU:0, one launch (start us, length us, event | category | flops | bytes accessed | tf_op | source)
XLA Modules:
  0.0 117.7 jit_solution(17033469524067486295)
XLA Ops:
  0.6 3.1 %collective-permute-start = (f32[1536,128]{1,0:T(8,128)}, f32[1536,128]{1,0:T(8,128)S(1)}, u32[]{:S(2)}, u32[]{:S(2)}) collective-permute-start(f32[1536,128]{1,0:T(8,128)} %refs_0_.1), channel_id=1, source_target_pairs={{0,1},{1,3},{3,2},{2,0},{4,5},{5,7},{7,6},{6,4},{8,9},{9,11},{11,1... | collective-permute-start | bytes 2359304 | tf_op jit(solution)/shard_map/ppermute | solution.py:269
  3.7 3.7 %all-to-all-start = ((f32[4,384,128]{2,1,0:T(8,128)}), f32[4,384,128]{2,1,0:T(8,128)S(1)}, u32[]{:S(2)}, u32[]{:S(2)}) async-start(f32[4,384,128]{2,1,0:T(8,128)} %bitcast.22), calls=%async_computation | async-start | bytes 1572864 | tf_op jit(solution)/shard_map/all_to_all | solution.py:261
  7.4 0.9 convert_reduce_fusion.1
  8.3 0.7 multiply_add_fusion
  9.9 0.7 fusion.6
  10.5 1.5 %scatter_fusion = f32[16,8,128]{2,1,0:T(8,128)S(1)} fusion(f32[16,8,128]{2,1,0:T(8,128)S(1)} %broadcast_in_dim.18, s32[12]{0:T(128)S(1)} %fusion.6, f32[12,8,128]{2,1,0:T(8,128)} %bitcast.25), kind=kCustom, calls=%fused_computation | custom fusion | bytes 147504 | tf_op jit(solution)/shard_map/scatter | solution.py:212
  12.7 5.3 %all-to-all-done = f32[4,384,128]{2,1,0:T(8,128)S(1)} async-done(((f32[4,384,128]{2,1,0:T(8,128)}), f32[4,384,128]{2,1,0:T(8,128)S(1)}, u32[]{:S(2)}, u32[]{:S(2)}) %all-to-all-start) | async-done | bytes 786464 | tf_op jit(solution)/shard_map/all_to_all | solution.py:261
  18.0 4.5 %collective-permute-done.refs_1_ = f32[1536,128]{1,0:T(8,128)S(1)} collective-permute-done((f32[1536,128]{1,0:T(8,128)}, f32[1536,128]{1,0:T(8,128)S(1)}, u32[]{:S(2)}, u32[]{:S(2)}) %collective-permute-start) | collective-permute-done | bytes 786464 | tf_op jit(solution)/shard_map/ppermute | solution.py:269
  22.5 24.0 %all_to_all.15.panel_ref = f32[4,384,128]{2,1,0:T(8,128)} all-to-all(f32[4,384,128]{2,1,0:T(8,128)S(1)} %all-to-all-done), channel_id=1, replica_groups=mesh['row'=8,'col'=4] {'col'}, dimensions={0} | all-to-all | bytes 1572864 | tf_op jit(solution)/shard_map/all_to_all | solution.py:270
  46.7 3.0 %pair_factor.1 = (f32[256,384]{1,0:T(8,128)}, f32[256,384]{1,0:T(8,128)}) custom-call(f32[512,512]{1,0:T(8,128)} %d_ref.3, f32[4,384,128]{2,1,0:T(8,128)} %all_to_all.15.panel_ref), custom_call_target="tpu_custom_call" | custom-call | flops 603979776 | bytes 1572864 | tf_op jit(solution)/shard_map/pair_factor/pallas_call | solution.py:48
  49.7 1.5 %collective-permute-start.1 = (f32[256,384]{1,0:T(8,128)}, f32[256,384]{1,0:T(8,128)S(1)}, u32[]{:S(2)}, u32[]{:S(2)}) collective-permute-start(f32[256,384]{1,0:T(8,128)} %get-tuple-element.19.refs_4_), channel_id=1, source_target_pairs={{0,8},{4,12},{8,24},{12,28},{16,0},{20,4},{24,16},{28,20},{1,9},{5... | collective-permute-start | bytes 1179656 | tf_op jit(solution)/shard_map/ppermute | solution.py:282
  51.8 3.7 %all-to-all-start.2 = ((f32[8,3,8,128]{3,2,1,0:T(8,128)}), f32[8,3,8,128]{3,2,1,0:T(8,128)S(1)}, u32[]{:S(2)}, u32[]{:S(2)}) async-start(f32[8,3,8,128]{3,2,1,0:T(8,128)} %select_maximum_fusion), calls=%async_computation.2 | async-start | bytes 196608 | tf_op jit(solution)/shard_map/all_to_all | solution.py:220
  56.6 4.9 %all-to-all-done.2 = f32[8,3,8,128]{3,2,1,0:T(8,128)S(1)} async-done(((f32[8,3,8,128]{3,2,1,0:T(8,128)}), f32[8,3,8,128]{3,2,1,0:T(8,128)S(1)}, u32[]{:S(2)}, u32[]{:S(2)}) %all-to-all-start.2) | async-done | bytes 98336 | tf_op jit(solution)/shard_map/all_to_all | solution.py:220
  61.6 3.9 %collective-permute-done.3.refs_2_ = f32[1536,128]{1,0:T(8,128)S(1)} collective-permute-done((f32[1536,128]{1,0:T(8,128)S(1)}, f32[1536,128]{1,0:T(8,128)S(1)}, u32[]{:S(2)}, u32[]{:S(2)}) %collective-permute-start.3) | collective-permute-done | bytes 786464 | tf_op jit(solution)/shard_map/ppermute | solution.py:272
  65.5 1.5 %collective-permute-start.9 = (f32[256,384]{1,0:T(8,128)S(1)}, f32[256,384]{1,0:T(8,128)}, u32[]{:S(2)}, u32[]{:S(2)}) collective-permute-start(f32[256,384]{1,0:T(8,128)S(1)} %collective-permute-done.1.refs_8_), channel_id=1, source_target_pairs={{0,8},{4,12},{8,24},{12,28},{16,0},{20,4},{24,16},{28,20},{1,9},{5... | collective-permute-start | bytes 1179656 | tf_op jit(solution)/shard_map/ppermute | solution.py:282
  69.1 5.4 %collective-permute-done.9.refs_12_ = f32[256,384]{1,0:T(8,128)} collective-permute-done((f32[256,384]{1,0:T(8,128)S(1)}, f32[256,384]{1,0:T(8,128)}, u32[]{:S(2)}, u32[]{:S(2)}) %collective-permute-start.9) | collective-permute-done | bytes 393248 | tf_op jit(solution)/shard_map/ppermute | solution.py:282
  74.6 1.5 %collective-permute-start.13 = (f32[256,384]{1,0:T(8,128)}, f32[256,384]{1,0:T(8,128)}, u32[]{:S(2)}, u32[]{:S(2)}) collective-permute-start(f32[256,384]{1,0:T(8,128)} %collective-permute-done.9.refs_12_), channel_id=1, source_target_pairs={{0,8},{4,12},{8,24},{12,28},{16,0},{20,4},{24,16},{28,20},{1,9},{5... | collective-permute-start | bytes 1179656 | tf_op jit(solution)/shard_map/ppermute | solution.py:282
  77.1 0.7 convert_reduce_fusion.2.start_ref
  78.5 4.3 %collective-permute-done.13.refs_16_ = f32[256,384]{1,0:T(8,128)} collective-permute-done((f32[256,384]{1,0:T(8,128)}, f32[256,384]{1,0:T(8,128)}, u32[]{:S(2)}, u32[]{:S(2)}) %collective-permute-start.13) | collective-permute-done | bytes 393248 | tf_op jit(solution)/shard_map/ppermute | solution.py:282
  82.7 1.5 %collective-permute-done.15.refs_18_ = f32[256,384]{1,0:T(8,128)} collective-permute-done((f32[256,384]{1,0:T(8,128)}, f32[256,384]{1,0:T(8,128)}, u32[]{:S(2)}, u32[]{:S(2)}) %collective-permute-start.15) | collective-permute-done | bytes 393248 | tf_op jit(solution)/shard_map/ppermute | solution.py:282
  84.3 0.7 multiply_reduce_fusion.entry_ref
  85.1 4.9 %collective-permute-done.4.refs_3_ = f32[1536,128]{1,0:T(8,128)S(1)} collective-permute-done((f32[1536,128]{1,0:T(8,128)S(1)}, f32[1536,128]{1,0:T(8,128)S(1)}, u32[]{:S(2)}, u32[]{:S(2)}) %collective-permute-start.4) | collective-permute-done | bytes 786464 | tf_op jit(solution)/shard_map/ppermute | solution.py:289
  90.0 0.8 copy-done.3
  91.1 26.6 %front.1 = (f32[1536,3072]{1,0:T(8,128)}, f32[1536,128]{1,0:T(8,128)}) custom-call(s32[2]{0:T(128)} %pad_add_fusion.1.place_ref, s32[3,16]{1,0:T(4,128)} %multiply_reduce_fusion.entry_ref, s32[7]{0:T(128)} %convert_reduce_fusion.2.start_ref, f32[512,512]{1,0:T(8,128)} %d_ref.3, f32[24,8,128]{2,1,0:T(8,128)} %bitcast.24, f32[1536,3072]{1,0:T(8,128)} %trail_ref.1, ...), custom_call_target="tpu_custom_call" | custom-call | flops 16911433728 | bytes 44040192 | tf_op jit(solution)/shard_map/front/pallas_call | solution.py:167
  (72 shorter events, 7.7 us)
Async XLA Ops:
  0.6 21.8 %collective-permute-start = (f32[1536,128]{1,0:T(8,128)}, f32[1536,128]{1,0:T(8,128)S(1)}, u32[]{:S(2)}, u32[]{:S(2)}) collective-permute-start(f32[1536,128]{1,0:T(8,128)} %refs_0_.1), channel_id=1, source_target_pairs={{0,1},{1,3},{3,2},{2,0},{4,5},{5,7},{7,6},{6,4},{8,9},{9,11},{11,1... | collective-permute-start | bytes 2359304 | tf_op jit(solution)/shard_map/ppermute | solution.py:269
  3.7 14.3 %all-to-all-start = ((f32[4,384,128]{2,1,0:T(8,128)}), f32[4,384,128]{2,1,0:T(8,128)S(1)}, u32[]{:S(2)}, u32[]{:S(2)}) async-start(f32[4,384,128]{2,1,0:T(8,128)} %bitcast.22), calls=%async_computation | async-start | bytes 1572864 | tf_op jit(solution)/shard_map/all_to_all | solution.py:261
  22.5 67.5 %copy-start.1 = (f32[1536,128]{1,0:T(8,128)}, f32[1536,128]{1,0:T(8,128)S(1)}, u32[]{:S(2)}) copy-start(f32[1536,128]{1,0:T(8,128)S(1)} %collective-permute-done.refs_1_) | copy-start | bytes 2359300
  46.5 19.0 %collective-permute-start.3 = (f32[1536,128]{1,0:T(8,128)S(1)}, f32[1536,128]{1,0:T(8,128)S(1)}, u32[]{:S(2)}, u32[]{:S(2)}) collective-permute-start(f32[1536,128]{1,0:T(8,128)S(1)} %collective-permute-done.refs_1_), channel_id=1, source_target_pairs={{0,1},{1,3},{3,2},{2,0},{4,5},{5,7},{7,6},{6,4},{8,9},{9,11},{11,1... | collective-permute-start | bytes 2359304 | tf_op jit(solution)/shard_map/ppermute | solution.py:272
  49.7 11.9 %collective-permute-start.1 = (f32[256,384]{1,0:T(8,128)}, f32[256,384]{1,0:T(8,128)S(1)}, u32[]{:S(2)}, u32[]{:S(2)}) collective-permute-start(f32[256,384]{1,0:T(8,128)} %get-tuple-element.19.refs_4_), channel_id=1, source_target_pairs={{0,8},{4,12},{8,24},{12,28},{16,0},{20,4},{24,16},{28,20},{1,9},{5... | collective-permute-start | bytes 1179656 | tf_op jit(solution)/shard_map/ppermute | solution.py:282
  51.2 10.4 %collective-permute-start.2 = (f32[256,384]{1,0:T(8,128)}, f32[256,384]{1,0:T(8,128)}, u32[]{:S(2)}, u32[]{:S(2)}) collective-permute-start(f32[256,384]{1,0:T(8,128)} %get-tuple-element.20.refs_6_), channel_id=1, source_target_pairs={{0,16},{4,20},{8,0},{12,4},{16,24},{20,28},{24,8},{28,12},{1,17},{... | collective-permute-start | bytes 1179656 | tf_op jit(solution)/shard_map/ppermute | solution.py:282
  51.8 9.7 %all-to-all-start.2 = ((f32[8,3,8,128]{3,2,1,0:T(8,128)}), f32[8,3,8,128]{3,2,1,0:T(8,128)S(1)}, u32[]{:S(2)}, u32[]{:S(2)}) async-start(f32[8,3,8,128]{3,2,1,0:T(8,128)} %select_maximum_fusion), calls=%async_computation.2 | async-start | bytes 196608 | tf_op jit(solution)/shard_map/all_to_all | solution.py:220
  56.1 12.2 %collective-permute-start.5 = (f32[256,384]{1,0:T(8,128)}, f32[256,384]{1,0:T(8,128)S(1)}, u32[]{:S(2)}, u32[]{:S(2)}) collective-permute-start(f32[256,384]{1,0:T(8,128)} %get-tuple-element.19.refs_4_), channel_id=1, source_target_pairs={{0,4},{4,0},{8,12},{12,8},{16,20},{20,16},{24,28},{28,24},{1,5},{5... | collective-permute-start | bytes 1179656 | tf_op jit(solution)/shard_map/ppermute | solution.py:288
  56.6 12.5 %collective-permute-start.6 = (f32[256,384]{1,0:T(8,128)}, f32[256,384]{1,0:T(8,128)}, u32[]{:S(2)}, u32[]{:S(2)}) collective-permute-start(f32[256,384]{1,0:T(8,128)} %get-tuple-element.20.refs_6_), channel_id=1, source_target_pairs={{0,4},{4,0},{8,12},{12,8},{16,20},{20,16},{24,28},{28,24},{1,5},{5... | collective-permute-start | bytes 1179656 | tf_op jit(solution)/shard_map/ppermute | solution.py:288
  61.5 28.5 %copy-start = (f32[8,3,8,128]{3,2,1,0:T(8,128)}, f32[8,3,8,128]{3,2,1,0:T(8,128)S(1)}, u32[]{:S(2)}) copy-start(f32[8,3,8,128]{3,2,1,0:T(8,128)S(1)} %all-to-all-done.2) | copy-start | bytes 294916
  61.6 28.4 %copy-start.4 = (f32[256,384]{1,0:T(8,128)}, f32[256,384]{1,0:T(8,128)S(1)}, u32[]{:S(2)}) copy-start(f32[256,384]{1,0:T(8,128)S(1)} %collective-permute-done.1.refs_8_) | copy-start | bytes 1179652
  65.5 24.5 %copy-start.2 = (f32[1536,128]{1,0:T(8,128)}, f32[1536,128]{1,0:T(8,128)S(1)}, u32[]{:S(2)}) copy-start(f32[1536,128]{1,0:T(8,128)S(1)} %collective-permute-done.3.refs_2_) | copy-start | bytes 2359300
  65.5 9.1 %collective-permute-start.9 = (f32[256,384]{1,0:T(8,128)S(1)}, f32[256,384]{1,0:T(8,128)}, u32[]{:S(2)}, u32[]{:S(2)}) collective-permute-start(f32[256,384]{1,0:T(8,128)S(1)} %collective-permute-done.1.refs_8_), channel_id=1, source_target_pairs={{0,8},{4,12},{8,24},{12,28},{16,0},{20,4},{24,16},{28,20},{1,9},{5... | collective-permute-start | bytes 1179656 | tf_op jit(solution)/shard_map/ppermute | solution.py:282
  67.0 9.2 %collective-permute-start.11 = (f32[256,384]{1,0:T(8,128)}, f32[256,384]{1,0:T(8,128)}, u32[]{:S(2)}, u32[]{:S(2)}) collective-permute-start(f32[256,384]{1,0:T(8,128)} %collective-permute-done.2.refs_10_), channel_id=1, source_target_pairs={{0,16},{4,20},{8,0},{12,4},{16,24},{20,28},{24,8},{28,12},{1,17},{... | collective-permute-start | bytes 1179656 | tf_op jit(solution)/shard_map/ppermute | solution.py:282
  68.3 9.6 %collective-permute-start.7 = (f32[256,384]{1,0:T(8,128)S(1)}, f32[256,384]{1,0:T(8,128)}, u32[]{:S(2)}, u32[]{:S(2)}) collective-permute-start(f32[256,384]{1,0:T(8,128)S(1)} %collective-permute-done.1.refs_8_), channel_id=1, source_target_pairs={{0,4},{4,0},{8,12},{12,8},{16,20},{20,16},{24,28},{28,24},{1,5},{5... | collective-permute-start | bytes 1179656 | tf_op jit(solution)/shard_map/ppermute | solution.py:288
  68.4 9.6 %collective-permute-start.8 = (f32[256,384]{1,0:T(8,128)}, f32[256,384]{1,0:T(8,128)}, u32[]{:S(2)}, u32[]{:S(2)}) collective-permute-start(f32[256,384]{1,0:T(8,128)} %collective-permute-done.2.refs_10_), channel_id=1, source_target_pairs={{0,4},{4,0},{8,12},{12,8},{16,20},{20,16},{24,28},{28,24},{1,5},{5... | collective-permute-start | bytes 1179656 | tf_op jit(solution)/shard_map/ppermute | solution.py:288
  69.1 20.8 %collective-permute-start.4 = (f32[1536,128]{1,0:T(8,128)S(1)}, f32[1536,128]{1,0:T(8,128)S(1)}, u32[]{:S(2)}, u32[]{:S(2)}) collective-permute-start(f32[1536,128]{1,0:T(8,128)S(1)} %collective-permute-done.3.refs_2_), channel_id=1, source_target_pairs={{0,1},{1,3},{3,2},{2,0},{4,5},{5,7},{7,6},{6,4},{8,9},{9,11},{11,1... | collective-permute-start | bytes 2359304 | tf_op jit(solution)/shard_map/ppermute | solution.py:289
  74.6 8.2 %collective-permute-start.13 = (f32[256,384]{1,0:T(8,128)}, f32[256,384]{1,0:T(8,128)}, u32[]{:S(2)}, u32[]{:S(2)}) collective-permute-start(f32[256,384]{1,0:T(8,128)} %collective-permute-done.9.refs_12_), channel_id=1, source_target_pairs={{0,8},{4,12},{8,24},{12,28},{16,0},{20,4},{24,16},{28,20},{1,9},{5... | collective-permute-start | bytes 1179656 | tf_op jit(solution)/shard_map/ppermute | solution.py:282
  76.2 8.1 %collective-permute-start.15 = (f32[256,384]{1,0:T(8,128)}, f32[256,384]{1,0:T(8,128)}, u32[]{:S(2)}, u32[]{:S(2)}) collective-permute-start(f32[256,384]{1,0:T(8,128)} %collective-permute-done.11.refs_14_), channel_id=1, source_target_pairs={{0,16},{4,20},{8,0},{12,4},{16,24},{20,28},{24,8},{28,12},{1,17},{... | collective-permute-start | bytes 1179656 | tf_op jit(solution)/shard_map/ppermute | solution.py:282
  77.9 7.2 %collective-permute-start.10 = (f32[256,384]{1,0:T(8,128)}, f32[256,384]{1,0:T(8,128)S(1)}, u32[]{:S(2)}, u32[]{:S(2)}) collective-permute-start(f32[256,384]{1,0:T(8,128)} %collective-permute-done.9.refs_12_), channel_id=1, source_target_pairs={{0,4},{4,0},{8,12},{12,8},{16,20},{20,16},{24,28},{28,24},{1,5},{5... | collective-permute-start | bytes 1179656 | tf_op jit(solution)/shard_map/ppermute | solution.py:288
  78.0 7.1 %collective-permute-start.12 = (f32[256,384]{1,0:T(8,128)}, f32[256,384]{1,0:T(8,128)S(1)}, u32[]{:S(2)}, u32[]{:S(2)}) collective-permute-start(f32[256,384]{1,0:T(8,128)} %collective-permute-done.11.refs_14_), channel_id=1, source_target_pairs={{0,4},{4,0},{8,12},{12,8},{16,20},{20,16},{24,28},{28,24},{1,5},{5... | collective-permute-start | bytes 1179656 | tf_op jit(solution)/shard_map/ppermute | solution.py:288
  82.7 7.2 %collective-permute-start.14 = (f32[256,384]{1,0:T(8,128)}, f32[256,384]{1,0:T(8,128)S(1)}, u32[]{:S(2)}, u32[]{:S(2)}) collective-permute-start(f32[256,384]{1,0:T(8,128)} %collective-permute-done.13.refs_16_), channel_id=1, source_target_pairs={{0,4},{4,0},{8,12},{12,8},{16,20},{20,16},{24,28},{28,24},{1,5},{5... | collective-permute-start | bytes 1179656 | tf_op jit(solution)/shard_map/ppermute | solution.py:288
  84.3 5.7 %collective-permute-start.16 = (f32[256,384]{1,0:T(8,128)}, f32[256,384]{1,0:T(8,128)S(1)}, u32[]{:S(2)}, u32[]{:S(2)}) collective-permute-start(f32[256,384]{1,0:T(8,128)} %collective-permute-done.15.refs_18_), channel_id=1, source_target_pairs={{0,4},{4,0},{8,12},{12,8},{16,20},{20,16},{24,28},{28,24},{1,5},{5... | collective-permute-start | bytes 1179656 | tf_op jit(solution)/shard_map/ppermute | solution.py:288
  85.1 5.0 %copy-start.7 = (f32[256,384]{1,0:T(8,128)}, f32[256,384]{1,0:T(8,128)S(1)}, u32[]{:S(2)}) copy-start(f32[256,384]{1,0:T(8,128)S(1)} %collective-permute-done.12.refs_15_) | copy-start | bytes 1179652
  (5 other events, 8.8 us)

commit v9 on v8

--- a/solution.py
+++ b/solution.py
@@ -77,10 +77,11 @@
     part = width // 4
 
     def own_copies():
-        for n, s in enumerate(own_plan):
+        for n, (s, row) in enumerate(own_plan):
             source = ring_place(place_ref[1], s) if ringed else s
             lanes = pl.ds(pl.multiple_of(source * part, part), part)
-            yield pltpu.make_async_copy(own_pieces[n], own_stage.at[:, lanes], sem.at[n])
+            target = own_stage.at[pl.ds(row, own_pieces[n].shape[0]), lanes]
+            yield pltpu.make_async_copy(own_pieces[n], target, sem.at[n])
 
     def pair_copies():
         for n, (upper, steps, swap) in enumerate(plan):
@@ -247,8 +248,7 @@
     col_index = lax.axis_index("col")
     tile_cols = local_cols // TILE_COLS
     tiles_dev = (local_rows // TILE_ROWS) * tile_cols
-    bm = 768 if local_rows % 768 == 0 else local_rows
-    bn = 1024
+    bm, bn = local_rows, 512
     n_i, n_j = local_rows // bm, local_cols // bn
 
     row_index = lax.axis_index("row")
@@ -266,10 +266,15 @@
             axis_index_groups=[[0, 2, 4, 6], [1, 3, 5, 7]],
             tiled=True,
         )
-        spread, first, tiles = lax.optimization_barrier((spread, ring(panel), tiles))
+        first = ring(panel)
+        half = local_rows // 2
+        spread, upper, lower, tiles = lax.optimization_barrier(
+            (spread, first[:half], first[half:], tiles)
+        )
         wanted = lax.all_to_all(spread, "col", split_axis=0, concat_axis=0, tiled=True)
-        wanted, first, tiles = lax.optimization_barrier((wanted, first, tiles))
-        second = ring(first)
+        wanted, upper, lower, tiles = lax.optimization_barrier((wanted, upper, lower, tiles))
+        second = [ring(upper), ring(lower)]
+        third = [ring(x) for x in second]
         siblings = [(p, p ^ 1) for p in range(row_devices)]
         turns = [
             [(2 * c + m, 2 * step[c] + m) for c in range(4) for m in range(2)]
@@ -281,12 +286,15 @@
             if n > 0:
                 held = [lax.ppermute(x, "row", turn) for x, turn in zip(held, turns)]
             if n == 1:
-                *held, second = lax.optimization_barrier((*held, second))
+                *held, second[0], second[1] = lax.optimization_barrier((*held, *second))
+            if n == 2:
+                *held, third[0] = lax.optimization_barrier((*held, third[0]))
             for h, x in enumerate(held):
                 steps = n if h == 0 else -n
                 plan += [(h, steps, 0), (h, steps, 1)]
                 pieces += [x, lax.ppermute(x, "row", siblings)]
-        own = [panel, first, second, ring(second)]
+        own = [panel, first, *second, *third]
+        own_plan = [(0, 0), (1, 0), (2, 0), (2, half), (3, 0), (3, half)]
     else:
         whole = lax.all_gather(panel, "col", axis=0)
         column = lax.all_gather(panel, "row", axis=0, tiled=True)
@@ -294,6 +302,7 @@
         partner = lax.all_to_all(column, "col", split_axis=0, concat_axis=0, tiled=True)
         pieces, plan = pair_factor(diag_inverse, partner, 768), [(0, 0, 0), (1, 0, 0)]
         own = [whole[s] for s in range(col_devices)]
+        own_plan = [(s, 0) for s in range(col_devices)]
 
     agg, landing = exchange_tiles(tiles, tiles_dev)
     entries, starts = order_tiles(
@@ -307,7 +316,7 @@
         agg,
         trailing,
         own,
-        list(range(4)),
+        own_plan,
         pieces,
         plan,
         ringed,

time: 118 us -> 121 us (1.025)
  waiting for transfers between devices: 34.8 us -> 37.2 us
  starting transfers between devices: 18.4 us -> 20.3 us
    ppermute x3 -> x5, waiting for transfers between devices: 13.2 us -> 30.1 us  [the longest x2 18.5 us: per_device(): third = [ring(x) for x in second]]
    ppermute x6, waiting for transfers between devices: 11.4 us -> 0.18 us  [per_device(): held = [lax.ppermute(x, 'row', turn) for x, turn in zip(held, turns)]]
    all_to_all x1, waiting for transfers between devices: 5.28 us -> 0.01 us  [per_device(): lax.all_to_all(panel.reshape(4, quarter, part), 'row', split_axis=0, conc...]
    ppermute x3 -> x5, starting transfers between devices: 3.29 us -> 5.16 us  [the longest x1 3.08 us: per_device(): first = ring(panel)]
    ppermute x8, waiting for transfers between devices: 0.02 us -> 1.84 us  [per_device(): pieces += [x, lax.ppermute(x, 'row', siblings)]]
  transfers between devices with their start and end apart: 19 -> 21, of which waited for: 9 -> 10; matrix products, arithmetic and copies ran while one was open for 7% -> 7% of each run, Pallas kernels for 3% -> 2%
where the time goes in v9:
time: 121 us; the launch traced here: 120 us
  waiting for transfers between devices  37.2 us (31%)
  Pallas kernels  28.5 us (24%)
  blocking collectives  24.1 us (20%)
  starting transfers between devices  20.3 us (17%)
  other arithmetic  5.98 us (5%)
  local copies, waits for them, and re-layouts  3.41 us (3%)
    pallas_call x1, Pallas kernels, front(): pl.pallas_call(functools.partial(front_kernel, ringed, own_plan, plan), g...  25.5 us
    all_to_all x1, blocking collectives, per_device(): lax.all_to_all(spread, 'col', split_axis=0, concat_axis=0, tiled=True)  24.1 us
    ppermute x2, waiting for transfers between devices, per_device(): third = [ring(x) for x in second]  18.5 us
    ppermute x1, waiting for transfers between devices, per_device(): first = ring(panel)  9.76 us
    ppermute x6, starting transfers between devices, per_device(): held = [lax.ppermute(x, 'row', turn) for x, turn in zip(held, turns)]  6.18 us
    all_to_all x1, waiting for transfers between devices, exchange_tiles(): got = lax.all_to_all(send, 'row', split_axis=0, concat_axis=0, tiled=True)  5.1 us
    all_to_all x1, starting transfers between devices, exchange_tiles(): got = lax.all_to_all(send, 'row', split_axis=0, concat_axis=0, tiled=True)  3.73 us
    all_to_all x1, starting transfers between devices, per_device(): lax.all_to_all(panel.reshape(4, quarter, part), 'row', split_axis=0, conc...  3.72 us
  transfers between devices with their start and end apart: 21, of which 10 were waited for; matrix products, arithmetic and copies ran while one was open for 7% of the time, Pallas kernels for 2%

profile of v9, /device:TPU:0, one launch (start us, length us, event | category | flops | bytes accessed | tf_op | source)
XLA Modules:
  0.0 120.3 jit_solution(2948225709445424643)
XLA Ops:
  0.6 3.1 %collective-permute-start = (f32[1536,128]{1,0:T(8,128)}, f32[1536,128]{1,0:T(8,128)S(1)}, u32[]{:S(2)}, u32[]{:S(2)}) collective-permute-start(f32[1536,128]{1,0:T(8,128)} %refs_0_.1), channel_id=1, source_target_pairs={{0,1},{1,3},{3,2},{2,0},{4,5},{5,7},{7,6},{6,4},{8,9},{9,11},{11,1... | collective-permute-start | bytes 2359304 | tf_op jit(solution)/shard_map/ppermute | solution.py:269
  3.7 3.7 %all-to-all-start = ((f32[4,384,128]{2,1,0:T(8,128)}), f32[4,384,128]{2,1,0:T(8,128)S(1)}, u32[]{:S(2)}, u32[]{:S(2)}) async-start(f32[4,384,128]{2,1,0:T(8,128)} %bitcast.22), calls=%async_computation | async-start | bytes 1572864 | tf_op jit(solution)/shard_map/all_to_all | solution.py:261
  7.4 0.9 convert_reduce_fusion.1
  8.3 0.7 multiply_add_fusion
  9.0 0.7 add_bitcast_fusion
  9.9 0.7 fusion.6
  10.5 1.5 %scatter_fusion = f32[16,8,128]{2,1,0:T(8,128)S(1)} fusion(f32[16,8,128]{2,1,0:T(8,128)S(1)} %broadcast_in_dim.18, s32[12]{0:T(128)S(1)} %fusion.6, f32[12,8,128]{2,1,0:T(8,128)} %bitcast.25), kind=kCustom, calls=%fused_computation | custom fusion | bytes 147504 | tf_op jit(solution)/shard_map/scatter | solution.py:213
  12.1 0.6 select_maximum_fusion
  12.7 9.8 %collective-permute-done.refs_1_ = f32[1536,128]{1,0:T(8,128)S(1)} collective-permute-done((f32[1536,128]{1,0:T(8,128)}, f32[1536,128]{1,0:T(8,128)S(1)}, u32[]{:S(2)}, u32[]{:S(2)}) %collective-permute-start) | collective-permute-done | bytes 786464 | tf_op jit(solution)/shard_map/ppermute | solution.py:269
  22.5 24.1 %all_to_all.15.panel_ref = f32[4,384,128]{2,1,0:T(8,128)} all-to-all(f32[4,384,128]{2,1,0:T(8,128)S(1)} %all-to-all-done), channel_id=1, replica_groups=mesh['row'=8,'col'=4] {'col'}, dimensions={0} | all-to-all | bytes 1572864 | tf_op jit(solution)/shard_map/all_to_all | solution.py:274
  46.8 1.8 %collective-permute-start.4 = (f32[768,128]{1,0:T(8,128)S(1)}, f32[768,128]{1,0:T(8,128)S(1)}, u32[]{:S(2)}, u32[]{:S(2)}) collective-permute-start(f32[768,128]{1,0:T(8,128)S(1)} %get-tuple-element.28), channel_id=1, source_target_pairs={{0,1},{1,3},{3,2},{2,0},{4,5},{5,7},{7,6},{6,4},{8,9},{9,11},{11,1... | collective-permute-start | bytes 1179656 | tf_op jit(solution)/shard_map/ppermute | solution.py:276
  48.6 3.0 %pair_factor.1 = (f32[256,384]{1,0:T(8,128)}, f32[256,384]{1,0:T(8,128)}) custom-call(f32[512,512]{1,0:T(8,128)} %d_ref.3, f32[4,384,128]{2,1,0:T(8,128)} %all_to_all.15.panel_ref), custom_call_target="tpu_custom_call" | custom-call | flops 603979776 | bytes 1572864 | tf_op jit(solution)/shard_map/pair_factor/pallas_call | solution.py:48
  51.6 1.5 %collective-permute-start.1 = (f32[256,384]{1,0:T(8,128)}, f32[256,384]{1,0:T(8,128)S(1)}, u32[]{:S(2)}, u32[]{:S(2)}) collective-permute-start(f32[256,384]{1,0:T(8,128)} %get-tuple-element.25.refs_6_), channel_id=1, source_target_pairs={{0,8},{4,12},{8,24},{12,28},{16,0},{20,4},{24,16},{28,20},{1,9},{5... | collective-permute-start | bytes 1179656 | tf_op jit(solution)/shard_map/ppermute | solution.py:287
  53.6 3.7 %all-to-all-start.2 = ((f32[8,3,8,128]{3,2,1,0:T(8,128)}), f32[8,3,8,128]{3,2,1,0:T(8,128)S(1)}, u32[]{:S(2)}, u32[]{:S(2)}) async-start(f32[8,3,8,128]{3,2,1,0:T(8,128)} %select_maximum_fusion), calls=%async_computation.2 | async-start | bytes 196608 | tf_op jit(solution)/shard_map/all_to_all | solution.py:221
  57.4 0.6 pad_add_fusion.1.place_ref
  58.5 5.1 %all-to-all-done.2 = f32[8,3,8,128]{3,2,1,0:T(8,128)S(1)} async-done(((f32[8,3,8,128]{3,2,1,0:T(8,128)}), f32[8,3,8,128]{3,2,1,0:T(8,128)S(1)}, u32[]{:S(2)}, u32[]{:S(2)}) %all-to-all-start.2) | async-done | bytes 98336 | tf_op jit(solution)/shard_map/all_to_all | solution.py:221
  63.8 1.8 %collective-permute-done.4.refs_3_ = f32[768,128]{1,0:T(8,128)S(1)} collective-permute-done((f32[768,128]{1,0:T(8,128)S(1)}, f32[768,128]{1,0:T(8,128)S(1)}, u32[]{:S(2)}, u32[]{:S(2)}) %collective-permute-start.4) | collective-permute-done | bytes 393248 | tf_op jit(solution)/shard_map/ppermute | solution.py:276
  65.6 1.5 %collective-permute-start.5 = (f32[256,384]{1,0:T(8,128)S(1)}, f32[256,384]{1,0:T(8,128)S(1)}, u32[]{:S(2)}, u32[]{:S(2)}) collective-permute-start(f32[256,384]{1,0:T(8,128)S(1)} %collective-permute-done.1.refs_10_), channel_id=1, source_target_pairs={{0,8},{4,12},{8,24},{12,28},{16,0},{20,4},{24,16},{28,20},{1,9},{5... | collective-permute-start | bytes 1179656 | tf_op jit(solution)/shard_map/ppermute | solution.py:287
  68.4 9.4 %collective-permute-done.7.refs_4_ = f32[768,128]{1,0:T(8,128)} collective-permute-done((f32[768,128]{1,0:T(8,128)S(1)}, f32[768,128]{1,0:T(8,128)}, u32[]{:S(2)}, u32[]{:S(2)}) %collective-permute-start.7) | collective-permute-done | bytes 393248 | tf_op jit(solution)/shard_map/ppermute | solution.py:277
  77.9 1.7 %collective-permute-start.15 = (f32[256,384]{1,0:T(8,128)S(1)}, f32[256,384]{1,0:T(8,128)}, u32[]{:S(2)}, u32[]{:S(2)}) collective-permute-start(f32[256,384]{1,0:T(8,128)S(1)} %collective-permute-done.5.refs_14_), channel_id=1, source_target_pairs={{0,8},{4,12},{8,24},{12,28},{16,0},{20,4},{24,16},{28,20},{1,9},{5... | collective-permute-start | bytes 1179656 | tf_op jit(solution)/shard_map/ppermute | solution.py:287
  80.0 0.7 convert_reduce_fusion.2.start_ref
  81.3 9.1 %collective-permute-done.8.refs_5_ = f32[768,128]{1,0:T(8,128)} collective-permute-done((f32[768,128]{1,0:T(8,128)S(1)}, f32[768,128]{1,0:T(8,128)}, u32[]{:S(2)}, u32[]{:S(2)}) %collective-permute-start.8) | collective-permute-done | bytes 393248 | tf_op jit(solution)/shard_map/ppermute | solution.py:277
  91.4 0.7 multiply_reduce_fusion.entry_ref
  94.8 25.5 %front.1 = (f32[1536,3072]{1,0:T(8,128)}, f32[1536,128]{1,0:T(8,128)}) custom-call(s32[2]{0:T(128)} %pad_add_fusion.1.place_ref, s32[3,16]{1,0:T(4,128)} %multiply_reduce_fusion.entry_ref, s32[7]{0:T(128)} %convert_reduce_fusion.2.start_ref, f32[512,512]{1,0:T(8,128)} %d_ref.3, f32[24,8,128]{2,1,0:T(8,128)} %bitcast.24, f32[1536,3072]{1,0:T(8,128)} %trail_ref.1, ...), custom_call_target="tpu_custom_call" | custom-call | flops 16911433728 | bytes 44040192 | tf_op jit(solution)/shard_map/front/pallas_call | solution.py:168
  (83 shorter events, 7.5 us)
Async XLA Ops:
  0.6 21.8 %collective-permute-start = (f32[1536,128]{1,0:T(8,128)}, f32[1536,128]{1,0:T(8,128)S(1)}, u32[]{:S(2)}, u32[]{:S(2)}) collective-permute-start(f32[1536,128]{1,0:T(8,128)} %refs_0_.1), channel_id=1, source_target_pairs={{0,1},{1,3},{3,2},{2,0},{4,5},{5,7},{7,6},{6,4},{8,9},{9,11},{11,1... | collective-permute-start | bytes 2359304 | tf_op jit(solution)/shard_map/ppermute | solution.py:269
  3.7 18.8 %all-to-all-start = ((f32[4,384,128]{2,1,0:T(8,128)}), f32[4,384,128]{2,1,0:T(8,128)S(1)}, u32[]{:S(2)}, u32[]{:S(2)}) async-start(f32[4,384,128]{2,1,0:T(8,128)} %bitcast.22), calls=%async_computation | async-start | bytes 1572864 | tf_op jit(solution)/shard_map/all_to_all | solution.py:261
  22.5 71.5 %copy-start = (f32[1536,128]{1,0:T(8,128)}, f32[1536,128]{1,0:T(8,128)S(1)}, u32[]{:S(2)}) copy-start(f32[1536,128]{1,0:T(8,128)S(1)} %collective-permute-done.refs_1_) | copy-start | bytes 2359300
  46.6 17.1 %collective-permute-start.3 = (f32[768,128]{1,0:T(8,128)S(1)}, f32[768,128]{1,0:T(8,128)S(1)}, u32[]{:S(2)}, u32[]{:S(2)}) collective-permute-start(f32[768,128]{1,0:T(8,128)S(1)} %get-tuple-element.27), channel_id=1, source_target_pairs={{0,1},{1,3},{3,2},{2,0},{4,5},{5,7},{7,6},{6,4},{8,9},{9,11},{11,1... | collective-permute-start | bytes 1179656 | tf_op jit(solution)/shard_map/ppermute | solution.py:276
  46.8 18.8 %collective-permute-start.4 = (f32[768,128]{1,0:T(8,128)S(1)}, f32[768,128]{1,0:T(8,128)S(1)}, u32[]{:S(2)}, u32[]{:S(2)}) collective-permute-start(f32[768,128]{1,0:T(8,128)S(1)} %get-tuple-element.28), channel_id=1, source_target_pairs={{0,1},{1,3},{3,2},{2,0},{4,5},{5,7},{7,6},{6,4},{8,9},{9,11},{11,1... | collective-permute-start | bytes 1179656 | tf_op jit(solution)/shard_map/ppermute | solution.py:276
  51.6 14.0 %collective-permute-start.1 = (f32[256,384]{1,0:T(8,128)}, f32[256,384]{1,0:T(8,128)S(1)}, u32[]{:S(2)}, u32[]{:S(2)}) collective-permute-start(f32[256,384]{1,0:T(8,128)} %get-tuple-element.25.refs_6_), channel_id=1, source_target_pairs={{0,8},{4,12},{8,24},{12,28},{16,0},{20,4},{24,16},{28,20},{1,9},{5... | collective-permute-start | bytes 1179656 | tf_op jit(solution)/shard_map/ppermute | solution.py:287
  53.1 12.5 %collective-permute-start.2 = (f32[256,384]{1,0:T(8,128)}, f32[256,384]{1,0:T(8,128)S(1)}, u32[]{:S(2)}, u32[]{:S(2)}) collective-permute-start(f32[256,384]{1,0:T(8,128)} %get-tuple-element.26.refs_8_), channel_id=1, source_target_pairs={{0,16},{4,20},{8,0},{12,4},{16,24},{20,28},{24,8},{28,12},{1,17},{... | collective-permute-start | bytes 1179656 | tf_op jit(solution)/shard_map/ppermute | solution.py:287
  53.6 9.9 %all-to-all-start.2 = ((f32[8,3,8,128]{3,2,1,0:T(8,128)}), f32[8,3,8,128]{3,2,1,0:T(8,128)S(1)}, u32[]{:S(2)}, u32[]{:S(2)}) async-start(f32[8,3,8,128]{3,2,1,0:T(8,128)} %select_maximum_fusion), calls=%async_computation.2 | async-start | bytes 196608 | tf_op jit(solution)/shard_map/all_to_all | solution.py:221
  58.0 21.7 %collective-permute-start.9 = (f32[256,384]{1,0:T(8,128)}, f32[256,384]{1,0:T(8,128)}, u32[]{:S(2)}, u32[]{:S(2)}) collective-permute-start(f32[256,384]{1,0:T(8,128)} %get-tuple-element.25.refs_6_), channel_id=1, source_target_pairs={{0,4},{4,0},{8,12},{12,8},{16,20},{20,16},{24,28},{28,24},{1,5},{5... | collective-permute-start | bytes 1179656 | tf_op jit(solution)/shard_map/ppermute | solution.py:295
  63.6 30.4 %copy-start.1 = (f32[8,3,8,128]{3,2,1,0:T(8,128)}, f32[8,3,8,128]{3,2,1,0:T(8,128)S(1)}, u32[]{:S(2)}) copy-start(f32[8,3,8,128]{3,2,1,0:T(8,128)S(1)} %all-to-all-done.2) | copy-start | bytes 294916
  63.7 30.3 %copy-start.2 = (f32[768,128]{1,0:T(8,128)}, f32[768,128]{1,0:T(8,128)S(1)}, u32[]{:S(2)}) copy-start(f32[768,128]{1,0:T(8,128)S(1)} %collective-permute-done.3.refs_2_) | copy-start | bytes 1179652
  63.7 17.5 %collective-permute-start.10 = (f32[256,384]{1,0:T(8,128)}, f32[256,384]{1,0:T(8,128)S(1)}, u32[]{:S(2)}, u32[]{:S(2)}) collective-permute-start(f32[256,384]{1,0:T(8,128)} %get-tuple-element.26.refs_8_), channel_id=1, source_target_pairs={{0,4},{4,0},{8,12},{12,8},{16,20},{20,16},{24,28},{28,24},{1,5},{5... | collective-permute-start | bytes 1179656 | tf_op jit(solution)/shard_map/ppermute | solution.py:295
  65.6 12.3 %collective-permute-start.5 = (f32[256,384]{1,0:T(8,128)S(1)}, f32[256,384]{1,0:T(8,128)S(1)}, u32[]{:S(2)}, u32[]{:S(2)}) collective-permute-start(f32[256,384]{1,0:T(8,128)S(1)} %collective-permute-done.1.refs_10_), channel_id=1, source_target_pairs={{0,8},{4,12},{8,24},{12,28},{16,0},{20,4},{24,16},{28,20},{1,9},{5... | collective-permute-start | bytes 1179656 | tf_op jit(solution)/shard_map/ppermute | solution.py:287
  67.1 10.8 %collective-permute-start.6 = (f32[256,384]{1,0:T(8,128)S(1)}, f32[256,384]{1,0:T(8,128)}, u32[]{:S(2)}, u32[]{:S(2)}) collective-permute-start(f32[256,384]{1,0:T(8,128)S(1)} %collective-permute-done.2.refs_12_), channel_id=1, source_target_pairs={{0,16},{4,20},{8,0},{12,4},{16,24},{20,28},{24,8},{28,12},{1,17},{... | collective-permute-start | bytes 1179656 | tf_op jit(solution)/shard_map/ppermute | solution.py:287
  67.7 10.2 %collective-permute-start.7 = (f32[768,128]{1,0:T(8,128)S(1)}, f32[768,128]{1,0:T(8,128)}, u32[]{:S(2)}, u32[]{:S(2)}) collective-permute-start(f32[768,128]{1,0:T(8,128)S(1)} %collective-permute-done.3.refs_2_), channel_id=1, source_target_pairs={{0,1},{1,3},{3,2},{2,0},{4,5},{5,7},{7,6},{6,4},{8,9},{9,11},{11,1... | collective-permute-start | bytes 1179656 | tf_op jit(solution)/shard_map/ppermute | solution.py:277
  77.8 12.5 %collective-permute-start.11 = (f32[256,384]{1,0:T(8,128)S(1)}, f32[256,384]{1,0:T(8,128)}, u32[]{:S(2)}, u32[]{:S(2)}) collective-permute-start(f32[256,384]{1,0:T(8,128)S(1)} %collective-permute-done.1.refs_10_), channel_id=1, source_target_pairs={{0,4},{4,0},{8,12},{12,8},{16,20},{20,16},{24,28},{28,24},{1,5},{5... | collective-permute-start | bytes 1179656 | tf_op jit(solution)/shard_map/ppermute | solution.py:295
  77.8 12.5 %collective-permute-start.8 = (f32[768,128]{1,0:T(8,128)S(1)}, f32[768,128]{1,0:T(8,128)}, u32[]{:S(2)}, u32[]{:S(2)}) collective-permute-start(f32[768,128]{1,0:T(8,128)S(1)} %collective-permute-done.4.refs_3_), channel_id=1, source_target_pairs={{0,1},{1,3},{3,2},{2,0},{4,5},{5,7},{7,6},{6,4},{8,9},{9,11},{11,1... | collective-permute-start | bytes 1179656 | tf_op jit(solution)/shard_map/ppermute | solution.py:277
  77.9 13.0 %collective-permute-start.15 = (f32[256,384]{1,0:T(8,128)S(1)}, f32[256,384]{1,0:T(8,128)}, u32[]{:S(2)}, u32[]{:S(2)}) collective-permute-start(f32[256,384]{1,0:T(8,128)S(1)} %collective-permute-done.5.refs_14_), channel_id=1, source_target_pairs={{0,8},{4,12},{8,24},{12,28},{16,0},{20,4},{24,16},{28,20},{1,9},{5... | collective-permute-start | bytes 1179656 | tf_op jit(solution)/shard_map/ppermute | solution.py:287
  79.6 11.5 %collective-permute-start.17 = (f32[256,384]{1,0:T(8,128)}, f32[256,384]{1,0:T(8,128)}, u32[]{:S(2)}, u32[]{:S(2)}) collective-permute-start(f32[256,384]{1,0:T(8,128)} %collective-permute-done.6.refs_16_), channel_id=1, source_target_pairs={{0,16},{4,20},{8,0},{12,4},{16,24},{20,28},{24,8},{28,12},{1,17},{... | collective-permute-start | bytes 1179656 | tf_op jit(solution)/shard_map/ppermute | solution.py:287
  81.2 11.0 %collective-permute-start.12 = (f32[256,384]{1,0:T(8,128)S(1)}, f32[256,384]{1,0:T(8,128)S(1)}, u32[]{:S(2)}, u32[]{:S(2)}) collective-permute-start(f32[256,384]{1,0:T(8,128)S(1)} %collective-permute-done.2.refs_12_), channel_id=1, source_target_pairs={{0,4},{4,0},{8,12},{12,8},{16,20},{20,16},{24,28},{28,24},{1,5},{5... | collective-permute-start | bytes 1179656 | tf_op jit(solution)/shard_map/ppermute | solution.py:295
  90.4 2.2 %collective-permute-start.13 = (f32[256,384]{1,0:T(8,128)S(1)}, f32[256,384]{1,0:T(8,128)S(1)}, u32[]{:S(2)}, u32[]{:S(2)}) collective-permute-start(f32[256,384]{1,0:T(8,128)S(1)} %collective-permute-done.5.refs_14_), channel_id=1, source_target_pairs={{0,4},{4,0},{8,12},{12,8},{16,20},{20,16},{24,28},{28,24},{1,5},{5... | collective-permute-start | bytes 1179656 | tf_op jit(solution)/shard_map/ppermute | solution.py:295
  90.4 2.5 %collective-permute-start.14 = (f32[256,384]{1,0:T(8,128)}, f32[256,384]{1,0:T(8,128)S(1)}, u32[]{:S(2)}, u32[]{:S(2)}) collective-permute-start(f32[256,384]{1,0:T(8,128)} %collective-permute-done.6.refs_16_), channel_id=1, source_target_pairs={{0,4},{4,0},{8,12},{12,8},{16,20},{20,16},{24,28},{28,24},{1,5},{5... | collective-permute-start | bytes 1179656 | tf_op jit(solution)/shard_map/ppermute | solution.py:295
  90.9 2.5 %collective-permute-start.16 = (f32[256,384]{1,0:T(8,128)}, f32[256,384]{1,0:T(8,128)S(1)}, u32[]{:S(2)}, u32[]{:S(2)}) collective-permute-start(f32[256,384]{1,0:T(8,128)} %collective-permute-done.15.refs_18_), channel_id=1, source_target_pairs={{0,4},{4,0},{8,12},{12,8},{16,20},{20,16},{24,28},{28,24},{1,5},{5... | collective-permute-start | bytes 1179656 | tf_op jit(solution)/shard_map/ppermute | solution.py:295
  91.1 2.9 %collective-permute-start.18 = (f32[256,384]{1,0:T(8,128)}, f32[256,384]{1,0:T(8,128)S(1)}, u32[]{:S(2)}, u32[]{:S(2)}) collective-permute-start(f32[256,384]{1,0:T(8,128)} %collective-permute-done.17.refs_20_), channel_id=1, source_target_pairs={{0,4},{4,0},{8,12},{12,8},{16,20},{20,16},{24,28},{28,24},{1,5},{5... | collective-permute-start | bytes 1179656 | tf_op jit(solution)/shard_map/ppermute | solution.py:295
  (10 other events, 120.6 us)

commit v10 on v8

--- a/solution.py
+++ b/solution.py
@@ -247,8 +247,7 @@
     col_index = lax.axis_index("col")
     tile_cols = local_cols // TILE_COLS
     tiles_dev = (local_rows // TILE_ROWS) * tile_cols
-    bm = 768 if local_rows % 768 == 0 else local_rows
-    bn = 1024
+    bm, bn = local_rows, 512
     n_i, n_j = local_rows // bm, local_cols // bn
 
     row_index = lax.axis_index("row")
@@ -268,7 +267,8 @@
         )
         spread, first, tiles = lax.optimization_barrier((spread, ring(panel), tiles))
         wanted = lax.all_to_all(spread, "col", split_axis=0, concat_axis=0, tiled=True)
-        wanted, first, tiles = lax.optimization_barrier((wanted, first, tiles))
+        wanted, first, mine, tiles = lax.optimization_barrier((wanted, first, panel, tiles))
+        third = lax.ppermute(mine, "col", list(PREV.items()))
         second = ring(first)
         siblings = [(p, p ^ 1) for p in range(row_devices)]
         turns = [
@@ -281,12 +281,12 @@
             if n > 0:
                 held = [lax.ppermute(x, "row", turn) for x, turn in zip(held, turns)]
             if n == 1:
-                *held, second = lax.optimization_barrier((*held, second))
+                *held, third = lax.optimization_barrier((*held, third))
             for h, x in enumerate(held):
                 steps = n if h == 0 else -n
                 plan += [(h, steps, 0), (h, steps, 1)]
                 pieces += [x, lax.ppermute(x, "row", siblings)]
-        own = [panel, first, second, ring(second)]
+        own = [panel, first, second, third]
     else:
         whole = lax.all_gather(panel, "col", axis=0)
         column = lax.all_gather(panel, "row", axis=0, tiled=True)

time: 118 us -> 113 us (0.958)
  waiting for transfers between devices: 34.8 us -> 30.4 us
  starting transfers between devices: 18.4 us -> 19.6 us
    ppermute x1, waiting for transfers between devices: 4.89 us -> 1.4 us  [per_device(): third = lax.ppermute(mine, 'col', list(PREV.items()))]
    ppermute x6, waiting for transfers between devices: 11.4 us -> 8.58 us  [per_device(): held = [lax.ppermute(x, 'row', turn) for x, turn in zip(held, turns)]]
    ppermute x1, starting transfers between devices: 0.21 us -> 1.66 us  [per_device(): second = ring(first)]
  transfers between devices with their start and end apart: 19 -> 19, of which waited for: 9 -> 9; matrix products, arithmetic and copies ran while one was open for 7% -> 8% of each run, Pallas kernels for 3% -> 3%
where the time goes in v10:
time: 113 us
  waiting for transfers between devices  30.4 us (27%)
  Pallas kernels  28.5 us (25%)
  blocking collectives  24 us (21%)
  starting transfers between devices  19.6 us (17%)
  other arithmetic  6.02 us (5%)
  local copies, waits for them, and re-layouts  3.36 us (3%)
    pallas_call x1, Pallas kernels, front(): pl.pallas_call(functools.partial(front_kernel, ringed, own_plan, plan), g...  25.5 us
    all_to_all x1, blocking collectives, per_device(): lax.all_to_all(spread, 'col', split_axis=0, concat_axis=0, tiled=True)  24 us
    ppermute x6, waiting for transfers between devices, per_device(): held = [lax.ppermute(x, 'row', turn) for x, turn in zip(held, turns)]  8.58 us
    ppermute x6, starting transfers between devices, per_device(): held = [lax.ppermute(x, 'row', turn) for x, turn in zip(held, turns)]  6.08 us
    all_to_all x1, waiting for transfers between devices, per_device(): lax.all_to_all(panel.reshape(4, quarter, part), 'row', split_axis=0, conc...  5.28 us
    all_to_all x1, waiting for transfers between devices, exchange_tiles(): got = lax.all_to_all(send, 'row', split_axis=0, concat_axis=0, tiled=True)  4.99 us
    ppermute x1, waiting for transfers between devices, per_device(): second = ring(first)  4.55 us
    ppermute x1, waiting for transfers between devices, per_device(): ring(panel)  4.47 us
  transfers between devices with their start and end apart: 19, of which 9 were waited for; matrix products, arithmetic and copies ran while one was open for 8% of the time, Pallas kernels for 3%

profile of v10, /device:TPU:0, one launch (start us, length us, event | category | flops | bytes accessed | tf_op | source)
XLA Modules:
  0.0 112.8 jit_solution(8558452010405252049)
XLA Ops:
  0.6 3.1 %collective-permute-start = (f32[1536,128]{1,0:T(8,128)}, f32[1536,128]{1,0:T(8,128)S(1)}, u32[]{:S(2)}, u32[]{:S(2)}) collective-permute-start(f32[1536,128]{1,0:T(8,128)} %refs_0_.1), channel_id=1, source_target_pairs={{0,1},{1,3},{3,2},{2,0},{4,5},{5,7},{7,6},{6,4},{8,9},{9,11},{11,1... | collective-permute-start | bytes 2359304 | tf_op jit(solution)/shard_map/ppermute | solution.py:268
  3.7 3.7 %all-to-all-start = ((f32[4,384,128]{2,1,0:T(8,128)}), f32[4,384,128]{2,1,0:T(8,128)S(1)}, u32[]{:S(2)}, u32[]{:S(2)}) async-start(f32[4,384,128]{2,1,0:T(8,128)} %bitcast.22), calls=%async_computation | async-start | bytes 1572864 | tf_op jit(solution)/shard_map/all_to_all | solution.py:260
  7.4 0.9 convert_reduce_fusion.1
  9.9 0.7 fusion.6
  10.5 1.5 %scatter_fusion = f32[16,8,128]{2,1,0:T(8,128)S(1)} fusion(f32[16,8,128]{2,1,0:T(8,128)S(1)} %broadcast_in_dim.18, s32[12]{0:T(128)S(1)} %fusion.6, f32[12,8,128]{2,1,0:T(8,128)} %bitcast.25), kind=kCustom, calls=%fused_computation | custom fusion | bytes 147504 | tf_op jit(solution)/shard_map/scatter | solution.py:212
  12.7 5.3 %all-to-all-done = f32[4,384,128]{2,1,0:T(8,128)S(1)} async-done(((f32[4,384,128]{2,1,0:T(8,128)}), f32[4,384,128]{2,1,0:T(8,128)S(1)}, u32[]{:S(2)}, u32[]{:S(2)}) %all-to-all-start) | async-done | bytes 786464 | tf_op jit(solution)/shard_map/all_to_all | solution.py:260
  18.0 4.5 %collective-permute-done.refs_1_ = f32[1536,128]{1,0:T(8,128)S(1)} collective-permute-done((f32[1536,128]{1,0:T(8,128)}, f32[1536,128]{1,0:T(8,128)S(1)}, u32[]{:S(2)}, u32[]{:S(2)}) %collective-permute-start) | collective-permute-done | bytes 786464 | tf_op jit(solution)/shard_map/ppermute | solution.py:268
  22.5 24.0 %all_to_all.15.panel_ref = f32[4,384,128]{2,1,0:T(8,128)} all-to-all(f32[4,384,128]{2,1,0:T(8,128)S(1)} %all-to-all-done), channel_id=1, replica_groups=mesh['row'=8,'col'=4] {'col'}, dimensions={0} | all-to-all | bytes 1572864 | tf_op jit(solution)/shard_map/all_to_all | solution.py:269
  46.7 3.0 %pair_factor.1 = (f32[256,384]{1,0:T(8,128)}, f32[256,384]{1,0:T(8,128)}) custom-call(f32[512,512]{1,0:T(8,128)} %d_ref.3, f32[4,384,128]{2,1,0:T(8,128)} %all_to_all.15.panel_ref), custom_call_target="tpu_custom_call" | custom-call | flops 603979776 | bytes 1572864 | tf_op jit(solution)/shard_map/pair_factor/pallas_call | solution.py:48
  49.7 1.5 %collective-permute-start.2 = (f32[256,384]{1,0:T(8,128)}, f32[256,384]{1,0:T(8,128)S(1)}, u32[]{:S(2)}, u32[]{:S(2)}) collective-permute-start(f32[256,384]{1,0:T(8,128)} %get-tuple-element.20.refs_4_), channel_id=1, source_target_pairs={{0,8},{4,12},{8,24},{12,28},{16,0},{20,4},{24,16},{28,20},{1,9},{5... | collective-permute-start | bytes 1179656 | tf_op jit(solution)/shard_map/ppermute | solution.py:282
  51.8 3.7 %all-to-all-start.2 = ((f32[8,3,8,128]{3,2,1,0:T(8,128)}), f32[8,3,8,128]{3,2,1,0:T(8,128)S(1)}, u32[]{:S(2)}, u32[]{:S(2)}) async-start(f32[8,3,8,128]{3,2,1,0:T(8,128)} %select_maximum_fusion), calls=%async_computation.2 | async-start | bytes 196608 | tf_op jit(solution)/shard_map/all_to_all | solution.py:220
  56.6 5.0 %all-to-all-done.2 = f32[8,3,8,128]{3,2,1,0:T(8,128)S(1)} async-done(((f32[8,3,8,128]{3,2,1,0:T(8,128)}), f32[8,3,8,128]{3,2,1,0:T(8,128)S(1)}, u32[]{:S(2)}, u32[]{:S(2)}) %all-to-all-start.2) | async-done | bytes 98336 | tf_op jit(solution)/shard_map/all_to_all | solution.py:220
  61.7 1.7 %collective-permute-start.1 = (f32[1536,128]{1,0:T(8,128)S(1)}, f32[1536,128]{1,0:T(8,128)S(1)}, u32[]{:S(2)}, u32[]{:S(2)}) collective-permute-start(f32[1536,128]{1,0:T(8,128)S(1)} %collective-permute-done.refs_1_), channel_id=1, source_target_pairs={{0,1},{1,3},{3,2},{2,0},{4,5},{5,7},{7,6},{6,4},{8,9},{9,11},{11,1... | collective-permute-start | bytes 2359304 | tf_op jit(solution)/shard_map/ppermute | solution.py:272
  63.4 1.4 %collective-permute-done.4.refs_3_ = f32[1536,128]{1,0:T(8,128)S(1)} collective-permute-done((f32[1536,128]{1,0:T(8,128)}, f32[1536,128]{1,0:T(8,128)S(1)}, u32[]{:S(2)}, u32[]{:S(2)}) %collective-permute-start.4) | collective-permute-done | bytes 786464 | tf_op jit(solution)/shard_map/ppermute | solution.py:271
  64.8 1.5 %collective-permute-start.9 = (f32[256,384]{1,0:T(8,128)S(1)}, f32[256,384]{1,0:T(8,128)}, u32[]{:S(2)}, u32[]{:S(2)}) collective-permute-start(f32[256,384]{1,0:T(8,128)S(1)} %collective-permute-done.2.refs_8_), channel_id=1, source_target_pairs={{0,8},{4,12},{8,24},{12,28},{16,0},{20,4},{24,16},{28,20},{1,9},{5... | collective-permute-start | bytes 1179656 | tf_op jit(solution)/shard_map/ppermute | solution.py:282
  67.7 6.5 %collective-permute-done.9.refs_12_ = f32[256,384]{1,0:T(8,128)} collective-permute-done((f32[256,384]{1,0:T(8,128)S(1)}, f32[256,384]{1,0:T(8,128)}, u32[]{:S(2)}, u32[]{:S(2)}) %collective-permute-start.9) | collective-permute-done | bytes 393248 | tf_op jit(solution)/shard_map/ppermute | solution.py:282
  74.2 1.8 %collective-permute-start.13 = (f32[256,384]{1,0:T(8,128)}, f32[256,384]{1,0:T(8,128)}, u32[]{:S(2)}, u32[]{:S(2)}) collective-permute-start(f32[256,384]{1,0:T(8,128)} %collective-permute-done.9.refs_12_), channel_id=1, source_target_pairs={{0,8},{4,12},{8,24},{12,28},{16,0},{20,4},{24,16},{28,20},{1,9},{5... | collective-permute-start | bytes 1179656 | tf_op jit(solution)/shard_map/ppermute | solution.py:282
  76.2 0.7 convert_reduce_fusion.2.start_ref
  77.4 4.5 %collective-permute-done.1.refs_2_ = f32[1536,128]{1,0:T(8,128)S(1)} collective-permute-done((f32[1536,128]{1,0:T(8,128)S(1)}, f32[1536,128]{1,0:T(8,128)S(1)}, u32[]{:S(2)}, u32[]{:S(2)}) %collective-permute-start.1) | collective-permute-done | bytes 786464 | tf_op jit(solution)/shard_map/ppermute | solution.py:272
  82.8 1.8 %collective-permute-done.15.refs_18_ = f32[256,384]{1,0:T(8,128)} collective-permute-done((f32[256,384]{1,0:T(8,128)}, f32[256,384]{1,0:T(8,128)}, u32[]{:S(2)}, u32[]{:S(2)}) %collective-permute-start.15) | collective-permute-done | bytes 393248 | tf_op jit(solution)/shard_map/ppermute | solution.py:282
  84.6 0.7 multiply_reduce_fusion.entry_ref
  85.4 1.1 collective-permute-done.16.refs_19_
  86.6 0.7 copy-done.9
  87.3 25.5 %front.1 = (f32[1536,3072]{1,0:T(8,128)}, f32[1536,128]{1,0:T(8,128)}) custom-call(s32[2]{0:T(128)} %pad_add_fusion.1.place_ref, s32[3,16]{1,0:T(4,128)} %multiply_reduce_fusion.entry_ref, s32[7]{0:T(128)} %convert_reduce_fusion.2.start_ref, f32[512,512]{1,0:T(8,128)} %d_ref.3, f32[24,8,128]{2,1,0:T(8,128)} %bitcast.24, f32[1536,3072]{1,0:T(8,128)} %trail_ref.1, ...), custom_call_target="tpu_custom_call" | custom-call | flops 16911433728 | bytes 44040192 | tf_op jit(solution)/shard_map/front/pallas_call | solution.py:167
  (72 shorter events, 7.2 us)
Async XLA Ops:
  0.6 21.8 %collective-permute-start = (f32[1536,128]{1,0:T(8,128)}, f32[1536,128]{1,0:T(8,128)S(1)}, u32[]{:S(2)}, u32[]{:S(2)}) collective-permute-start(f32[1536,128]{1,0:T(8,128)} %refs_0_.1), channel_id=1, source_target_pairs={{0,1},{1,3},{3,2},{2,0},{4,5},{5,7},{7,6},{6,4},{8,9},{9,11},{11,1... | collective-permute-start | bytes 2359304 | tf_op jit(solution)/shard_map/ppermute | solution.py:268
  3.7 14.3 %all-to-all-start = ((f32[4,384,128]{2,1,0:T(8,128)}), f32[4,384,128]{2,1,0:T(8,128)S(1)}, u32[]{:S(2)}, u32[]{:S(2)}) async-start(f32[4,384,128]{2,1,0:T(8,128)} %bitcast.22), calls=%async_computation | async-start | bytes 1572864 | tf_op jit(solution)/shard_map/all_to_all | solution.py:260
  22.5 64.1 %copy-start.1 = (f32[1536,128]{1,0:T(8,128)}, f32[1536,128]{1,0:T(8,128)S(1)}, u32[]{:S(2)}) copy-start(f32[1536,128]{1,0:T(8,128)S(1)} %collective-permute-done.refs_1_) | copy-start | bytes 2359300
  46.5 18.3 %collective-permute-start.4 = (f32[1536,128]{1,0:T(8,128)}, f32[1536,128]{1,0:T(8,128)S(1)}, u32[]{:S(2)}, u32[]{:S(2)}) collective-permute-start(f32[1536,128]{1,0:T(8,128)} %refs_0_.1), channel_id=1, source_target_pairs={{1,0},{3,1},{2,3},{0,2},{5,4},{7,5},{6,7},{4,6},{9,8},{11,9},{10,1... | collective-permute-start | bytes 2359304 | tf_op jit(solution)/shard_map/ppermute | solution.py:271
  49.7 12.0 %collective-permute-start.2 = (f32[256,384]{1,0:T(8,128)}, f32[256,384]{1,0:T(8,128)S(1)}, u32[]{:S(2)}, u32[]{:S(2)}) collective-permute-start(f32[256,384]{1,0:T(8,128)} %get-tuple-element.20.refs_4_), channel_id=1, source_target_pairs={{0,8},{4,12},{8,24},{12,28},{16,0},{20,4},{24,16},{28,20},{1,9},{5... | collective-permute-start | bytes 1179656 | tf_op jit(solution)/shard_map/ppermute | solution.py:282
  51.2 12.2 %collective-permute-start.3 = (f32[256,384]{1,0:T(8,128)}, f32[256,384]{1,0:T(8,128)}, u32[]{:S(2)}, u32[]{:S(2)}) collective-permute-start(f32[256,384]{1,0:T(8,128)} %get-tuple-element.21.refs_6_), channel_id=1, source_target_pairs={{0,16},{4,20},{8,0},{12,4},{16,24},{20,28},{24,8},{28,12},{1,17},{... | collective-permute-start | bytes 1179656 | tf_op jit(solution)/shard_map/ppermute | solution.py:282
  51.8 9.9 %all-to-all-start.2 = ((f32[8,3,8,128]{3,2,1,0:T(8,128)}), f32[8,3,8,128]{3,2,1,0:T(8,128)S(1)}, u32[]{:S(2)}, u32[]{:S(2)}) async-start(f32[8,3,8,128]{3,2,1,0:T(8,128)} %select_maximum_fusion), calls=%async_computation.2 | async-start | bytes 196608 | tf_op jit(solution)/shard_map/all_to_all | solution.py:220
  56.1 11.5 %collective-permute-start.5 = (f32[256,384]{1,0:T(8,128)}, f32[256,384]{1,0:T(8,128)}, u32[]{:S(2)}, u32[]{:S(2)}) collective-permute-start(f32[256,384]{1,0:T(8,128)} %get-tuple-element.20.refs_4_), channel_id=1, source_target_pairs={{0,4},{4,0},{8,12},{12,8},{16,20},{20,16},{24,28},{28,24},{1,5},{5... | collective-permute-start | bytes 1179656 | tf_op jit(solution)/shard_map/ppermute | solution.py:288
  56.6 20.7 %collective-permute-start.6 = (f32[256,384]{1,0:T(8,128)}, f32[256,384]{1,0:T(8,128)}, u32[]{:S(2)}, u32[]{:S(2)}) collective-permute-start(f32[256,384]{1,0:T(8,128)} %get-tuple-element.21.refs_6_), channel_id=1, source_target_pairs={{0,4},{4,0},{8,12},{12,8},{16,20},{20,16},{24,28},{28,24},{1,5},{5... | collective-permute-start | bytes 1179656 | tf_op jit(solution)/shard_map/ppermute | solution.py:288
  61.6 24.9 %copy-start = (f32[8,3,8,128]{3,2,1,0:T(8,128)}, f32[8,3,8,128]{3,2,1,0:T(8,128)S(1)}, u32[]{:S(2)}) copy-start(f32[8,3,8,128]{3,2,1,0:T(8,128)S(1)} %all-to-all-done.2) | copy-start | bytes 294916
  61.7 24.8 %copy-start.4 = (f32[256,384]{1,0:T(8,128)}, f32[256,384]{1,0:T(8,128)S(1)}, u32[]{:S(2)}) copy-start(f32[256,384]{1,0:T(8,128)S(1)} %collective-permute-done.2.refs_8_) | copy-start | bytes 1179652
  61.7 20.2 %collective-permute-start.1 = (f32[1536,128]{1,0:T(8,128)S(1)}, f32[1536,128]{1,0:T(8,128)S(1)}, u32[]{:S(2)}, u32[]{:S(2)}) collective-permute-start(f32[1536,128]{1,0:T(8,128)S(1)} %collective-permute-done.refs_1_), channel_id=1, source_target_pairs={{0,1},{1,3},{3,2},{2,0},{4,5},{5,7},{7,6},{6,4},{8,9},{9,11},{11,1... | collective-permute-start | bytes 2359304 | tf_op jit(solution)/shard_map/ppermute | solution.py:272
  64.8 21.7 %copy-start.2 = (f32[1536,128]{1,0:T(8,128)}, f32[1536,128]{1,0:T(8,128)S(1)}, u32[]{:S(2)}) copy-start(f32[1536,128]{1,0:T(8,128)S(1)} %collective-permute-done.4.refs_3_) | copy-start | bytes 2359300
  64.8 9.4 %collective-permute-start.9 = (f32[256,384]{1,0:T(8,128)S(1)}, f32[256,384]{1,0:T(8,128)}, u32[]{:S(2)}, u32[]{:S(2)}) collective-permute-start(f32[256,384]{1,0:T(8,128)S(1)} %collective-permute-done.2.refs_8_), channel_id=1, source_target_pairs={{0,8},{4,12},{8,24},{12,28},{16,0},{20,4},{24,16},{28,20},{1,9},{5... | collective-permute-start | bytes 1179656 | tf_op jit(solution)/shard_map/ppermute | solution.py:282
  66.3 9.6 %collective-permute-start.11 = (f32[256,384]{1,0:T(8,128)}, f32[256,384]{1,0:T(8,128)}, u32[]{:S(2)}, u32[]{:S(2)}) collective-permute-start(f32[256,384]{1,0:T(8,128)} %collective-permute-done.3.refs_10_), channel_id=1, source_target_pairs={{0,16},{4,20},{8,0},{12,4},{16,24},{20,28},{24,8},{28,12},{1,17},{... | collective-permute-start | bytes 1179656 | tf_op jit(solution)/shard_map/ppermute | solution.py:282
  67.6 14.4 %collective-permute-start.7 = (f32[256,384]{1,0:T(8,128)S(1)}, f32[256,384]{1,0:T(8,128)}, u32[]{:S(2)}, u32[]{:S(2)}) collective-permute-start(f32[256,384]{1,0:T(8,128)S(1)} %collective-permute-done.2.refs_8_), channel_id=1, source_target_pairs={{0,4},{4,0},{8,12},{12,8},{16,20},{20,16},{24,28},{28,24},{1,5},{5... | collective-permute-start | bytes 1179656 | tf_op jit(solution)/shard_map/ppermute | solution.py:288
  74.2 8.6 %collective-permute-start.13 = (f32[256,384]{1,0:T(8,128)}, f32[256,384]{1,0:T(8,128)}, u32[]{:S(2)}, u32[]{:S(2)}) collective-permute-start(f32[256,384]{1,0:T(8,128)} %collective-permute-done.9.refs_12_), channel_id=1, source_target_pairs={{0,8},{4,12},{8,24},{12,28},{16,0},{20,4},{24,16},{28,20},{1,9},{5... | collective-permute-start | bytes 1179656 | tf_op jit(solution)/shard_map/ppermute | solution.py:282
  75.9 8.7 %collective-permute-start.15 = (f32[256,384]{1,0:T(8,128)}, f32[256,384]{1,0:T(8,128)}, u32[]{:S(2)}, u32[]{:S(2)}) collective-permute-start(f32[256,384]{1,0:T(8,128)} %collective-permute-done.11.refs_14_), channel_id=1, source_target_pairs={{0,16},{4,20},{8,0},{12,4},{16,24},{20,28},{24,8},{28,12},{1,17},{... | collective-permute-start | bytes 1179656 | tf_op jit(solution)/shard_map/ppermute | solution.py:282
  77.3 8.0 %collective-permute-start.8 = (f32[256,384]{1,0:T(8,128)}, f32[256,384]{1,0:T(8,128)S(1)}, u32[]{:S(2)}, u32[]{:S(2)}) collective-permute-start(f32[256,384]{1,0:T(8,128)} %collective-permute-done.3.refs_10_), channel_id=1, source_target_pairs={{0,4},{4,0},{8,12},{12,8},{16,20},{20,16},{24,28},{28,24},{1,5},{5... | collective-permute-start | bytes 1179656 | tf_op jit(solution)/shard_map/ppermute | solution.py:288
  82.0 4.6 %copy-start.3 = (f32[1536,128]{1,0:T(8,128)}, f32[1536,128]{1,0:T(8,128)S(1)}, u32[]{:S(2)}) copy-start(f32[1536,128]{1,0:T(8,128)S(1)} %collective-permute-done.1.refs_2_) | copy-start | bytes 2359300
  82.0 3.4 %collective-permute-start.10 = (f32[256,384]{1,0:T(8,128)}, f32[256,384]{1,0:T(8,128)S(1)}, u32[]{:S(2)}, u32[]{:S(2)}) collective-permute-start(f32[256,384]{1,0:T(8,128)} %collective-permute-done.9.refs_12_), channel_id=1, source_target_pairs={{0,4},{4,0},{8,12},{12,8},{16,20},{20,16},{24,28},{28,24},{1,5},{5... | collective-permute-start | bytes 1179656 | tf_op jit(solution)/shard_map/ppermute | solution.py:288
  82.0 3.4 %collective-permute-start.12 = (f32[256,384]{1,0:T(8,128)}, f32[256,384]{1,0:T(8,128)S(1)}, u32[]{:S(2)}, u32[]{:S(2)}) collective-permute-start(f32[256,384]{1,0:T(8,128)} %collective-permute-done.11.refs_14_), channel_id=1, source_target_pairs={{0,4},{4,0},{8,12},{12,8},{16,20},{20,16},{24,28},{28,24},{1,5},{5... | collective-permute-start | bytes 1179656 | tf_op jit(solution)/shard_map/ppermute | solution.py:288
  82.8 2.6 %collective-permute-start.14 = (f32[256,384]{1,0:T(8,128)}, f32[256,384]{1,0:T(8,128)S(1)}, u32[]{:S(2)}, u32[]{:S(2)}) collective-permute-start(f32[256,384]{1,0:T(8,128)} %collective-permute-done.13.refs_16_), channel_id=1, source_target_pairs={{0,4},{4,0},{8,12},{12,8},{16,20},{20,16},{24,28},{28,24},{1,5},{5... | collective-permute-start | bytes 1179656 | tf_op jit(solution)/shard_map/ppermute | solution.py:288
  84.6 1.9 %collective-permute-start.16 = (f32[256,384]{1,0:T(8,128)}, f32[256,384]{1,0:T(8,128)S(1)}, u32[]{:S(2)}, u32[]{:S(2)}) collective-permute-start(f32[256,384]{1,0:T(8,128)} %collective-permute-done.15.refs_18_), channel_id=1, source_target_pairs={{0,4},{4,0},{8,12},{12,8},{16,20},{20,16},{24,28},{28,24},{1,5},{5... | collective-permute-start | bytes 1179656 | tf_op jit(solution)/shard_map/ppermute | solution.py:288
  (5 other events, 5.5 us)

commit v11 on v10

--- a/solution.py
+++ b/solution.py
@@ -216,8 +216,7 @@
     return jnp.concatenate([send, numbers], axis=1)
 
 
-def exchange_tiles(send, tiles_dev):
-    got = lax.all_to_all(send, "row", split_axis=0, concat_axis=0, tiled=True)
+def unpack_tiles(got, tiles_dev):
     landing = got[:, CAP, 0, :CAP].astype(jnp.int32)
     landing = jnp.pad(landing, ((0, 0), (0, 1)), constant_values=tiles_dev)
     return got.reshape(-1, TILE_ROWS, TILE_COLS), landing.reshape(-1)
@@ -253,6 +252,7 @@
     row_index = lax.axis_index("row")
     place = jnp.stack([row_index, col_index]).astype(jnp.int32)
     tiles = pack_tiles(agg_vals, agg_dest, agg_tile, tiles_dev)
+    tiles = lax.all_to_all(tiles, "row", split_axis=0, concat_axis=0, tiled=True)
     ringed = row_devices == 8 and col_devices == 4
     if ringed:
         quarter = local_rows // 4
@@ -295,7 +295,7 @@
         pieces, plan = pair_factor(diag_inverse, partner, 768), [(0, 0, 0), (1, 0, 0)]
         own = [whole[s] for s in range(col_devices)]
 
-    agg, landing = exchange_tiles(tiles, tiles_dev)
+    agg, landing = unpack_tiles(tiles, tiles_dev)
     entries, starts = order_tiles(
         landing, row_devices * CAP, tiles_dev, tile_cols, bm, bn, n_i, n_j
     )

time: 113 us -> 123 us (1.088)
  blocking collectives: 24 us -> 46.1 us
  starting transfers between devices: 19.6 us -> 12 us
  waiting for transfers between devices: 30.4 us -> 26.1 us
    all_to_all x0 -> x2, blocking collectives: none -> 23.8 us  [the longest x1 15.1 us: per_device(): lax.all_to_all(panel.reshape(4, quarter, part), 'row', split_axis=0, conc...]
    all_to_all x2 -> x0, waiting for transfers between devices: 10.3 us -> none  [the longest x1 5.28 us: per_device(): lax.all_to_all(panel.reshape(4, quarter, part), 'row', split_axis=0, conc...]
    ppermute x6, waiting for transfers between devices: 8.58 us -> 17.3 us  [per_device(): held = [lax.ppermute(x, 'row', turn) for x, turn in zip(held, turns)]]
    all_to_all x2 -> x0, starting transfers between devices: 7.44 us -> none  [the longest x1 3.72 us: exchange_tiles(): got = lax.all_to_all(send, 'row', split_axis=0, concat_axis=0, tiled=True)]
    ppermute x1, waiting for transfers between devices: 4.47 us -> 0.01 us  [per_device(): ring(panel)]
    ppermute x1, waiting for transfers between devices: 1.4 us -> 5.82 us  [per_device(): third = lax.ppermute(mine, 'col', list(PREV.items()))]
    ppermute x1, waiting for transfers between devices: 4.55 us -> 1.8 us  [per_device(): second = ring(first)]
    all_to_all x1, blocking collectives: 24 us -> 22.3 us  [per_device(): lax.all_to_all(spread, 'col', split_axis=0, concat_axis=0, tiled=True)]
  transfers between devices with their start and end apart: 19 -> 17, of which waited for: 9 -> 8; matrix products, arithmetic and copies ran while one was open for 8% -> 7% of each run, Pallas kernels for 3% -> 2%
where the time goes in v11:
time: 123 us
  blocking collectives  46.1 us (37%)
  Pallas kernels  28.5 us (23%)
  waiting for transfers between devices  26.1 us (21%)
  starting transfers between devices  12 us (10%)
  other arithmetic  5.3 us (4%)
  local copies, waits for them, and re-layouts  3.77 us (3%)
    pallas_call x1, Pallas kernels, front(): pl.pallas_call(functools.partial(front_kernel, ringed, own_plan, plan), g...  25.5 us
    all_to_all x1, blocking collectives, per_device(): lax.all_to_all(spread, 'col', split_axis=0, concat_axis=0, tiled=True)  22.3 us
    ppermute x6, waiting for transfers between devices, per_device(): held = [lax.ppermute(x, 'row', turn) for x, turn in zip(held, turns)]  17.3 us
    all_to_all x1, blocking collectives, per_device(): lax.all_to_all(panel.reshape(4, quarter, part), 'row', split_axis=0, conc...  15.1 us
    all_to_all x1, blocking collectives, per_device(): lax.all_to_all(tiles, 'row', split_axis=0, concat_axis=0, tiled=True)  8.71 us
    ppermute x6, starting transfers between devices, per_device(): held = [lax.ppermute(x, 'row', turn) for x, turn in zip(held, turns)]  6.02 us
    ppermute x1, waiting for transfers between devices, per_device(): third = lax.ppermute(mine, 'col', list(PREV.items()))  5.82 us
    ppermute x1, starting transfers between devices, per_device(): ring(panel)  3.08 us
  transfers between devices with their start and end apart: 17, of which 8 were waited for; matrix products, arithmetic and copies ran while one was open for 7% of the time, Pallas kernels for 2%

profile of v11, /device:TPU:0, one launch (start us, length us, event | category | flops | bytes accessed | tf_op | source)
XLA Modules:
  0.0 122.7 jit_solution(15812284240206604929)
XLA Ops:
  0.6 3.1 %collective-permute-start = (f32[1536,128]{1,0:T(8,128)}, f32[1536,128]{1,0:T(8,128)S(1)}, u32[]{:S(2)}, u32[]{:S(2)}) collective-permute-start(f32[1536,128]{1,0:T(8,128)} %refs_0_.1), channel_id=1, source_target_pairs={{0,1},{1,3},{3,2},{2,0},{4,5},{5,7},{7,6},{6,4},{8,9},{9,11},{11,1... | collective-permute-start | bytes 2359304 | tf_op jit(solution)/shard_map/ppermute | solution.py:268
  3.7 0.9 convert_reduce_fusion.1
  4.6 0.7 multiply_add_fusion
  6.8 1.5 %scatter_fusion = f32[16,8,128]{2,1,0:T(8,128)S(1)} fusion(f32[16,8,128]{2,1,0:T(8,128)S(1)} %broadcast_in_dim.18, s32[12]{0:T(128)S(1)} %fusion.7, f32[12,8,128]{2,1,0:T(8,128)} %bitcast.25), kind=kCustom, calls=%fused_computation | custom fusion | bytes 147504 | tf_op jit(solution)/shard_map/scatter | solution.py:212
  8.4 8.7 %all_to_all.15 = f32[8,3,8,128]{3,2,1,0:T(8,128)S(1)} all-to-all(f32[8,3,8,128]{3,2,1,0:T(8,128)S(1)} %select_maximum_fusion), channel_id=1, replica_groups=mesh['row'=8,'col'=4] {'row'}, dimensions={0} | all-to-all | bytes 196608 | tf_op jit(solution)/shard_map/all_to_all | solution.py:255
  17.1 15.1 %all_to_all.16 = f32[4,384,128]{2,1,0:T(8,128)S(1)} all-to-all(f32[4,384,128]{2,1,0:T(8,128)} %bitcast.22), channel_id=1, replica_groups={{0,8,16,24},{4,12,20,28},{1,9,17,25},{5,13,21,29},{2,10,18,26},{6,14,22..., dimensions={0} | all-to-all | bytes 1572864 | tf_op jit(solution)/shard_map/all_to_all | solution.py:260
  32.2 22.3 %all_to_all.17.panel_ref = f32[4,384,128]{2,1,0:T(8,128)} all-to-all(f32[4,384,128]{2,1,0:T(8,128)S(1)} %all_to_all.16), channel_id=1, replica_groups=mesh['row'=8,'col'=4] {'col'}, dimensions={0} | all-to-all | bytes 1572864 | tf_op jit(solution)/shard_map/all_to_all | solution.py:269
  54.8 3.0 %pair_factor.1 = (f32[256,384]{1,0:T(8,128)}, f32[256,384]{1,0:T(8,128)}) custom-call(f32[512,512]{1,0:T(8,128)} %d_ref.3, f32[4,384,128]{2,1,0:T(8,128)} %all_to_all.17.panel_ref), custom_call_target="tpu_custom_call" | custom-call | flops 603979776 | bytes 1572864 | tf_op jit(solution)/shard_map/pair_factor/pallas_call | solution.py:48
  57.8 1.2 collective-permute-start.2
  59.0 0.9 collective-permute-start.3
  61.4 6.2 %collective-permute-done.2.refs_8_ = f32[256,384]{1,0:T(8,128)} collective-permute-done((f32[256,384]{1,0:T(8,128)}, f32[256,384]{1,0:T(8,128)}, u32[]{:S(2)}, u32[]{:S(2)}) %collective-permute-start.2) | collective-permute-done | bytes 393248 | tf_op jit(solution)/shard_map/ppermute | solution.py:282
  67.6 1.4 %collective-permute-start.1 = (f32[1536,128]{1,0:T(8,128)S(1)}, f32[1536,128]{1,0:T(8,128)S(1)}, u32[]{:S(2)}, u32[]{:S(2)}) collective-permute-start(f32[1536,128]{1,0:T(8,128)S(1)} %collective-permute-done.refs_1_), channel_id=1, source_target_pairs={{0,1},{1,3},{3,2},{2,0},{4,5},{5,7},{7,6},{6,4},{8,9},{9,11},{11,1... | collective-permute-start | bytes 2359304 | tf_op jit(solution)/shard_map/ppermute | solution.py:272
  69.0 5.8 %collective-permute-done.4.refs_3_ = f32[1536,128]{1,0:T(8,128)S(1)} collective-permute-done((f32[1536,128]{1,0:T(8,128)}, f32[1536,128]{1,0:T(8,128)S(1)}, u32[]{:S(2)}, u32[]{:S(2)}) %collective-permute-start.4) | collective-permute-done | bytes 786464 | tf_op jit(solution)/shard_map/ppermute | solution.py:271
  74.9 1.4 %collective-permute-start.9 = (f32[256,384]{1,0:T(8,128)}, f32[256,384]{1,0:T(8,128)S(1)}, u32[]{:S(2)}, u32[]{:S(2)}) collective-permute-start(f32[256,384]{1,0:T(8,128)} %collective-permute-done.2.refs_8_), channel_id=1, source_target_pairs={{0,8},{4,12},{8,24},{12,28},{16,0},{20,4},{24,16},{28,20},{1,9},{5... | collective-permute-start | bytes 1179656 | tf_op jit(solution)/shard_map/ppermute | solution.py:282
  77.7 7.0 %collective-permute-done.9.refs_12_ = f32[256,384]{1,0:T(8,128)S(1)} collective-permute-done((f32[256,384]{1,0:T(8,128)}, f32[256,384]{1,0:T(8,128)S(1)}, u32[]{:S(2)}, u32[]{:S(2)}) %collective-permute-start.9) | collective-permute-done | bytes 393248 | tf_op jit(solution)/shard_map/ppermute | solution.py:282
  84.7 1.4 %collective-permute-start.13 = (f32[256,384]{1,0:T(8,128)S(1)}, f32[256,384]{1,0:T(8,128)}, u32[]{:S(2)}, u32[]{:S(2)}) collective-permute-start(f32[256,384]{1,0:T(8,128)S(1)} %collective-permute-done.9.refs_12_), channel_id=1, source_target_pairs={{0,8},{4,12},{8,24},{12,28},{16,0},{20,4},{24,16},{28,20},{1,9},{5... | collective-permute-start | bytes 1179656 | tf_op jit(solution)/shard_map/ppermute | solution.py:282
  86.9 0.7 convert_reduce_fusion.2.start_ref
  88.1 1.8 %collective-permute-done.1.refs_2_ = f32[1536,128]{1,0:T(8,128)S(1)} collective-permute-done((f32[1536,128]{1,0:T(8,128)S(1)}, f32[1536,128]{1,0:T(8,128)S(1)}, u32[]{:S(2)}, u32[]{:S(2)}) %collective-permute-start.1) | collective-permute-done | bytes 786464 | tf_op jit(solution)/shard_map/ppermute | solution.py:272
  90.4 2.2 %collective-permute-done.13.refs_16_ = f32[256,384]{1,0:T(8,128)} collective-permute-done((f32[256,384]{1,0:T(8,128)S(1)}, f32[256,384]{1,0:T(8,128)}, u32[]{:S(2)}, u32[]{:S(2)}) %collective-permute-start.13) | collective-permute-done | bytes 393248 | tf_op jit(solution)/shard_map/ppermute | solution.py:282
  92.6 1.8 %collective-permute-done.15.refs_18_ = f32[256,384]{1,0:T(8,128)} collective-permute-done((f32[256,384]{1,0:T(8,128)}, f32[256,384]{1,0:T(8,128)}, u32[]{:S(2)}, u32[]{:S(2)}) %collective-permute-start.15) | collective-permute-done | bytes 393248 | tf_op jit(solution)/shard_map/ppermute | solution.py:282
  94.5 0.7 multiply_reduce_fusion.entry_ref
  95.2 1.2 collective-permute-done.16.refs_19_
  96.5 0.7 copy-done.9
  97.2 25.5 %front.1 = (f32[1536,3072]{1,0:T(8,128)}, f32[1536,128]{1,0:T(8,128)}) custom-call(s32[2]{0:T(128)} %pad_add_fusion.1.place_ref, s32[3,16]{1,0:T(4,128)} %multiply_reduce_fusion.entry_ref, s32[7]{0:T(128)} %convert_reduce_fusion.2.start_ref, f32[512,512]{1,0:T(8,128)} %d_ref.3, f32[24,8,128]{2,1,0:T(8,128)} %bitcast.24, f32[1536,3072]{1,0:T(8,128)} %trail_ref.1, ...), custom_call_target="tpu_custom_call" | custom-call | flops 16911433728 | bytes 44040192 | tf_op jit(solution)/shard_map/front/pallas_call | solution.py:167
  (69 shorter events, 6.7 us)
Async XLA Ops:
  0.6 31.5 %collective-permute-start = (f32[1536,128]{1,0:T(8,128)}, f32[1536,128]{1,0:T(8,128)S(1)}, u32[]{:S(2)}, u32[]{:S(2)}) collective-permute-start(f32[1536,128]{1,0:T(8,128)} %refs_0_.1), channel_id=1, source_target_pairs={{0,1},{1,3},{3,2},{2,0},{4,5},{5,7},{7,6},{6,4},{8,9},{9,11},{11,1... | collective-permute-start | bytes 2359304 | tf_op jit(solution)/shard_map/ppermute | solution.py:268
  17.1 79.3 %copy-start = (f32[8,3,8,128]{3,2,1,0:T(8,128)}, f32[8,3,8,128]{3,2,1,0:T(8,128)S(1)}, u32[]{:S(2)}) copy-start(f32[8,3,8,128]{3,2,1,0:T(8,128)S(1)} %all_to_all.15) | copy-start | bytes 294916
  32.2 64.2 %copy-start.1 = (f32[1536,128]{1,0:T(8,128)}, f32[1536,128]{1,0:T(8,128)S(1)}, u32[]{:S(2)}) copy-start(f32[1536,128]{1,0:T(8,128)S(1)} %collective-permute-done.refs_1_) | copy-start | bytes 2359300
  54.5 20.3 %collective-permute-start.4 = (f32[1536,128]{1,0:T(8,128)}, f32[1536,128]{1,0:T(8,128)S(1)}, u32[]{:S(2)}, u32[]{:S(2)}) collective-permute-start(f32[1536,128]{1,0:T(8,128)} %refs_0_.1), channel_id=1, source_target_pairs={{1,0},{3,1},{2,3},{0,2},{5,4},{7,5},{6,7},{4,6},{9,8},{11,9},{10,1... | collective-permute-start | bytes 2359304 | tf_op jit(solution)/shard_map/ppermute | solution.py:271
  57.8 9.8 %collective-permute-start.2 = (f32[256,384]{1,0:T(8,128)}, f32[256,384]{1,0:T(8,128)}, u32[]{:S(2)}, u32[]{:S(2)}) collective-permute-start(f32[256,384]{1,0:T(8,128)} %get-tuple-element.20.refs_4_), channel_id=1, source_target_pairs={{0,8},{4,12},{8,24},{12,28},{16,0},{20,4},{24,16},{28,20},{1,9},{5... | collective-permute-start | bytes 1179656 | tf_op jit(solution)/shard_map/ppermute | solution.py:282
  59.0 10.1 %collective-permute-start.3 = (f32[256,384]{1,0:T(8,128)}, f32[256,384]{1,0:T(8,128)}, u32[]{:S(2)}, u32[]{:S(2)}) collective-permute-start(f32[256,384]{1,0:T(8,128)} %get-tuple-element.21.refs_6_), channel_id=1, source_target_pairs={{0,16},{4,20},{8,0},{12,4},{16,24},{20,28},{24,8},{28,12},{1,17},{... | collective-permute-start | bytes 1179656 | tf_op jit(solution)/shard_map/ppermute | solution.py:282
  60.4 17.2 %collective-permute-start.5 = (f32[256,384]{1,0:T(8,128)}, f32[256,384]{1,0:T(8,128)}, u32[]{:S(2)}, u32[]{:S(2)}) collective-permute-start(f32[256,384]{1,0:T(8,128)} %get-tuple-element.20.refs_4_), channel_id=1, source_target_pairs={{0,4},{4,0},{8,12},{12,8},{16,20},{20,16},{24,28},{28,24},{1,5},{5... | collective-permute-start | bytes 1179656 | tf_op jit(solution)/shard_map/ppermute | solution.py:288
  60.4 27.6 %collective-permute-start.6 = (f32[256,384]{1,0:T(8,128)}, f32[256,384]{1,0:T(8,128)}, u32[]{:S(2)}, u32[]{:S(2)}) collective-permute-start(f32[256,384]{1,0:T(8,128)} %get-tuple-element.21.refs_6_), channel_id=1, source_target_pairs={{0,4},{4,0},{8,12},{12,8},{16,20},{20,16},{24,28},{28,24},{1,5},{5... | collective-permute-start | bytes 1179656 | tf_op jit(solution)/shard_map/ppermute | solution.py:288
  67.6 22.3 %collective-permute-start.1 = (f32[1536,128]{1,0:T(8,128)S(1)}, f32[1536,128]{1,0:T(8,128)S(1)}, u32[]{:S(2)}, u32[]{:S(2)}) collective-permute-start(f32[1536,128]{1,0:T(8,128)S(1)} %collective-permute-done.refs_1_), channel_id=1, source_target_pairs={{0,1},{1,3},{3,2},{2,0},{4,5},{5,7},{7,6},{6,4},{8,9},{9,11},{11,1... | collective-permute-start | bytes 2359304 | tf_op jit(solution)/shard_map/ppermute | solution.py:272
  74.9 21.5 %copy-start.2 = (f32[1536,128]{1,0:T(8,128)}, f32[1536,128]{1,0:T(8,128)S(1)}, u32[]{:S(2)}) copy-start(f32[1536,128]{1,0:T(8,128)S(1)} %collective-permute-done.4.refs_3_) | copy-start | bytes 2359300
  74.9 9.9 %collective-permute-start.9 = (f32[256,384]{1,0:T(8,128)}, f32[256,384]{1,0:T(8,128)S(1)}, u32[]{:S(2)}, u32[]{:S(2)}) collective-permute-start(f32[256,384]{1,0:T(8,128)} %collective-permute-done.2.refs_8_), channel_id=1, source_target_pairs={{0,8},{4,12},{8,24},{12,28},{16,0},{20,4},{24,16},{28,20},{1,9},{5... | collective-permute-start | bytes 1179656 | tf_op jit(solution)/shard_map/ppermute | solution.py:282
  76.2 10.1 %collective-permute-start.11 = (f32[256,384]{1,0:T(8,128)}, f32[256,384]{1,0:T(8,128)}, u32[]{:S(2)}, u32[]{:S(2)}) collective-permute-start(f32[256,384]{1,0:T(8,128)} %collective-permute-done.3.refs_10_), channel_id=1, source_target_pairs={{0,16},{4,20},{8,0},{12,4},{16,24},{20,28},{24,8},{28,12},{1,17},{... | collective-permute-start | bytes 1179656 | tf_op jit(solution)/shard_map/ppermute | solution.py:282
  77.7 12.3 %collective-permute-start.7 = (f32[256,384]{1,0:T(8,128)}, f32[256,384]{1,0:T(8,128)}, u32[]{:S(2)}, u32[]{:S(2)}) collective-permute-start(f32[256,384]{1,0:T(8,128)} %collective-permute-done.2.refs_8_), channel_id=1, source_target_pairs={{0,4},{4,0},{8,12},{12,8},{16,20},{20,16},{24,28},{28,24},{1,5},{5... | collective-permute-start | bytes 1179656 | tf_op jit(solution)/shard_map/ppermute | solution.py:288
  84.7 11.7 %copy-start.4 = (f32[256,384]{1,0:T(8,128)}, f32[256,384]{1,0:T(8,128)S(1)}, u32[]{:S(2)}) copy-start(f32[256,384]{1,0:T(8,128)S(1)} %collective-permute-done.9.refs_12_) | copy-start | bytes 1179652
  84.7 7.9 %collective-permute-start.13 = (f32[256,384]{1,0:T(8,128)S(1)}, f32[256,384]{1,0:T(8,128)}, u32[]{:S(2)}, u32[]{:S(2)}) collective-permute-start(f32[256,384]{1,0:T(8,128)S(1)} %collective-permute-done.9.refs_12_), channel_id=1, source_target_pairs={{0,8},{4,12},{8,24},{12,28},{16,0},{20,4},{24,16},{28,20},{1,9},{5... | collective-permute-start | bytes 1179656 | tf_op jit(solution)/shard_map/ppermute | solution.py:282
  86.3 8.1 %collective-permute-start.15 = (f32[256,384]{1,0:T(8,128)}, f32[256,384]{1,0:T(8,128)}, u32[]{:S(2)}, u32[]{:S(2)}) collective-permute-start(f32[256,384]{1,0:T(8,128)} %collective-permute-done.11.refs_14_), channel_id=1, source_target_pairs={{0,16},{4,20},{8,0},{12,4},{16,24},{20,28},{24,8},{28,12},{1,17},{... | collective-permute-start | bytes 1179656 | tf_op jit(solution)/shard_map/ppermute | solution.py:282
  88.0 7.1 %collective-permute-start.8 = (f32[256,384]{1,0:T(8,128)}, f32[256,384]{1,0:T(8,128)S(1)}, u32[]{:S(2)}, u32[]{:S(2)}) collective-permute-start(f32[256,384]{1,0:T(8,128)} %collective-permute-done.3.refs_10_), channel_id=1, source_target_pairs={{0,4},{4,0},{8,12},{12,8},{16,20},{20,16},{24,28},{28,24},{1,5},{5... | collective-permute-start | bytes 1179656 | tf_op jit(solution)/shard_map/ppermute | solution.py:288
  89.9 6.5 %copy-start.3 = (f32[1536,128]{1,0:T(8,128)}, f32[1536,128]{1,0:T(8,128)S(1)}, u32[]{:S(2)}) copy-start(f32[1536,128]{1,0:T(8,128)S(1)} %collective-permute-done.1.refs_2_) | copy-start | bytes 2359300
  89.9 5.3 %collective-permute-start.10 = (f32[256,384]{1,0:T(8,128)S(1)}, f32[256,384]{1,0:T(8,128)S(1)}, u32[]{:S(2)}, u32[]{:S(2)}) collective-permute-start(f32[256,384]{1,0:T(8,128)S(1)} %collective-permute-done.9.refs_12_), channel_id=1, source_target_pairs={{0,4},{4,0},{8,12},{12,8},{16,20},{20,16},{24,28},{28,24},{1,5},{5... | collective-permute-start | bytes 1179656 | tf_op jit(solution)/shard_map/ppermute | solution.py:288
  89.9 5.3 %collective-permute-start.12 = (f32[256,384]{1,0:T(8,128)}, f32[256,384]{1,0:T(8,128)S(1)}, u32[]{:S(2)}, u32[]{:S(2)}) collective-permute-start(f32[256,384]{1,0:T(8,128)} %collective-permute-done.11.refs_14_), channel_id=1, source_target_pairs={{0,4},{4,0},{8,12},{12,8},{16,20},{20,16},{24,28},{28,24},{1,5},{5... | collective-permute-start | bytes 1179656 | tf_op jit(solution)/shard_map/ppermute | solution.py:288
  92.6 2.6 %collective-permute-start.14 = (f32[256,384]{1,0:T(8,128)}, f32[256,384]{1,0:T(8,128)S(1)}, u32[]{:S(2)}, u32[]{:S(2)}) collective-permute-start(f32[256,384]{1,0:T(8,128)} %collective-permute-done.13.refs_16_), channel_id=1, source_target_pairs={{0,4},{4,0},{8,12},{12,8},{16,20},{20,16},{24,28},{28,24},{1,5},{5... | collective-permute-start | bytes 1179656 | tf_op jit(solution)/shard_map/ppermute | solution.py:288
  94.4 1.9 %collective-permute-start.16 = (f32[256,384]{1,0:T(8,128)}, f32[256,384]{1,0:T(8,128)S(1)}, u32[]{:S(2)}, u32[]{:S(2)}) collective-permute-start(f32[256,384]{1,0:T(8,128)} %collective-permute-done.15.refs_18_), channel_id=1, source_target_pairs={{0,4},{4,0},{8,12},{12,8},{16,20},{20,16},{24,28},{28,24},{1,5},{5... | collective-permute-start | bytes 1179656 | tf_op jit(solution)/shard_map/ppermute | solution.py:288
  95.2 1.2 %copy-start.5 = (f32[256,384]{1,0:T(8,128)}, f32[256,384]{1,0:T(8,128)S(1)}, u32[]{:S(2)}) copy-start(f32[256,384]{1,0:T(8,128)S(1)} %collective-permute-done.8.refs_11_) | copy-start | bytes 1179652
  95.2 1.2 %copy-start.6 = (f32[256,384]{1,0:T(8,128)}, f32[256,384]{1,0:T(8,128)S(1)}, u32[]{:S(2)}) copy-start(f32[256,384]{1,0:T(8,128)S(1)} %collective-permute-done.10.refs_13_) | copy-start | bytes 1179652
  (3 other events, 3.2 us)

commit v12 on v10

--- a/solution.py
+++ b/solution.py
@@ -247,7 +247,7 @@
     col_index = lax.axis_index("col")
     tile_cols = local_cols // TILE_COLS
     tiles_dev = (local_rows // TILE_ROWS) * tile_cols
-    bm, bn = local_rows, 512
+    bm, bn = local_rows, 768
     n_i, n_j = local_rows // bm, local_cols // bn
 
     row_index = lax.axis_index("row")

time: 113 us -> 114 us (level)
  no operation moved by 1% of the time
where the time goes in v12:
time: 114 us; the launch traced here: 113 us
  waiting for transfers between devices  30.4 us (27%)
  Pallas kernels  29 us (25%)
  blocking collectives  24 us (21%)
  starting transfers between devices  19.6 us (17%)
  other arithmetic  6.02 us (5%)
  local copies, waits for them, and re-layouts  3.36 us (3%)
    pallas_call x1, Pallas kernels, front(): pl.pallas_call(functools.partial(front_kernel, ringed, own_plan, plan), g...  26 us
    all_to_all x1, blocking collectives, per_device(): lax.all_to_all(spread, 'col', split_axis=0, concat_axis=0, tiled=True)  24 us
    ppermute x6, waiting for transfers between devices, per_device(): held = [lax.ppermute(x, 'row', turn) for x, turn in zip(held, turns)]  8.58 us
    ppermute x6, starting transfers between devices, per_device(): held = [lax.ppermute(x, 'row', turn) for x, turn in zip(held, turns)]  6.08 us
    all_to_all x1, waiting for transfers between devices, per_device(): lax.all_to_all(panel.reshape(4, quarter, part), 'row', split_axis=0, conc...  5.28 us
    all_to_all x1, waiting for transfers between devices, exchange_tiles(): got = lax.all_to_all(send, 'row', split_axis=0, concat_axis=0, tiled=True)  4.99 us
    ppermute x1, waiting for transfers between devices, per_device(): second = ring(first)  4.55 us
    ppermute x1, waiting for transfers between devices, per_device(): ring(panel)  4.47 us
  transfers between devices with their start and end apart: 19, of which 9 were waited for; matrix products, arithmetic and copies ran while one was open for 8% of the time, Pallas kernels for 3%

profile of v12, /device:TPU:0, one launch (start us, length us, event | category | flops | bytes accessed | tf_op | source)
XLA Modules:
  0.0 113.2 jit_solution(2271437247108276706)
XLA Ops:
  0.6 3.1 %collective-permute-start = (f32[1536,128]{1,0:T(8,128)}, f32[1536,128]{1,0:T(8,128)S(1)}, u32[]{:S(2)}, u32[]{:S(2)}) collective-permute-start(f32[1536,128]{1,0:T(8,128)} %refs_0_.1), channel_id=1, source_target_pairs={{0,1},{1,3},{3,2},{2,0},{4,5},{5,7},{7,6},{6,4},{8,9},{9,11},{11,1... | collective-permute-start | bytes 2359304 | tf_op jit(solution)/shard_map/ppermute | solution.py:268
  3.7 3.7 %all-to-all-start = ((f32[4,384,128]{2,1,0:T(8,128)}), f32[4,384,128]{2,1,0:T(8,128)S(1)}, u32[]{:S(2)}, u32[]{:S(2)}) async-start(f32[4,384,128]{2,1,0:T(8,128)} %bitcast.22), calls=%async_computation | async-start | bytes 1572864 | tf_op jit(solution)/shard_map/all_to_all | solution.py:260
  7.4 0.9 convert_reduce_fusion.1
  9.9 0.7 fusion.6
  10.5 1.5 %scatter_fusion = f32[16,8,128]{2,1,0:T(8,128)S(1)} fusion(f32[16,8,128]{2,1,0:T(8,128)S(1)} %broadcast_in_dim.18, s32[12]{0:T(128)S(1)} %fusion.6, f32[12,8,128]{2,1,0:T(8,128)} %bitcast.25), kind=kCustom, calls=%fused_computation | custom fusion | bytes 147504 | tf_op jit(solution)/shard_map/scatter | solution.py:212
  12.7 5.3 %all-to-all-done = f32[4,384,128]{2,1,0:T(8,128)S(1)} async-done(((f32[4,384,128]{2,1,0:T(8,128)}), f32[4,384,128]{2,1,0:T(8,128)S(1)}, u32[]{:S(2)}, u32[]{:S(2)}) %all-to-all-start) | async-done | bytes 786464 | tf_op jit(solution)/shard_map/all_to_all | solution.py:260
  18.0 4.5 %collective-permute-done.refs_1_ = f32[1536,128]{1,0:T(8,128)S(1)} collective-permute-done((f32[1536,128]{1,0:T(8,128)}, f32[1536,128]{1,0:T(8,128)S(1)}, u32[]{:S(2)}, u32[]{:S(2)}) %collective-permute-start) | collective-permute-done | bytes 786464 | tf_op jit(solution)/shard_map/ppermute | solution.py:268
  22.5 24.0 %all_to_all.15.panel_ref = f32[4,384,128]{2,1,0:T(8,128)} all-to-all(f32[4,384,128]{2,1,0:T(8,128)S(1)} %all-to-all-done), channel_id=1, replica_groups=mesh['row'=8,'col'=4] {'col'}, dimensions={0} | all-to-all | bytes 1572864 | tf_op jit(solution)/shard_map/all_to_all | solution.py:269
  46.7 3.0 %pair_factor.1 = (f32[256,384]{1,0:T(8,128)}, f32[256,384]{1,0:T(8,128)}) custom-call(f32[512,512]{1,0:T(8,128)} %d_ref.3, f32[4,384,128]{2,1,0:T(8,128)} %all_to_all.15.panel_ref), custom_call_target="tpu_custom_call" | custom-call | flops 603979776 | bytes 1572864 | tf_op jit(solution)/shard_map/pair_factor/pallas_call | solution.py:48
  49.7 1.5 %collective-permute-start.2 = (f32[256,384]{1,0:T(8,128)}, f32[256,384]{1,0:T(8,128)S(1)}, u32[]{:S(2)}, u32[]{:S(2)}) collective-permute-start(f32[256,384]{1,0:T(8,128)} %get-tuple-element.20.refs_4_), channel_id=1, source_target_pairs={{0,8},{4,12},{8,24},{12,28},{16,0},{20,4},{24,16},{28,20},{1,9},{5... | collective-permute-start | bytes 1179656 | tf_op jit(solution)/shard_map/ppermute | solution.py:282
  51.8 3.7 %all-to-all-start.2 = ((f32[8,3,8,128]{3,2,1,0:T(8,128)}), f32[8,3,8,128]{3,2,1,0:T(8,128)S(1)}, u32[]{:S(2)}, u32[]{:S(2)}) async-start(f32[8,3,8,128]{3,2,1,0:T(8,128)} %select_maximum_fusion), calls=%async_computation.2 | async-start | bytes 196608 | tf_op jit(solution)/shard_map/all_to_all | solution.py:220
  56.6 5.0 %all-to-all-done.2 = f32[8,3,8,128]{3,2,1,0:T(8,128)S(1)} async-done(((f32[8,3,8,128]{3,2,1,0:T(8,128)}), f32[8,3,8,128]{3,2,1,0:T(8,128)S(1)}, u32[]{:S(2)}, u32[]{:S(2)}) %all-to-all-start.2) | async-done | bytes 98336 | tf_op jit(solution)/shard_map/all_to_all | solution.py:220
  61.7 1.7 %collective-permute-start.1 = (f32[1536,128]{1,0:T(8,128)S(1)}, f32[1536,128]{1,0:T(8,128)S(1)}, u32[]{:S(2)}, u32[]{:S(2)}) collective-permute-start(f32[1536,128]{1,0:T(8,128)S(1)} %collective-permute-done.refs_1_), channel_id=1, source_target_pairs={{0,1},{1,3},{3,2},{2,0},{4,5},{5,7},{7,6},{6,4},{8,9},{9,11},{11,1... | collective-permute-start | bytes 2359304 | tf_op jit(solution)/shard_map/ppermute | solution.py:272
  63.4 1.4 %collective-permute-done.4.refs_3_ = f32[1536,128]{1,0:T(8,128)S(1)} collective-permute-done((f32[1536,128]{1,0:T(8,128)}, f32[1536,128]{1,0:T(8,128)S(1)}, u32[]{:S(2)}, u32[]{:S(2)}) %collective-permute-start.4) | collective-permute-done | bytes 786464 | tf_op jit(solution)/shard_map/ppermute | solution.py:271
  64.8 1.5 %collective-permute-start.9 = (f32[256,384]{1,0:T(8,128)S(1)}, f32[256,384]{1,0:T(8,128)}, u32[]{:S(2)}, u32[]{:S(2)}) collective-permute-start(f32[256,384]{1,0:T(8,128)S(1)} %collective-permute-done.2.refs_8_), channel_id=1, source_target_pairs={{0,8},{4,12},{8,24},{12,28},{16,0},{20,4},{24,16},{28,20},{1,9},{5... | collective-permute-start | bytes 1179656 | tf_op jit(solution)/shard_map/ppermute | solution.py:282
  67.7 6.5 %collective-permute-done.9.refs_12_ = f32[256,384]{1,0:T(8,128)} collective-permute-done((f32[256,384]{1,0:T(8,128)S(1)}, f32[256,384]{1,0:T(8,128)}, u32[]{:S(2)}, u32[]{:S(2)}) %collective-permute-start.9) | collective-permute-done | bytes 393248 | tf_op jit(solution)/shard_map/ppermute | solution.py:282
  74.2 1.8 %collective-permute-start.13 = (f32[256,384]{1,0:T(8,128)}, f32[256,384]{1,0:T(8,128)}, u32[]{:S(2)}, u32[]{:S(2)}) collective-permute-start(f32[256,384]{1,0:T(8,128)} %collective-permute-done.9.refs_12_), channel_id=1, source_target_pairs={{0,8},{4,12},{8,24},{12,28},{16,0},{20,4},{24,16},{28,20},{1,9},{5... | collective-permute-start | bytes 1179656 | tf_op jit(solution)/shard_map/ppermute | solution.py:282
  76.2 0.7 convert_reduce_fusion.2.start_ref
  77.4 4.5 %collective-permute-done.1.refs_2_ = f32[1536,128]{1,0:T(8,128)S(1)} collective-permute-done((f32[1536,128]{1,0:T(8,128)S(1)}, f32[1536,128]{1,0:T(8,128)S(1)}, u32[]{:S(2)}, u32[]{:S(2)}) %collective-permute-start.1) | collective-permute-done | bytes 786464 | tf_op jit(solution)/shard_map/ppermute | solution.py:272
  82.8 1.8 %collective-permute-done.15.refs_18_ = f32[256,384]{1,0:T(8,128)} collective-permute-done((f32[256,384]{1,0:T(8,128)}, f32[256,384]{1,0:T(8,128)}, u32[]{:S(2)}, u32[]{:S(2)}) %collective-permute-start.15) | collective-permute-done | bytes 393248 | tf_op jit(solution)/shard_map/ppermute | solution.py:282
  84.6 0.7 multiply_reduce_fusion.entry_ref
  85.4 1.1 collective-permute-done.16.refs_19_
  86.6 0.7 copy-done.9
  87.3 26.0 %front.1 = (f32[1536,3072]{1,0:T(8,128)}, f32[1536,128]{1,0:T(8,128)}) custom-call(s32[2]{0:T(128)} %pad_add_fusion.1.place_ref, s32[3,16]{1,0:T(4,128)} %multiply_reduce_fusion.entry_ref, s32[5]{0:T(128)} %convert_reduce_fusion.2.start_ref, f32[512,512]{1,0:T(8,128)} %d_ref.3, f32[24,8,128]{2,1,0:T(8,128)} %bitcast.24, f32[1536,3072]{1,0:T(8,128)} %trail_ref.1, ...), custom_call_target="tpu_custom_call" | custom-call | flops 16911433728 | bytes 44040192 | tf_op jit(solution)/shard_map/front/pallas_call | solution.py:167
  (72 shorter events, 7.2 us)
Async XLA Ops:
  0.6 21.8 %collective-permute-start = (f32[1536,128]{1,0:T(8,128)}, f32[1536,128]{1,0:T(8,128)S(1)}, u32[]{:S(2)}, u32[]{:S(2)}) collective-permute-start(f32[1536,128]{1,0:T(8,128)} %refs_0_.1), channel_id=1, source_target_pairs={{0,1},{1,3},{3,2},{2,0},{4,5},{5,7},{7,6},{6,4},{8,9},{9,11},{11,1... | collective-permute-start | bytes 2359304 | tf_op jit(solution)/shard_map/ppermute | solution.py:268
  3.7 14.3 %all-to-all-start = ((f32[4,384,128]{2,1,0:T(8,128)}), f32[4,384,128]{2,1,0:T(8,128)S(1)}, u32[]{:S(2)}, u32[]{:S(2)}) async-start(f32[4,384,128]{2,1,0:T(8,128)} %bitcast.22), calls=%async_computation | async-start | bytes 1572864 | tf_op jit(solution)/shard_map/all_to_all | solution.py:260
  22.5 64.1 %copy-start.1 = (f32[1536,128]{1,0:T(8,128)}, f32[1536,128]{1,0:T(8,128)S(1)}, u32[]{:S(2)}) copy-start(f32[1536,128]{1,0:T(8,128)S(1)} %collective-permute-done.refs_1_) | copy-start | bytes 2359300
  46.5 18.3 %collective-permute-start.4 = (f32[1536,128]{1,0:T(8,128)}, f32[1536,128]{1,0:T(8,128)S(1)}, u32[]{:S(2)}, u32[]{:S(2)}) collective-permute-start(f32[1536,128]{1,0:T(8,128)} %refs_0_.1), channel_id=1, source_target_pairs={{1,0},{3,1},{2,3},{0,2},{5,4},{7,5},{6,7},{4,6},{9,8},{11,9},{10,1... | collective-permute-start | bytes 2359304 | tf_op jit(solution)/shard_map/ppermute | solution.py:271
  49.7 12.0 %collective-permute-start.2 = (f32[256,384]{1,0:T(8,128)}, f32[256,384]{1,0:T(8,128)S(1)}, u32[]{:S(2)}, u32[]{:S(2)}) collective-permute-start(f32[256,384]{1,0:T(8,128)} %get-tuple-element.20.refs_4_), channel_id=1, source_target_pairs={{0,8},{4,12},{8,24},{12,28},{16,0},{20,4},{24,16},{28,20},{1,9},{5... | collective-permute-start | bytes 1179656 | tf_op jit(solution)/shard_map/ppermute | solution.py:282
  51.2 12.2 %collective-permute-start.3 = (f32[256,384]{1,0:T(8,128)}, f32[256,384]{1,0:T(8,128)}, u32[]{:S(2)}, u32[]{:S(2)}) collective-permute-start(f32[256,384]{1,0:T(8,128)} %get-tuple-element.21.refs_6_), channel_id=1, source_target_pairs={{0,16},{4,20},{8,0},{12,4},{16,24},{20,28},{24,8},{28,12},{1,17},{... | collective-permute-start | bytes 1179656 | tf_op jit(solution)/shard_map/ppermute | solution.py:282
  51.8 9.9 %all-to-all-start.2 = ((f32[8,3,8,128]{3,2,1,0:T(8,128)}), f32[8,3,8,128]{3,2,1,0:T(8,128)S(1)}, u32[]{:S(2)}, u32[]{:S(2)}) async-start(f32[8,3,8,128]{3,2,1,0:T(8,128)} %select_maximum_fusion), calls=%async_computation.2 | async-start | bytes 196608 | tf_op jit(solution)/shard_map/all_to_all | solution.py:220
  56.1 11.5 %collective-permute-start.5 = (f32[256,384]{1,0:T(8,128)}, f32[256,384]{1,0:T(8,128)}, u32[]{:S(2)}, u32[]{:S(2)}) collective-permute-start(f32[256,384]{1,0:T(8,128)} %get-tuple-element.20.refs_4_), channel_id=1, source_target_pairs={{0,4},{4,0},{8,12},{12,8},{16,20},{20,16},{24,28},{28,24},{1,5},{5... | collective-permute-start | bytes 1179656 | tf_op jit(solution)/shard_map/ppermute | solution.py:288
  56.6 20.7 %collective-permute-start.6 = (f32[256,384]{1,0:T(8,128)}, f32[256,384]{1,0:T(8,128)}, u32[]{:S(2)}, u32[]{:S(2)}) collective-permute-start(f32[256,384]{1,0:T(8,128)} %get-tuple-element.21.refs_6_), channel_id=1, source_target_pairs={{0,4},{4,0},{8,12},{12,8},{16,20},{20,16},{24,28},{28,24},{1,5},{5... | collective-permute-start | bytes 1179656 | tf_op jit(solution)/shard_map/ppermute | solution.py:288
  61.6 24.9 %copy-start = (f32[8,3,8,128]{3,2,1,0:T(8,128)}, f32[8,3,8,128]{3,2,1,0:T(8,128)S(1)}, u32[]{:S(2)}) copy-start(f32[8,3,8,128]{3,2,1,0:T(8,128)S(1)} %all-to-all-done.2) | copy-start | bytes 294916
  61.7 24.8 %copy-start.4 = (f32[256,384]{1,0:T(8,128)}, f32[256,384]{1,0:T(8,128)S(1)}, u32[]{:S(2)}) copy-start(f32[256,384]{1,0:T(8,128)S(1)} %collective-permute-done.2.refs_8_) | copy-start | bytes 1179652
  61.7 20.2 %collective-permute-start.1 = (f32[1536,128]{1,0:T(8,128)S(1)}, f32[1536,128]{1,0:T(8,128)S(1)}, u32[]{:S(2)}, u32[]{:S(2)}) collective-permute-start(f32[1536,128]{1,0:T(8,128)S(1)} %collective-permute-done.refs_1_), channel_id=1, source_target_pairs={{0,1},{1,3},{3,2},{2,0},{4,5},{5,7},{7,6},{6,4},{8,9},{9,11},{11,1... | collective-permute-start | bytes 2359304 | tf_op jit(solution)/shard_map/ppermute | solution.py:272
  64.8 21.7 %copy-start.2 = (f32[1536,128]{1,0:T(8,128)}, f32[1536,128]{1,0:T(8,128)S(1)}, u32[]{:S(2)}) copy-start(f32[1536,128]{1,0:T(8,128)S(1)} %collective-permute-done.4.refs_3_) | copy-start | bytes 2359300
  64.8 9.4 %collective-permute-start.9 = (f32[256,384]{1,0:T(8,128)S(1)}, f32[256,384]{1,0:T(8,128)}, u32[]{:S(2)}, u32[]{:S(2)}) collective-permute-start(f32[256,384]{1,0:T(8,128)S(1)} %collective-permute-done.2.refs_8_), channel_id=1, source_target_pairs={{0,8},{4,12},{8,24},{12,28},{16,0},{20,4},{24,16},{28,20},{1,9},{5... | collective-permute-start | bytes 1179656 | tf_op jit(solution)/shard_map/ppermute | solution.py:282
  66.3 9.6 %collective-permute-start.11 = (f32[256,384]{1,0:T(8,128)}, f32[256,384]{1,0:T(8,128)}, u32[]{:S(2)}, u32[]{:S(2)}) collective-permute-start(f32[256,384]{1,0:T(8,128)} %collective-permute-done.3.refs_10_), channel_id=1, source_target_pairs={{0,16},{4,20},{8,0},{12,4},{16,24},{20,28},{24,8},{28,12},{1,17},{... | collective-permute-start | bytes 1179656 | tf_op jit(solution)/shard_map/ppermute | solution.py:282
  67.6 14.4 %collective-permute-start.7 = (f32[256,384]{1,0:T(8,128)S(1)}, f32[256,384]{1,0:T(8,128)}, u32[]{:S(2)}, u32[]{:S(2)}) collective-permute-start(f32[256,384]{1,0:T(8,128)S(1)} %collective-permute-done.2.refs_8_), channel_id=1, source_target_pairs={{0,4},{4,0},{8,12},{12,8},{16,20},{20,16},{24,28},{28,24},{1,5},{5... | collective-permute-start | bytes 1179656 | tf_op jit(solution)/shard_map/ppermute | solution.py:288
  74.2 8.6 %collective-permute-start.13 = (f32[256,384]{1,0:T(8,128)}, f32[256,384]{1,0:T(8,128)}, u32[]{:S(2)}, u32[]{:S(2)}) collective-permute-start(f32[256,384]{1,0:T(8,128)} %collective-permute-done.9.refs_12_), channel_id=1, source_target_pairs={{0,8},{4,12},{8,24},{12,28},{16,0},{20,4},{24,16},{28,20},{1,9},{5... | collective-permute-start | bytes 1179656 | tf_op jit(solution)/shard_map/ppermute | solution.py:282
  75.9 8.7 %collective-permute-start.15 = (f32[256,384]{1,0:T(8,128)}, f32[256,384]{1,0:T(8,128)}, u32[]{:S(2)}, u32[]{:S(2)}) collective-permute-start(f32[256,384]{1,0:T(8,128)} %collective-permute-done.11.refs_14_), channel_id=1, source_target_pairs={{0,16},{4,20},{8,0},{12,4},{16,24},{20,28},{24,8},{28,12},{1,17},{... | collective-permute-start | bytes 1179656 | tf_op jit(solution)/shard_map/ppermute | solution.py:282
  77.3 8.0 %collective-permute-start.8 = (f32[256,384]{1,0:T(8,128)}, f32[256,384]{1,0:T(8,128)S(1)}, u32[]{:S(2)}, u32[]{:S(2)}) collective-permute-start(f32[256,384]{1,0:T(8,128)} %collective-permute-done.3.refs_10_), channel_id=1, source_target_pairs={{0,4},{4,0},{8,12},{12,8},{16,20},{20,16},{24,28},{28,24},{1,5},{5... | collective-permute-start | bytes 1179656 | tf_op jit(solution)/shard_map/ppermute | solution.py:288
  82.0 4.6 %copy-start.3 = (f32[1536,128]{1,0:T(8,128)}, f32[1536,128]{1,0:T(8,128)S(1)}, u32[]{:S(2)}) copy-start(f32[1536,128]{1,0:T(8,128)S(1)} %collective-permute-done.1.refs_2_) | copy-start | bytes 2359300
  82.0 3.4 %collective-permute-start.10 = (f32[256,384]{1,0:T(8,128)}, f32[256,384]{1,0:T(8,128)S(1)}, u32[]{:S(2)}, u32[]{:S(2)}) collective-permute-start(f32[256,384]{1,0:T(8,128)} %collective-permute-done.9.refs_12_), channel_id=1, source_target_pairs={{0,4},{4,0},{8,12},{12,8},{16,20},{20,16},{24,28},{28,24},{1,5},{5... | collective-permute-start | bytes 1179656 | tf_op jit(solution)/shard_map/ppermute | solution.py:288
  82.0 3.4 %collective-permute-start.12 = (f32[256,384]{1,0:T(8,128)}, f32[256,384]{1,0:T(8,128)S(1)}, u32[]{:S(2)}, u32[]{:S(2)}) collective-permute-start(f32[256,384]{1,0:T(8,128)} %collective-permute-done.11.refs_14_), channel_id=1, source_target_pairs={{0,4},{4,0},{8,12},{12,8},{16,20},{20,16},{24,28},{28,24},{1,5},{5... | collective-permute-start | bytes 1179656 | tf_op jit(solution)/shard_map/ppermute | solution.py:288
  82.8 2.6 %collective-permute-start.14 = (f32[256,384]{1,0:T(8,128)}, f32[256,384]{1,0:T(8,128)S(1)}, u32[]{:S(2)}, u32[]{:S(2)}) collective-permute-start(f32[256,384]{1,0:T(8,128)} %collective-permute-done.13.refs_16_), channel_id=1, source_target_pairs={{0,4},{4,0},{8,12},{12,8},{16,20},{20,16},{24,28},{28,24},{1,5},{5... | collective-permute-start | bytes 1179656 | tf_op jit(solution)/shard_map/ppermute | solution.py:288
  84.6 1.9 %collective-permute-start.16 = (f32[256,384]{1,0:T(8,128)}, f32[256,384]{1,0:T(8,128)S(1)}, u32[]{:S(2)}, u32[]{:S(2)}) collective-permute-start(f32[256,384]{1,0:T(8,128)} %collective-permute-done.15.refs_18_), channel_id=1, source_target_pairs={{0,4},{4,0},{8,12},{12,8},{16,20},{20,16},{24,28},{28,24},{1,5},{5... | collective-permute-start | bytes 1179656 | tf_op jit(solution)/shard_map/ppermute | solution.py:288
  (5 other events, 5.5 us)
